TPU v7x, 32 devices: a whole 2x2x4 slice. The times are simulated.
32 devices in a mesh: rep: 4 (over y, x), fsdp: 8 (over z, core).
Axes of the slice: x: 2, y: 2, z: 4, core: 2. Of those that a mesh axis runs over, the one named last changes fastest.
Arguments:
- pixels: bfloat16 [32768, 6912], P(('rep', 'fsdp')), may hold values from -6 to 6
- image_class: int32 [32, 40], P(('rep', 'fsdp')), may hold values from 0 to 3, as said below
- resize_a: bfloat16 [64, 1024], replicated, may hold values from -0.75 to 0.75
- resize_b: bfloat16 [576, 1024], replicated, may hold values from -0.25 to 0.25
- resize_c: bfloat16 [2304, 1024], replicated, may hold values from -0.125 to 0.125
- posmap_a: bfloat16 [900, 49], replicated, may hold values from 0 to 0.3984375
- posmap_b: bfloat16 [100, 49], replicated, may hold values from 0 to 0.3984375
- posmap_c: bfloat16 [25, 49], replicated, may hold values from 0 to 0.3984375
- cotangent: bfloat16 [32768, 768], P(('rep', 'fsdp')), may hold values from -6 to 6
- patch_kernel: bfloat16 [3072, 768], P('fsdp'), may hold values from -0.109375 to 0.109375
- pos_table: bfloat16 [49, 768], P(None, 'fsdp'), may hold values from -3 to 3
- qkv_weight: bfloat16 [768, 2304], P('fsdp'), may hold values from -0.21875 to 0.21875
- out_weight: bfloat16 [768, 768], P('fsdp'), may hold values from -0.625 to 0.625
- up_weight: bfloat16 [768, 3072], P('fsdp'), may hold values from -0.21875 to 0.21875
- down_weight: bfloat16 [3072, 768], P('fsdp'), may hold values from -0.109375 to 0.109375
- biases: bfloat16 [7, 768], P(None, 'fsdp'), may hold values from -3 to 3
- up_bias: bfloat16 [3072], P('fsdp'), may hold values from -3 to 3
- gains: bfloat16 [2, 768], P(None, 'fsdp'), may hold values from 0.25 to 1.75
Outputs:
- output: bfloat16 [32768, 768], P(('rep', 'fsdp'))
- grad_pixels: bfloat16 [32768, 6912], P(('rep', 'fsdp'))
- grad_patch_kernel: float32 [3072, 768], P('fsdp')
- grad_pos_table: float32 [49, 768], P(None, 'fsdp')
- grad_qkv_weight: float32 [768, 2304], P('fsdp')
- grad_out_weight: float32 [768, 768], P('fsdp')
- grad_up_weight: float32 [768, 3072], P('fsdp')
- grad_down_weight: float32 [3072, 768], P('fsdp')
- grad_biases: float32 [7, 768], P(None, 'fsdp')
- grad_up_bias: float32 [3072], P('fsdp')
- grad_gains: float32 [2, 768], P(None, 'fsdp')
Inputs may be any that keep to these rules, and one draw needn't show every extreme that they name: `image_class`: class 3 marks an empty slot; in each row the empty slots come after all images, the token counts of a row's images sum to at most 1024, class 0 stands only in slot 0, and row 0 holds a class 0 image.
All inputs are finite; a program needn't handle non-finite values.
Results may differ from a plain program's by a relative error of at most 0.018.
Values may be sent and summed in bfloat16 or wider, within the bound.
No kernel may reach another device: no remote copies, remote signals or barrier semaphores. Data moves between devices by JAX's collectives and lax.ppermute only.
A program may use at most 320 MiB of HBM per device.

v0:
```python
import jax
import jax.numpy as jnp
from jax import lax
from jax.sharding import PartitionSpec as P

HEADS = 12
GRID_A = 30
GRID_B = 10
GRID_C = 5


def token_layout(classes, tokens_here):
    class_tokens = jnp.array(
        [GRID_A * GRID_A, GRID_B * GRID_B, GRID_C * GRID_C, 0], dtype=jnp.int32
    )
    class_ids = jnp.arange(4, dtype=jnp.int32)
    image_tokens = jnp.sum(
        jnp.where(classes[:, None] == class_ids[None, :], class_tokens[None, :], 0), axis=1
    )
    image_ends = jnp.cumsum(image_tokens)
    image_starts = image_ends - image_tokens
    positions = jnp.arange(tokens_here, dtype=jnp.int32)
    segment = jnp.sum((image_ends[None, :] <= positions[:, None]).astype(jnp.int32), axis=1)
    membership = segment[:, None] == jnp.arange(classes.shape[0], dtype=jnp.int32)[None, :]
    live_rows = jnp.any(membership, axis=1)
    category = jnp.sum(jnp.where(membership, classes[None, :], 0), axis=1) + jnp.where(
        live_rows, 0, 3
    )
    offset = positions - jnp.sum(jnp.where(membership, image_starts[None, :], 0), axis=1)
    return (segment, category, offset, live_rows)


def position_rows(category, offset, tables):
    rows_out = jnp.zeros((category.shape[0], tables[0].shape[1]), jnp.float32)
    for class_id, table_rows in enumerate(tables):
        row_index = jnp.clip(offset, 0, table_rows.shape[0] - 1)
        picked = jnp.take(table_rows, row_index, axis=0).astype(jnp.float32)
        rows_out = rows_out + jnp.where((category == class_id)[:, None], picked, 0.0)
    return rows_out


def layer_norm(values, gain_row, shift_row):
    center = values - jnp.mean(values, axis=-1, keepdims=True)
    spread = jnp.mean(center * center, axis=-1, keepdims=True)
    return center * lax.rsqrt(spread + 1e-06) * gain_row + shift_row


def gelu_tanh(values):
    return jax.nn.gelu(values, approximate=True)


def masked_scores(query, keys_block, same_image, scaling):
    scores = (
        jnp.einsum("qd,kd->qk", query, keys_block, preferred_element_type=jnp.float32) * scaling
    )
    return jnp.where(same_image, scores, -1e30)


def local(
    pixels,
    image_class,
    resize_a,
    resize_b,
    resize_c,
    posmap_a,
    posmap_b,
    posmap_c,
    cotangent,
    patch_kernel,
    pos_table,
    qkv_weight,
    out_weight,
    up_weight,
    down_weight,
    biases,
    up_bias,
    gains,
):
    tokens_here = pixels.shape[0]
    segment, category, offset, live_rows = token_layout(image_class[0], tokens_here)
    live = live_rows[:, None].astype(jnp.float32)
    same_image = segment[:, None] == segment[None, :]
    matrices = (resize_a, resize_b, resize_c)
    pixel_frame = pixels.reshape(tokens_here, 3, -1)
    resized = jnp.zeros((tokens_here, 3, resize_a.shape[1]), jnp.float32)
    for class_id, matrix in enumerate(matrices):
        area = matrix.shape[0]
        partial_rows = jnp.einsum(
            "tcp,pk->tck", pixel_frame[:, :, :area], matrix, preferred_element_type=jnp.float32
        )
        resized = resized + jnp.where((category == class_id)[:, None, None], partial_rows, 0.0)
    resized = resized.reshape(tokens_here, -1).astype(jnp.bfloat16)
    pos_rows = position_rows(category, offset, (posmap_a, posmap_b, posmap_c)).astype(jnp.bfloat16)
    gathered = (
        lax.all_gather(patch_kernel, "fsdp", axis=0, tiled=True),
        lax.all_gather(pos_table, "fsdp", axis=1, tiled=True),
        lax.all_gather(qkv_weight, "fsdp", axis=0, tiled=True),
        lax.all_gather(out_weight, "fsdp", axis=0, tiled=True),
        lax.all_gather(up_weight, "fsdp", axis=0, tiled=True),
        lax.all_gather(down_weight, "fsdp", axis=0, tiled=True),
        lax.all_gather(biases, "fsdp", axis=1, tiled=True),
        lax.all_gather(up_bias, "fsdp", axis=0, tiled=True),
        lax.all_gather(gains, "fsdp", axis=1, tiled=True),
    )
    kernel, pos_weight, qkv_proj, out_proj, up_proj, down_proj, bias_raw, up_raw, gain_raw = (
        gathered
    )
    bias_rows = bias_raw.astype(jnp.float32)
    up_shift = up_raw.astype(jnp.float32)
    gain_rows = gain_raw.astype(jnp.float32)
    embed = (
        jnp.dot(resized, kernel, preferred_element_type=jnp.float32)
        + bias_rows[0]
        + jnp.dot(pos_rows, pos_weight, preferred_element_type=jnp.float32)
    )
    normed1 = layer_norm(embed, gain_rows[0], bias_rows[1]).astype(jnp.bfloat16)
    features = embed.shape[1]
    head_size = features // HEADS
    scaling = head_size ** (-0.5)
    shift_vec = jnp.concatenate([bias_rows[2], jnp.zeros_like(bias_rows[2]), bias_rows[3]])
    projected = (jnp.dot(normed1, qkv_proj, preferred_element_type=jnp.float32) + shift_vec).astype(
        jnp.bfloat16
    )

    def to_heads(block):
        return block.reshape(tokens_here, HEADS, head_size).transpose(1, 0, 2)

    query_heads = to_heads(projected[:, :features])
    key_heads = to_heads(projected[:, features : 2 * features])
    value_heads = to_heads(projected[:, 2 * features :])

    def head_forward(inputs):
        query, keys_block, values_block = inputs
        scores = masked_scores(query, keys_block, same_image, scaling)
        row_max = jnp.max(scores, axis=-1, keepdims=True)
        weights = jnp.exp(scores - row_max)
        row_sum = jnp.sum(weights, axis=-1, keepdims=True)
        probs = (weights / row_sum).astype(jnp.bfloat16)
        head_out = jnp.einsum("qk,kd->qd", probs, values_block, preferred_element_type=jnp.float32)
        return (head_out, row_max, row_sum)

    head_outs, row_maxes, row_sums = lax.map(head_forward, (query_heads, key_heads, value_heads))
    mixed = head_outs.transpose(1, 0, 2).reshape(tokens_here, features).astype(jnp.bfloat16)
    hidden = embed + jnp.dot(mixed, out_proj, preferred_element_type=jnp.float32) + bias_rows[4]
    normed2 = layer_norm(hidden, gain_rows[1], bias_rows[5]).astype(jnp.bfloat16)
    pre_act = jnp.dot(normed2, up_proj, preferred_element_type=jnp.float32) + up_shift
    act = gelu_tanh(pre_act).astype(jnp.bfloat16)
    result = (
        hidden + jnp.dot(act, down_proj, preferred_element_type=jnp.float32) + bias_rows[6]
    ) * live
    output = result.astype(jnp.bfloat16)
    g_out = cotangent.astype(jnp.float32) * live
    g_branch = g_out.astype(jnp.bfloat16)
    grad_down = jnp.einsum("tf,td->fd", act, g_branch, preferred_element_type=jnp.float32)
    grad_bias_six = jnp.sum(g_branch.astype(jnp.float32), axis=0)
    g_act = jnp.einsum("td,fd->tf", g_branch, down_proj, preferred_element_type=jnp.float32)
    _, gelu_pull = jax.vjp(gelu_tanh, pre_act)
    g_pre = gelu_pull(g_act)[0].astype(jnp.bfloat16)
    grad_up = jnp.einsum("td,tf->df", normed2, g_pre, preferred_element_type=jnp.float32)
    grad_up_shift = jnp.sum(g_pre.astype(jnp.float32), axis=0)
    g_norm2 = jnp.einsum("tf,df->td", g_pre, up_proj, preferred_element_type=jnp.float32)
    _, norm_pull2 = jax.vjp(layer_norm, hidden, gain_rows[1], bias_rows[5])
    g_from_norm2, grad_gain_one, grad_bias_five = norm_pull2(g_norm2)
    g_hidden = g_out + g_from_norm2
    g_mix = g_hidden.astype(jnp.bfloat16)
    grad_out = jnp.einsum("td,te->de", mixed, g_mix, preferred_element_type=jnp.float32)
    grad_bias_four = jnp.sum(g_mix.astype(jnp.float32), axis=0)
    g_mixed = jnp.einsum("te,de->td", g_mix, out_proj, preferred_element_type=jnp.float32).astype(
        jnp.bfloat16
    )

    def head_backward(inputs):
        query, keys_block, values_block, grad_head, row_max, row_sum = inputs
        scores = masked_scores(query, keys_block, same_image, scaling)
        probs_float = jnp.exp(scores - row_max) / row_sum
        probs = probs_float.astype(jnp.bfloat16)
        grad_values = jnp.einsum("qk,qd->kd", probs, grad_head, preferred_element_type=jnp.float32)
        grad_probs = jnp.einsum(
            "qd,kd->qk", grad_head, values_block, preferred_element_type=jnp.float32
        )
        row_delta = jnp.sum(probs_float * grad_probs, axis=-1, keepdims=True)
        grad_scores = (probs_float * (grad_probs - row_delta)).astype(jnp.bfloat16)
        grad_query = (
            jnp.einsum("qk,kd->qd", grad_scores, keys_block, preferred_element_type=jnp.float32)
            * scaling
        )
        grad_keys = (
            jnp.einsum("qk,qd->kd", grad_scores, query, preferred_element_type=jnp.float32)
            * scaling
        )
        return (grad_query, grad_keys, grad_values)

    grad_heads = to_heads(g_mixed)
    grad_query, grad_keys, grad_values = lax.map(
        head_backward, (query_heads, key_heads, value_heads, grad_heads, row_maxes, row_sums)
    )

    def from_heads(block):
        return block.transpose(1, 0, 2).reshape(tokens_here, features)

    g_projected = jnp.concatenate(
        [from_heads(grad_query), from_heads(grad_keys), from_heads(grad_values)], axis=1
    ).astype(jnp.bfloat16)
    grad_qkv = jnp.einsum("td,te->de", normed1, g_projected, preferred_element_type=jnp.float32)
    projected_sums = jnp.sum(g_projected.astype(jnp.float32), axis=0)
    grad_bias_two = projected_sums[:features]
    grad_bias_three = projected_sums[2 * features :]
    g_norm1 = jnp.einsum("te,de->td", g_projected, qkv_proj, preferred_element_type=jnp.float32)
    _, norm_pull1 = jax.vjp(layer_norm, embed, gain_rows[0], bias_rows[1])
    g_from_norm1, grad_gain_zero, grad_bias_one = norm_pull1(g_norm1)
    g_embed = g_hidden + g_from_norm1
    g_emb = g_embed.astype(jnp.bfloat16)
    grad_bias_zero = jnp.sum(g_emb.astype(jnp.float32), axis=0)
    grad_kernel = jnp.einsum("tk,td->kd", resized, g_emb, preferred_element_type=jnp.float32)
    grad_pos = jnp.einsum("tp,td->pd", pos_rows, g_emb, preferred_element_type=jnp.float32)
    g_resized = jnp.einsum("td,kd->tk", g_emb, kernel, preferred_element_type=jnp.float32).astype(
        jnp.bfloat16
    )
    g_resized = g_resized.reshape(tokens_here, 3, -1)
    full_area = pixel_frame.shape[2]
    grad_frame = jnp.zeros((tokens_here, 3, full_area), jnp.float32)
    for class_id, matrix in enumerate(matrices):
        area = matrix.shape[0]
        partial_rows = jnp.einsum(
            "tck,pk->tcp", g_resized, matrix, preferred_element_type=jnp.float32
        )
        partial_rows = jnp.where((category == class_id)[:, None, None], partial_rows, 0.0)
        grad_frame = grad_frame + jnp.pad(partial_rows, ((0, 0), (0, 0), (0, full_area - area)))
    grad_pixels = grad_frame.reshape(tokens_here, -1).astype(jnp.bfloat16)
    grad_bias_rows = jnp.stack(
        [
            grad_bias_zero,
            grad_bias_one,
            grad_bias_two,
            grad_bias_three,
            grad_bias_four,
            grad_bias_five,
            grad_bias_six,
        ]
    )
    grad_gain_rows = jnp.stack([grad_gain_zero, grad_gain_one])
    summed = (
        lax.psum_scatter(
            grad_kernel.astype(jnp.bfloat16), "fsdp", scatter_dimension=0, tiled=True
        ).astype(jnp.float32),
        lax.psum_scatter(
            grad_pos.astype(jnp.bfloat16), "fsdp", scatter_dimension=1, tiled=True
        ).astype(jnp.float32),
        lax.psum_scatter(
            grad_qkv.astype(jnp.bfloat16), "fsdp", scatter_dimension=0, tiled=True
        ).astype(jnp.float32),
        lax.psum_scatter(
            grad_out.astype(jnp.bfloat16), "fsdp", scatter_dimension=0, tiled=True
        ).astype(jnp.float32),
        lax.psum_scatter(
            grad_up.astype(jnp.bfloat16), "fsdp", scatter_dimension=0, tiled=True
        ).astype(jnp.float32),
        lax.psum_scatter(
            grad_down.astype(jnp.bfloat16), "fsdp", scatter_dimension=0, tiled=True
        ).astype(jnp.float32),
        lax.psum_scatter(
            grad_bias_rows.astype(jnp.bfloat16), "fsdp", scatter_dimension=1, tiled=True
        ).astype(jnp.float32),
        lax.psum_scatter(
            grad_up_shift.astype(jnp.bfloat16), "fsdp", scatter_dimension=0, tiled=True
        ).astype(jnp.float32),
        lax.psum_scatter(
            grad_gain_rows.astype(jnp.bfloat16), "fsdp", scatter_dimension=1, tiled=True
        ).astype(jnp.float32),
    )
    totals = (
        lax.psum(summed[0].astype(jnp.bfloat16), "rep").astype(jnp.float32),
        lax.psum(summed[1].astype(jnp.bfloat16), "rep").astype(jnp.float32),
        lax.psum(summed[2].astype(jnp.bfloat16), "rep").astype(jnp.float32),
        lax.psum(summed[3].astype(jnp.bfloat16), "rep").astype(jnp.float32),
        lax.psum(summed[4].astype(jnp.bfloat16), "rep").astype(jnp.float32),
        lax.psum(summed[5].astype(jnp.bfloat16), "rep").astype(jnp.float32),
        lax.psum(summed[6].astype(jnp.bfloat16), "rep").astype(jnp.float32),
        lax.psum(summed[7].astype(jnp.bfloat16), "rep").astype(jnp.float32),
        lax.psum(summed[8].astype(jnp.bfloat16), "rep").astype(jnp.float32),
    )
    return (
        output,
        grad_pixels,
        totals[0],
        totals[1],
        totals[2],
        totals[3],
        totals[4],
        totals[5],
        totals[6],
        totals[7],
        totals[8],
    )


def solution(mesh):
    in_specs = (
        P(("rep", "fsdp"), None),
        P(("rep", "fsdp"), None),
        P(),
        P(),
        P(),
        P(),
        P(),
        P(),
        P(("rep", "fsdp"), None),
        P("fsdp", None),
        P(None, "fsdp"),
        P("fsdp", None),
        P("fsdp", None),
        P("fsdp", None),
        P("fsdp", None),
        P(None, "fsdp"),
        P("fsdp"),
        P(None, "fsdp"),
    )
    out_specs = (
        P(("rep", "fsdp"), None),
        P(("rep", "fsdp"), None),
        P("fsdp", None),
        P(None, "fsdp"),
        P("fsdp", None),
        P("fsdp", None),
        P("fsdp", None),
        P("fsdp", None),
        P(None, "fsdp"),
        P("fsdp"),
        P(None, "fsdp"),
    )
    return jax.shard_map(local, mesh=mesh, in_specs=in_specs, out_specs=out_specs, check_vma=False)
```

profile of v0, /device:TPU:0, one launch (start us, length us, event | category | flops | bytes accessed | tf_op | source)
XLA Modules:
  0.0 870.0 jit_solution(9931137593922794327)
XLA Ops:
  12.5 13.6 %all-gather.2 = bf16[8,96,2]{1,2,0:T(2,128)(2,1)S(1)} all-gather(bf16[1,96,2]{1,2,0:T(2,128)(2,1)} %bitcast.245), channel_id=1, replica_groups=mesh['rep'=4,'fsdp'=8] {'fsdp'}, dimensions={0}, use_global_device_ids=true | all-gather | bytes 3456 | tf_op jit(solution)/shard_map/all_gather | solution.py:103
  26.2 12.9 %all-gather.3 = bf16[8,1,384]{2,1,0:T(2,128)(2,1)S(1)} all-gather(bf16[1,1,384]{2,1,0:T(2,128)(2,1)S(1)} %reshape.322), channel_id=1, replica_groups=mesh['rep'=4,'fsdp'=8] {'fsdp'}, dimensions={0}, use_global_device_ids=true | all-gather | bytes 6912 | tf_op jit(solution)/shard_map/all_gather | solution.py:102
  39.8 13.0 %all-gather = bf16[8,96,7]{1,2,0:T(8,128)(2,1)S(1)} all-gather(bf16[1,96,7]{1,2,0:T(8,128)(2,1)} %bitcast.244), channel_id=1, replica_groups=mesh['rep'=4,'fsdp'=8] {'fsdp'}, dimensions={0}, use_global_device_ids=true | all-gather | bytes 12096 | tf_op jit(solution)/shard_map/all_gather | solution.py:101
  55.3 14.4 %all-gather.1 = bf16[8,96,49]{1,2,0:T(8,128)(2,1)S(1)} all-gather(bf16[1,96,49]{1,2,0:T(8,128)(2,1)} %bitcast.240), channel_id=1, replica_groups=mesh['rep'=4,'fsdp'=8] {'fsdp'}, dimensions={0}, use_global_device_ids=true | all-gather | bytes 84672 | tf_op jit(solution)/shard_map/all_gather | solution.py:96
  71.7 18.7 %copy.149 = bf16[1024,6912]{0,1:T(8,128)(2,1)} copy(bf16[1024,6912]{1,0:T(8,128)(2,1)} %param.23) | data formatting | bytes 28311552 | tf_op args[0]
  90.4 10.9 %fusion.64 = f32[1024,3,1024]{0,2,1:T(8,128)} fusion(bf16[1024,3,2304]{0,2,1:T(8,128)(2,1)} %bitcast.204, bf16[576,1024]{1,0:T(8,128)(2,1)S(1)} %copy-done), kind=kOutput, calls=%fused_computation.85 | convolution fusion | flops 3623878656 | bytes 17301504 | tf_op jit(solution)/shard_map/tcp,pk->tck/dot_general | solution.py:88
  101.3 7.3 fusion.73
  118.4 25.7 %add_convert_fusion.1 = bf16[1024,3,1024]{0,2,1:T(8,128)(2,1)} fusion(f32[1024,3,1024]{0,2,1:T(8,128)} %fusion.64, f32[1024,3,1024]{0,2,1:T(8,128)} %fusion.73, pred[1024]{0:T(1024)(128)(4,1)S(1)} %get-tuple-element.379, pred[1024]{0:T(1024)(128)(4,1)S(1)} %get-tuple-element.378, pred[1024]{0:T(1024)(128)(4,1)S(1)} %get-tuple-element.377, ...), kind=kOutput, calls=%fused_computation.72 | convolution fusion | flops 14514388992 | bytes 50334720 | tf_op jit(solution)/shard_map/tcp,pk->tck/dot_general | solution.py:88
  144.0 8.8 %fusion.98 = f32[1024,768]{0,1:T(8,128)S(1)} fusion(bf16[1024,3072]{0,1:T(8,128)(2,1)} %bitcast.249, bf16[3072,768]{1,0:T(8,128)(2,1)} %all-gather.10.cloned.1.call-done), kind=kOutput, calls=%fused_computation.179 | convolution fusion | flops 4831838208 | bytes 14155776 | tf_op jit(solution)/shard_map/dot_general | solution.py:112
  156.5 7.2 add_convert_fusion.2
  185.1 61.9 %while.30 = (s32[]{:T(128)}, bf16[12,1024,64]{1,2,0:T(8,128)(2,1)S(1)}, f32[12,1024,1]{1,2,0:T(1,128)S(1)}, f32[12,1024,1]{1,2,0:T(1,128)S(1)}, bf16[12,1024,64]...) while((s32[]{:T(128)}, ...), condition=%wide.region_11.12_spmd.clone, body=%wide.region_8.11_spmd.clone.sunk | while | flops 284162048 | bytes 13690985 | solution.py:142
  253.7 11.3 %fusion.86 = f32[1024,3072]{1,0:T(8,128)} fusion(bf16[768,3072]{1,0:T(8,128)(2,1)} %all-gather.16.cloned.1.call-done, f32[1024,768]{0,1:T(8,128)} %copy-done.4, f32[768]{0:T(1024)S(1)} %get-tuple-element.299, f32[768]{0:T(1024)S(1)} %get-tuple-element.306, f32[1024]{0:T(1024)S(1)} %fusion.79, f32[1024]{0:T(1024)S(1)} %broadcast_multiply_fusion), kind=kOutput, calls=%fused_computation.168 | convolution fusion | flops 4835770368 | bytes 20461568 | tf_op jit(solution)/shard_map/dot_general | solution.py:146
  265.0 16.8 %fusion.97 = (bf16[3072]{0:T(1024)(128)(2,1)}, bf16[1024,3072]{1,0:T(8,128)(2,1)S(1)}) fusion(f32[1024,3072]{1,0:T(8,128)} %fusion.86, f32[3072]{0:T(1024)S(1)} %bitcast.241, bf16[3072,768]{1,0:T(8,128)(2,1)} %all-gather.18.cloned.1.call-done, bf16[1024,768]{0,1:T(8,128)(2,1)S(1)} %copy-done.10, f32[1024]{0:T(1024)S(1)} %get-tuple-element.386), kind=kOutput, calls=%fused_computation.178 | convolution fusion | flops 4903400448 | bytes 25188352 | tf_op jit(solution)/shard_map/td,fd->tf/dot_general | solution.py:156
  281.8 7.3 fusion.96
  316.0 150.2 %while.31 = (s32[]{:T(128)}, bf16[12,1024,64]{1,2,0:T(8,128)(2,1)}, bf16[12,1024,64]{1,2,0:T(8,128)(2,1)}, bf16[12,1024,64]{1,2,0:T(8,128)(2,1)}, bf16[12,1024,6...) while((s32[]{:T(128)}, bf16[12,1024,64]{1,2,0:T(8,128)(2,1)}, ...), condition=%wide.region_18.19_spmd.clone, body=%wide.region_16.18_spmd.clone.sunk | while | flops 682753024 | bytes 34124928 | solution.py:194
  466.2 9.1 %convolution_convert_fusion.4 = bf16[768,2304]{1,0:T(8,128)(2,1)} fusion(bf16[1024,768]{0,1:T(8,128)(2,1)} %bitcast.209, bf16[1024,768]{0,1:T(8,128)(2,1)} %bitcast.212, bf16[1024,768]{0,1:T(8,128)(2,1)} %bitcast.215, f32[1024,768]{0,1:T(8,128)} %copy-done.2, f32[768]{0:T(1024)S(1)} %copy-done.51, f32[768]{0:T(1024)S(1)} %copy-done.32, ...), kind=kOutput, calls=%fused_computation.78 | convolution fusion | flops 3643736064 | bytes 11417600 | tf_op jit(solution)/shard_map/td,te->de/dot_general | solution.py:204
  475.4 13.3 %convolution_convert_fusion.1 = bf16[3072,768]{1,0:T(8,128)(2,1)} fusion(bf16[1024,768]{0,1:T(8,128)(2,1)S(1)} %copy-done.10, f32[1024]{0:T(1024)S(1)} %get-tuple-element.386, f32[1024,3072]{1,0:T(8,128)} %fusion.86, f32[3072]{0:T(1024)S(1)} %bitcast.242), kind=kOutput, calls=%fused_computation.75 | convolution fusion | flops 4868014080 | bytes 18890752 | tf_op jit(solution)/shard_map/tf,td->fd/dot_general | solution.py:154
  488.7 10.3 %convolution_convert_fusion.2 = bf16[768,3072]{1,0:T(8,128)(2,1)} fusion(bf16[1024,3072]{1,0:T(8,128)(2,1)} %copy-done.54, f32[1024,768]{0,1:T(8,128)} %copy-done.4, f32[768]{0:T(1024)S(1)} %get-tuple-element.299, f32[768]{0:T(1024)S(1)} %get-tuple-element.306, f32[1024]{0:T(1024)S(1)} %fusion.79, f32[1024]{0:T(1024)S(1)} %broadcast_multiply_fusion), kind=kOutput, calls=%fused_computation.76 | convolution fusion | flops 4838129664 | bytes 14170112 | tf_op jit(solution)/shard_map/td,tf->df/dot_general | solution.py:159
  499.1 9.1 %fusion.95 = (bf16[768]{0:T(1024)(128)(2,1)S(1)}, f32[1024,768]{1,0:T(8,128)}) fusion(bf16[768,2304]{1,0:T(8,128)(2,1)} %all-gather.12.cloned.1.call-done, bf16[1024,768]{0,1:T(8,128)(2,1)} %bitcast.210, bf16[1024,768]{0,1:T(8,128)(2,1)} %bitcast.213, bf16[1024,768]{0,1:T(8,128)(2,1)} %bitcast.216), kind=kOutput, calls=%fused_computation.176 | convolution fusion | flops 3638820096 | bytes 11404800 | tf_op jit(solution)/shard_map/te,de->td/dot_general | solution.py:208
  531.0 9.5 %convolution_convert_fusion = bf16[1024,3072]{1,0:T(8,128)(2,1)} fusion(bf16[1024,768]{0,1:T(8,128)(2,1)S(1)} %copy-done.18, bf16[3072,768]{1,0:T(8,128)(2,1)} %all-gather.10.cloned.1.call-done), kind=kOutput, calls=%fused_computation.74 | convolution fusion | flops 4834983936 | bytes 12582912 | tf_op jit(solution)/shard_map/td,kd->tk/dot_general | solution.py:216
  540.4 8.8 %copy.171 = bf16[1024,3072]{0,1:T(8,128)(2,1)} copy(bf16[1024,3072]{1,0:T(8,128)(2,1)} %convolution_convert_fusion) | data formatting | bytes 12582912 | tf_op jit(solution)/shard_map/convert_element_type | solution.py:216
  551.5 8.7 %broadcast_select_fusion = f32[1024,3,576]{0,2,1:T(8,128)} fusion(pred[1024]{0:T(1024)(128)(4,1)S(1)} %copy-done.49, bf16[1024,3,1024]{0,2,1:T(8,128)(2,1)} %bitcast.199, bf16[576,1024]{1,0:T(8,128)(2,1)S(1)} %copy-done), kind=kOutput, calls=%fused_computation.87 | convolution fusion | flops 3625648128 | bytes 14550016 | tf_op jit(solution)/shard_map/tck,pk->tcp/dot_general | solution.py:224
  567.2 12.5 %multiply_convert_fusion.2 = bf16[1024,768]{0,1:T(8,128)(2,1)} fusion(f32[1024,768]{0,1:T(8,128)} %copy-done.4, bf16[3072,768]{1,0:T(8,128)(2,1)} %all-gather.18.cloned.1.call-done, f32[1024]{0:T(1024)S(1)} %get-tuple-element.386, f32[768]{0:T(1024)} %get-tuple-element.300, f32[1024,3072]{1,0:T(8,128)} %fusion.86, f32[3072]{0:T(1024)S(1)} %bitcast.243), kind=kOutput, calls=%fused_computation.96 | convolution fusion | flops 4866441216 | bytes 22039552 | tf_op jit(solution)/shard_map/dot_general | solution.py:149
  584.5 44.9 %reduce-scatter.21.cloned.1.call-done = bf16[96,3072]{1,0:T(8,128)(2,1)} async-done(((bf16[768,3072]{1,0:T(8,128)(2,1)}), bf16[96,3072]{1,0:T(8,128)(2,1)}) %reduce-scatter.21.cloned.1.call-update) | async-done | bytes 589840 | tf_op jit(solution)/shard_map/reduce_scatter | solution.py:255
  629.4 55.6 %reduce-scatter.15.cloned.1.call-done = bf16[384,768]{1,0:T(8,128)(2,1)} async-done(((bf16[3072,768]{1,0:T(8,128)(2,1)}), bf16[384,768]{1,0:T(8,128)(2,1)}) %reduce-scatter.15.cloned.1.call-update) | async-done | bytes 589840 | tf_op jit(solution)/shard_map/reduce_scatter | solution.py:243
  685.1 21.2 %add_convert_fusion = bf16[1024,3,2304]{0,2,1:T(8,128)(2,1)} fusion(f32[1024,3,576]{0,2,1:T(8,128)} %broadcast_select_fusion, f32[1024,3,64]{0,2,1:T(8,128)S(1)} %copy-done.23, bf16[1024,3,1024]{0,2,1:T(8,128)(2,1)} %bitcast.200, pred[1024]{0:T(1024)(128)(4,1)S(1)} %copy-done.44, bf16[2304,1024]{1,0:T(8,128)(2,1)} %param.27), kind=kOutput, calls=%fused_computation.61 | convolution fusion | flops 14523826176 | bytes 33031168 | tf_op jit(solution)/shard_map/tck,pk->tcp/dot_general | solution.py:224
  706.3 18.6 %copy.179 = bf16[1024,6912]{1,0:T(8,128)(2,1)} copy(bf16[1024,6912]{0,1:T(8,128)(2,1)} %bitcast.207) | data formatting | bytes 28311552
  724.9 13.9 %all-reduce.2 = bf16[3072]{0:T(1024)(128)(2,1)S(1)} all-reduce(bf16[3072]{0:T(1024)(128)(2,1)S(1)} %copy-done.42), channel_id=9, replica_groups=mesh['rep'=4,'fsdp'=8] {'fsdp'}, use_global_device_ids=true, to_apply=%region_42.43.clone | all-reduce | flops 3072 | bytes 12288
  739.8 7.4 reduce-scatter.27.cloned.1.call-done
  748.0 30.6 %reduce-scatter.25.cloned.1.call-done = bf16[96,49]{1,0:T(8,128)(2,1)} async-done(((bf16[768,49]{1,0:T(8,128)(2,1)}), bf16[96,49]{1,0:T(8,128)(2,1)}) %reduce-scatter.25.cloned.1.call-update) | async-done | bytes 9424
  779.4 16.5 %all-reduce.3 = (bf16[49,96]{1,0:T(8,128)(2,1)S(1)}, bf16[7,96]{1,0:T(8,128)(2,1)S(1)}, bf16[384]{0:T(512)(128)(2,1)S(1)}, bf16[2,96]{1,0:T(2,128)(2,1)S(1)}) all-reduce(bf16[49,96]{1,0:T(8,128)(2,1)S(1)} %copy.189, bf16[7,96]{1,0:T(8,128)(2,1)S(1)} %copy.191, ...), channel_id=1, replica_groups=mesh['rep'=4,'fsdp'=8] {'rep'}, use_global_device_ids=true, to_apply=%region_24.25 | all-reduce | flops 5952 | bytes 23808 | tf_op jit(solution)/shard_map/psum | solution.py:273
  798.3 56.9 %all-reduce.7.cloned.1.call-done = (bf16[384,768]{1,0:T(8,128)(2,1)}, bf16[96,2304]{1,0:T(8,128)(2,1)}, bf16[96,768]{1,0:T(8,128)(2,1)}, bf16[96,3072]{1,0:T(8,128)(2,1)}, bf16[384,768]{1,0:T(8,128)(2,1)}) async-done(((bf16[384,768]{1,0:T(8,128)(2,1)}, bf16[96,2304]{1,0:T(8,128)(2,1)}, bf16[96,768]{1,0:T(8,128)(2,1)}, bf16[96,3072]{1,0:T(8,128)(2,1)}, bf16[384,768]{1,0:T(8,128)(2,1)}), ...) | async-done | bytes 2359312 | tf_op jit(solution)/shard_map/psum | solution.py:272
  (391 shorter events, 338.6 us)
Async XLA Ops:
  7.2 83.2 %copy-start = (bf16[576,1024]{1,0:T(8,128)(2,1)S(1)}, bf16[576,1024]{1,0:T(8,128)(2,1)}, u32[]{:S(2)}) copy-start(bf16[576,1024]{1,0:T(8,128)(2,1)} %param.26) | copy-start | bytes 3538948
  7.2 62.7 %copy-start.28 = (bf16[900,49]{0,1:T(8,128)(2,1)S(1)}, bf16[900,49]{0,1:T(8,128)(2,1)}, u32[]{:S(2)}) copy-start(bf16[900,49]{0,1:T(8,128)(2,1)} %param.28) | copy-start | bytes 264604
  7.2 62.9 %copy-start.13 = (bf16[1024,768]{1,0:T(8,128)(2,1)S(1)}, bf16[1024,768]{1,0:T(8,128)(2,1)}, u32[]{:S(2)}) copy-start(bf16[1024,768]{1,0:T(8,128)(2,1)} %param.31) | copy-start | bytes 4718596
  7.2 136.8 %all-gather.10.cloned.1.call-start = ((), (), s32[]{:S(2)}) async-start(), calls=%async_computation.8 | async-start | bytes 5308416 | tf_op jit(solution)/shard_map/all_gather | solution.py:95
  7.9 148.5 %all-gather.12.cloned.1.call-start = ((), (), s32[]{:S(2)}) async-start(), calls=%async_computation.9 | async-start | bytes 3981312 | tf_op jit(solution)/shard_map/all_gather | solution.py:97
  8.7 238.4 %all-gather.14.cloned.1.call-start = ((), (), s32[]{:S(2)}) async-start(), calls=%async_computation.10 | async-start | bytes 1327104 | tf_op jit(solution)/shard_map/all_gather | solution.py:98
  9.4 244.2 %all-gather.16.cloned.1.call-start = ((), (), s32[]{:S(2)}) async-start(), calls=%async_computation.11 | async-start | bytes 5308416 | tf_op jit(solution)/shard_map/all_gather | solution.py:99
  10.0 255.0 %all-gather.18.cloned.1.call-start = ((), (), s32[]{:S(2)}) async-start(), calls=%async_computation.12 | async-start | bytes 5308416 | tf_op jit(solution)/shard_map/all_gather | solution.py:100
  10.6 573.9 %reduce-scatter.19.cloned.1.call-start = ((), (), s32[]{:S(2)}) async-start(), calls=%async_computation.15 | async-start | bytes 1327104 | tf_op jit(solution)/shard_map/reduce_scatter | solution.py:252
  26.2 130.3 %copy-start.31 = (f32[768]{0:T(1024)}, f32[768]{0:T(1024)S(1)}, u32[]{:S(2)}) copy-start(f32[768]{0:T(1024)S(1)} %get-tuple-element.307) | copy-start | bytes 9220
  53.5 103.0 %copy-start.50 = (f32[768]{0:T(1024)}, f32[768]{0:T(1024)S(1)}, u32[]{:S(2)}) copy-start(f32[768]{0:T(1024)S(1)} %get-tuple-element.304) | copy-start | bytes 9220
  54.4 98.5 %copy-start.45 = (pred[1024]{0:T(1024)(128)(4,1)}, pred[1024]{0:T(1024)(128)(4,1)S(1)}, u32[]{:S(2)}) copy-start(pred[1024]{0:T(1024)(128)(4,1)S(1)} %get-tuple-element.380) | copy-start | bytes 3076
  54.4 98.5 %copy-start.46 = (pred[1024]{0:T(1024)(128)(4,1)}, pred[1024]{0:T(1024)(128)(4,1)S(1)}, u32[]{:S(2)}) copy-start(pred[1024]{0:T(1024)(128)(4,1)S(1)} %get-tuple-element.381) | copy-start | bytes 3076
  54.4 98.5 %copy-start.47 = (pred[1024]{0:T(1024)(128)(4,1)}, pred[1024]{0:T(1024)(128)(4,1)S(1)}, u32[]{:S(2)}) copy-start(pred[1024]{0:T(1024)(128)(4,1)S(1)} %get-tuple-element.382) | copy-start | bytes 3076
  108.6 44.3 %copy-start.38 = (pred[1024]{0:T(1024)(128)(4,1)}, pred[1024]{0:T(1024)(128)(4,1)S(1)}, u32[]{:S(2)}) copy-start(pred[1024]{0:T(1024)(128)(4,1)S(1)} %get-tuple-element.377) | copy-start | bytes 3076
  108.6 44.3 %copy-start.43 = (pred[1024]{0:T(1024)(128)(4,1)}, pred[1024]{0:T(1024)(128)(4,1)S(1)}, u32[]{:S(2)}) copy-start(pred[1024]{0:T(1024)(128)(4,1)S(1)} %get-tuple-element.379) | copy-start | bytes 3076
  108.6 44.3 %copy-start.48 = (pred[1024]{0:T(1024)(128)(4,1)}, pred[1024]{0:T(1024)(128)(4,1)S(1)}, u32[]{:S(2)}) copy-start(pred[1024]{0:T(1024)(128)(4,1)S(1)} %get-tuple-element.378) | copy-start | bytes 3076
  111.9 41.1 %copy-start.19 = (bf16[1024,49]{1,0:T(8,128)(2,1)}, bf16[1024,49]{1,0:T(8,128)(2,1)S(1)}, u32[]{:S(2)}) copy-start(bf16[1024,49]{1,0:T(8,128)(2,1)S(1)} %gather_fusion.1) | copy-start | bytes 301060
  303.3 281.1 %reduce-scatter.17.cloned.1.call-start = ((), (), s32[]{:S(2)}) async-start(), calls=%async_computation.14 | async-start | bytes 3981312 | tf_op jit(solution)/shard_map/reduce_scatter | solution.py:249
  316.0 150.2 %copy-start.30 = (f32[1024]{0:T(1024)S(1)}, f32[1024]{0:T(1024)}, u32[]{:S(2)}) copy-start(f32[1024]{0:T(1024)} %copy-done.29) | copy-start | bytes 12292
  316.0 150.2 %copy-start.32 = (f32[768]{0:T(1024)S(1)}, f32[768]{0:T(1024)}, u32[]{:S(2)}) copy-start(f32[768]{0:T(1024)} %copy-done.31) | copy-start | bytes 9220
  316.0 150.2 %copy-start.34 = (f32[1024]{0:T(1024)S(1)}, f32[1024]{0:T(1024)}, u32[]{:S(2)}) copy-start(f32[1024]{0:T(1024)} %copy-done.33) | copy-start | bytes 12292
  316.0 150.2 %copy-start.51 = (f32[768]{0:T(1024)S(1)}, f32[768]{0:T(1024)}, u32[]{:S(2)}) copy-start(f32[768]{0:T(1024)} %copy-done.50) | copy-start | bytes 9220
  475.3 109.2 %reduce-scatter.23.cloned.1.call-start = ((), (), s32[]{:S(2)}) async-start(), calls=%async_computation.17 | async-start | bytes 5308416 | tf_op jit(solution)/shard_map/reduce_scatter | solution.py:258
  488.7 140.7 %reduce-scatter.21.cloned.1.call-start = ((), (), s32[]{:S(2)}) async-start(), calls=%async_computation.16 | async-start | bytes 5308416 | tf_op jit(solution)/shard_map/reduce_scatter | solution.py:255
  499.1 185.9 %reduce-scatter.15.cloned.1.call-start = ((), (), s32[]{:S(2)}) async-start(), calls=%async_computation.13 | async-start | bytes 5308416 | tf_op jit(solution)/shard_map/reduce_scatter | solution.py:243
  528.2 210.8 %reduce-scatter.29.cloned.1.call-start = ((), (), s32[]{:S(2)}) async-start(), calls=%async_computation.20 | async-start | bytes 221184
  560.3 186.9 %reduce-scatter.27.cloned.1.call-start = ((), (), s32[]{:S(2)}) async-start(), calls=%async_computation.19 | async-start | bytes 221184
  561.4 217.2 %reduce-scatter.25.cloned.1.call-start = ((), (), s32[]{:S(2)}) async-start(), calls=%async_computation.18 | async-start | bytes 221184
  567.1 288.1 %all-reduce.7.cloned.1.call-start = ((), (), s32[]{:S(2)}) async-start(), calls=%async_computation.21 | async-start | bytes 4718592 | tf_op jit(solution)/shard_map/psum | solution.py:272
  581.8 103.2 %copy-start.23 = (f32[1024,3,64]{0,2,1:T(8,128)S(1)}, f32[1024,3,64]{0,2,1:T(8,128)}, u32[]{:S(2)}) copy-start(f32[1024,3,64]{0,2,1:T(8,128)} %convolution_select_fusion) | copy-start | bytes 2359300
  581.8 103.2 %copy-start.44 = (pred[1024]{0:T(1024)(128)(4,1)S(1)}, pred[1024]{0:T(1024)(128)(4,1)}, u32[]{:S(2)}) copy-start(pred[1024]{0:T(1024)(128)(4,1)} %copy-done.43) | copy-start | bytes 3076
  (41 other events, 343.6 us)
Sparse Core Ops, SparseCore 0:
  9.7 55.0 all-gather.9
  66.4 40.3 all-gather.11
  108.4 21.5 all-gather.13
  131.5 51.4 all-gather.15
  184.5 50.5 all-gather.17
  303.5 31.2 reduce-scatter.18
  475.4 42.2 reduce-scatter.16
  520.1 53.4 reduce-scatter.22
  576.1 53.3 reduce-scatter.20
  631.7 53.3 reduce-scatter.14
  687.4 28.6 reduce-scatter.28
  718.8 28.4 reduce-scatter.26
  750.1 28.4 reduce-scatter.24
  782.0 73.1 all-reduce.6
where the time goes:
time: 884 us; the launch traced here: 870 us
  matrix products  399 us (45%)
  waiting for transfers between devices  199 us (23%)
  local copies, waits for them, and re-layouts  116 us (13%)
  blocking collectives  84.5 us (10%)
  other arithmetic  54.6 us (6%)
  between operations  15.7 us (2%)
    unnamed x137, local copies, waits for them, and re-layouts  71.6 us
    psum x1, waiting for transfers between devices, local(): lax.psum(summed[0].astype(jnp.bfloat16), 'rep').astype(jnp.float32)  56.9 us
    reduce_scatter x1, waiting for transfers between devices, local(): lax.psum_scatter(grad_kernel.astype(jnp.bfloat16), 'fsdp', scatter_dimens...  55.6 us
    dot_general x24, matrix products, masked_scores(): jnp.einsum('qd,kd->qk', query, keys_block, preferred_element_type=jnp.flo...  54 us
    reduce_scatter x1, waiting for transfers between devices, local(): lax.psum_scatter(grad_up.astype(jnp.bfloat16), 'fsdp', scatter_dimension=...  44.9 us
    dot_general x3, matrix products, local(): jnp.einsum('tcp,pk->tck', pixel_frame[:, :, :area], matrix, preferred_ele...  43.8 us
    unnamed x17, waiting for transfers between devices  41.3 us
    dot_general x3, matrix products, local(): jnp.einsum('tck,pk->tcp', g_resized, matrix, preferred_element_type=jnp.f...  32 us
  transfers between devices with their start and end apart: 14, of which 5 were waited for; matrix products, arithmetic and copies ran while one was open for 59% of the time, Pallas kernels for 0%

commit v1 on v0

v1 whole, which is shorter than its diff:
```python
import jax
import jax.numpy as jnp
from jax import lax
from jax.experimental import pallas as pl
from jax.experimental.pallas import tpu as pltpu
from jax.sharding import PartitionSpec as P

HEADS = 12
GRID_A = 30
GRID_B = 10
GRID_C = 5
CHUNK = 16
TILE = 256
F32 = jnp.float32
BF16 = jnp.bfloat16
NEG = -1e30
VMEM = 60 * 1024 * 1024


def nt(a, b):
    return lax.dot_general(a, b, (((1,), (1,)), ((), ())), preferred_element_type=F32)


def nn(a, b):
    return lax.dot_general(a, b, (((1,), (0,)), ((), ())), preferred_element_type=F32)


def tn(a, b):
    return lax.dot_general(a, b, (((0,), (0,)), ((), ())), preferred_element_type=F32)


def params(**more):
    return pltpu.CompilerParams(vmem_limit_bytes=VMEM, **more)


def cost(flops, moved, exps=0):
    return pl.CostEstimate(flops=int(flops), bytes_accessed=int(moved), transcendentals=int(exps))


def token_layout(classes, tokens_here):
    class_tokens = jnp.array(
        [GRID_A * GRID_A, GRID_B * GRID_B, GRID_C * GRID_C, 0], dtype=jnp.int32
    )
    class_ids = jnp.arange(4, dtype=jnp.int32)
    image_tokens = jnp.sum(
        jnp.where(classes[:, None] == class_ids[None, :], class_tokens[None, :], 0), axis=1
    )
    image_ends = jnp.cumsum(image_tokens)
    image_starts = image_ends - image_tokens
    positions = jnp.arange(tokens_here, dtype=jnp.int32)
    segment = jnp.sum((image_ends[None, :] <= positions[:, None]).astype(jnp.int32), axis=1)
    membership = segment[:, None] == jnp.arange(classes.shape[0], dtype=jnp.int32)[None, :]
    live_rows = jnp.any(membership, axis=1)
    category = jnp.sum(jnp.where(membership, classes[None, :], 0), axis=1) + jnp.where(
        live_rows, 0, 3
    )
    offset = positions - jnp.sum(jnp.where(membership, image_starts[None, :], 0), axis=1)
    return (segment, category, offset, live_rows)


def chunk_lists(category):
    chunks = category.reshape(-1, CHUNK)
    here = jnp.any(chunks[None, :, :] == jnp.arange(3, dtype=jnp.int32)[:, None, None], axis=2)
    place = jnp.cumsum(here.astype(jnp.int32), axis=1) - 1
    count = chunks.shape[0]
    ids = jnp.arange(count, dtype=jnp.int32)
    hit = here[:, :, None] & (place[:, :, None] == ids[None, None, :])
    listed = jnp.sum(jnp.where(hit, ids[None, :, None], 0), axis=1)
    return jnp.concatenate([place[:, -1:] + 1, listed], axis=1).astype(jnp.int32)


def resize_rows(lists, cat_ref, src_ref, out_ref, lhs, class_id, width, product, columns):
    number = lists[class_id, 0]

    @pl.loop(0, (number + TILE // CHUNK - 1) // (TILE // CHUNK))
    def _(t):
        base = t * (TILE // CHUNK)
        for u in range(TILE // CHUNK):
            row = pl.multiple_of(lists[class_id, 1 + jnp.minimum(base + u, number - 1)] * CHUNK, CHUNK)
            lhs[u * CHUNK : (u + 1) * CHUNK, 0:width] = src_ref[pl.ds(row, CHUNK), 0:width]
        total = product(lhs[:, 0:width])
        for u in range(TILE // CHUNK):

            @pl.when(base + u < number)
            def _():
                row = pl.multiple_of(lists[class_id, 1 + base + u] * CHUNK, CHUNK)
                mine = cat_ref[pl.ds(row, CHUNK), :] == class_id
                old = out_ref[pl.ds(row, CHUNK), 0:columns].astype(F32)
                new = total[u * CHUNK : (u + 1) * CHUNK, :]
                out_ref[pl.ds(row, CHUNK), 0:columns] = jnp.where(mine, new, old).astype(
                    out_ref.dtype
                )


def resize_kernel(lists, px_ref, cat_ref, ra_ref, rb_ref, rc_ref, out_ref, lhs):
    out_ref[...] = jnp.zeros_like(out_ref)
    for class_id, matrix in enumerate((ra_ref, rb_ref, rc_ref)):
        resize_rows(
            lists, cat_ref, px_ref, out_ref, lhs, class_id, matrix.shape[0],
            lambda rows, matrix=matrix: nn(rows, matrix[...]), matrix.shape[1],
        )


def resize(lists, pixels, category, ra, rb, rc):
    tokens, wide = pixels.shape
    area = wide // 3
    base = rc.shape[1]
    whole = lambda a: pl.BlockSpec(a.shape, lambda c, s: (0, 0))
    return pl.pallas_call(
        resize_kernel,
        grid_spec=pltpu.PrefetchScalarGridSpec(
            num_scalar_prefetch=1,
            grid=(3,),
            in_specs=[pl.BlockSpec((tokens, area), lambda c, s: (0, c)), whole(category), whole(ra), whole(rb), whole(rc)],
            out_specs=pl.BlockSpec((tokens, base), lambda c, s: (0, c)),
            scratch_shapes=[pltpu.VMEM((TILE, area), BF16)],
        ),
        out_shape=jax.ShapeDtypeStruct((tokens, 3 * base), BF16),
        compiler_params=params(),
        cost_estimate=cost(tokens * 3 * base * 1200 * 2, tokens * wide * 2 + tokens * base * 6),
        name="resize",
    )(lists, pixels, category, ra, rb, rc)


def unresize_kernel(lists, g_ref, w_ref, cat_ref, ra_ref, rb_ref, rc_ref, out_ref, grow, lhs):
    tokens = g_ref.shape[0]
    out_ref[...] = jnp.zeros_like(out_ref)

    @pl.loop(0, tokens // TILE)
    def _(t):
        rows = pl.ds(pl.multiple_of(t * TILE, TILE), TILE)
        grow[rows, :] = nt(g_ref[rows, :], w_ref[0, 0]).astype(BF16)

    for class_id, matrix in enumerate((ra_ref, rb_ref, rc_ref)):
        resize_rows(
            lists, cat_ref, grow, out_ref, lhs, class_id, grow.shape[1],
            lambda rows, matrix=matrix: nt(rows, matrix[...]), matrix.shape[0],
        )


def unresize(lists, g_emb, groups, category, ra, rb, rc, area):
    tokens, width = g_emb.shape
    base = rc.shape[1]
    whole = lambda a: pl.BlockSpec(a.shape, lambda c, s: (0, 0))
    kernels = groups.reshape(4, 3, base, width)
    return pl.pallas_call(
        unresize_kernel,
        grid_spec=pltpu.PrefetchScalarGridSpec(
            num_scalar_prefetch=1,
            grid=(3,),
            in_specs=[
                whole(g_emb), pl.BlockSpec((1, 1, base, width), lambda c, s: (0, c, 0, 0)),
                whole(category), whole(ra), whole(rb), whole(rc),
            ],
            out_specs=pl.BlockSpec((tokens, area), lambda c, s: (0, c)),
            scratch_shapes=[pltpu.VMEM((tokens, base), BF16), pltpu.VMEM((TILE, base), BF16)],
        ),
        out_shape=jax.ShapeDtypeStruct((tokens, 3 * area), BF16),
        compiler_params=params(),
        cost_estimate=cost(tokens * 3 * base * 2000 * 2, tokens * area * 6 + tokens * base * 6),
        name="unresize",
    )(lists, g_emb, kernels, category, ra, rb, rc)


def norm_parts(values):
    center = values - jnp.mean(values, axis=-1, keepdims=True)
    rstd = lax.rsqrt(jnp.mean(center * center, axis=-1, keepdims=True) + 1e-06)
    return center * rstd, rstd


def norm_back(xhat, rstd, grad, gain):
    dxhat = grad * gain
    return rstd * (
        dxhat
        - jnp.mean(dxhat, axis=-1, keepdims=True)
        - xhat * jnp.mean(dxhat * xhat, axis=-1, keepdims=True)
    )


def square(ref):
    value = ref[...]
    return value.reshape(-1, value.shape[-1])


def row_tiles(tokens, body):
    @pl.loop(0, tokens // TILE)
    def _(t):
        body(pl.ds(pl.multiple_of(t * TILE, TILE), TILE))


def embed_kernel(res_ref, kern_ref, qkv_ref, pos_ref, table_ref, small_ref, embed_ref, norm_ref, proj_ref):
    step = pl.program_id(0)
    tokens = res_ref.shape[0]

    @pl.when(step == 0)
    def _():
        def body(rows):
            embed_ref[rows, :] = (
                nn(res_ref[rows, :], square(kern_ref)) + small_ref[0:1, :] + nn(pos_ref[rows, :], table_ref[...])
            )

        row_tiles(tokens, body)

    @pl.when((step > 0) & (step < 4))
    def _():
        def body(rows):
            embed_ref[rows, :] += nn(res_ref[rows, :], square(kern_ref))

        row_tiles(tokens, body)

    @pl.when(step == 3)
    def _():
        def body(rows):
            xhat, _ = norm_parts(embed_ref[rows, :])
            norm_ref[rows, :] = (xhat * small_ref[7:8, :] + small_ref[1:2, :]).astype(BF16)

        row_tiles(tokens, body)

    @pl.when(step >= 4)
    def _():
        shift = jnp.where(
            step == 4, small_ref[2:3, :], jnp.where(step == 6, small_ref[3:4, :], jnp.zeros_like(small_ref[3:4, :]))
        )

        def body(rows):
            proj_ref[rows, :] = (nn(norm_ref[rows, :], square(qkv_ref)) + shift).astype(BF16)

        row_tiles(tokens, body)


def embed_call(resized, rowwise, colwise, pos_rows, table, small):
    tokens = resized.shape[0]
    width = small.shape[1]
    bands, deep = colwise.shape[1], colwise.shape[3]
    whole = lambda a: pl.BlockSpec(a.shape, lambda s: (0, 0))
    fixed = pl.BlockSpec((tokens, width), lambda s: (0, 0))
    return pl.pallas_call(
        embed_kernel,
        grid=(7,),
        in_specs=[
            pl.BlockSpec((tokens, width), lambda s: (0, jnp.minimum(s, 3))),
            pl.BlockSpec((1, 1, width, width), lambda s: (0, jnp.minimum(s, 3), 0, 0)),
            pl.BlockSpec((1, bands, 1, deep, width), lambda s: (1, 0, jnp.maximum(s - 4, 0), 0, 0)),
            whole(pos_rows), whole(table), whole(small),
        ],
        out_specs=[fixed, fixed, pl.BlockSpec((tokens, width), lambda s: (0, jnp.maximum(s - 4, 0)))],
        out_shape=[
            jax.ShapeDtypeStruct((tokens, width), F32),
            jax.ShapeDtypeStruct((tokens, width), BF16),
            jax.ShapeDtypeStruct((tokens, 3 * width), BF16),
        ],
        compiler_params=params(),
        cost_estimate=cost(7 * 2 * tokens * width * width, tokens * width * 20 + 7 * width * width * 2),
        name="embed",
    )(resized, rowwise, colwise, pos_rows, table, small)


def attend_kernel(dense_ref, q_ref, k_ref, v_ref, oh_ref, km_ref, o_ref, lse_ref, kaug, vaug):
    tokens = q_ref.shape[0]
    lane = lax.broadcasted_iota(jnp.int32, (1, 128), 1)
    kaug[:, 0:128] = k_ref[...]
    kaug[:, 128:256] = km_ref[...]
    vaug[:, 0:128] = v_ref[...]
    vaug[:, 128:256] = jnp.ones((tokens, 128), BF16)

    def tile(rows, cols):
        q = q_ref[rows, :] * jnp.asarray(0.125, BF16)
        oh = oh_ref[rows, :]
        keys, vals = kaug[cols, :], vaug[cols, :]
        outs, logs = [], []
        for h in range(2):
            mine = (lane < 64) if h == 0 else (lane >= 64)
            left = jnp.concatenate([jnp.where(mine, q, jnp.zeros_like(q)), oh], axis=1)
            scores = nt(left, keys)
            top = jnp.max(scores, axis=1, keepdims=True)
            weights = jnp.exp(scores - top).astype(BF16)
            both = nn(weights, vals)
            total = both[:, 128:256]
            outs.append(both[:, 0:128] / total)
            logs.append(top + jnp.log(total))
        o_ref[rows, :] = jnp.where(lane < 64, outs[0], outs[1]).astype(o_ref.dtype)
        lse_ref[rows, :] = jnp.where(lane < 64, logs[0], logs[1])

    attend_tiles(dense_ref, tokens, tile)


def attend_tiles(dense_ref, tokens, tile):
    @pl.when(dense_ref[0] != 0)
    def _():
        @pl.loop(0, tokens // TILE)
        def _(t):
            tile(pl.ds(pl.multiple_of(t * TILE, TILE), TILE), pl.ds(0, tokens))

    @pl.when(dense_ref[0] == 0)
    def _():
        @pl.loop(0, tokens // TILE)
        def _(t):
            first = pl.multiple_of(jnp.clip(t * TILE - 128, 0, tokens - 512), 128)
            tile(pl.ds(pl.multiple_of(t * TILE, TILE), TILE), pl.ds(first, 512))


def attend(dense, projected, onehot, keymask):
    tokens = projected.shape[0]
    pairs = projected.shape[1] // 3 // 128
    part = lambda at: pl.BlockSpec((tokens, 128), lambda j, d: (0, at + j))
    whole = pl.BlockSpec((tokens, 128), lambda j, d: (0, 0))
    return pl.pallas_call(
        attend_kernel,
        grid_spec=pltpu.PrefetchScalarGridSpec(
            num_scalar_prefetch=1,
            grid=(pairs,),
            in_specs=[part(0), part(pairs), part(2 * pairs), whole, whole],
            out_specs=[part(0), part(0)],
            scratch_shapes=[pltpu.VMEM((tokens, 256), BF16), pltpu.VMEM((tokens, 256), BF16)],
        ),
        out_shape=[
            jax.ShapeDtypeStruct((tokens, pairs * 128), BF16),
            jax.ShapeDtypeStruct((tokens, pairs * 128), F32),
        ],
        compiler_params=params(),
        cost_estimate=cost(2 * 2 * 12 * tokens * tokens * 256, tokens * 2304 * 2 + tokens * 768 * 6, 12 * tokens * tokens),
        name="attend",
    )(dense, projected, projected, projected, onehot, keymask)


def split3(x):
    high = x.astype(BF16)
    rest = x - high.astype(F32)
    middle = rest.astype(BF16)
    low = (rest - middle.astype(F32)).astype(BF16)
    return high, middle, low


def attend_back_kernel(
    dense_ref, q_ref, k_ref, v_ref, g_ref, o_ref, lse_ref, oh_ref, km_ref, out_ref, kaug, vaug, dkeys, dvals
):
    tokens = q_ref.shape[0]
    lane = lax.broadcasted_iota(jnp.int32, (1, 128), 1)
    kaug[:, 0:128] = k_ref[...]
    kaug[:, 128:256] = km_ref[...]
    vaug[:, 0:128] = v_ref[...]
    vaug[:, 128:256] = jnp.broadcast_to(jnp.where(lane < 3, -1.0, 0.0).astype(BF16), (tokens, 128))
    dkeys[...] = jnp.zeros_like(dkeys)
    dvals[...] = jnp.zeros_like(dvals)

    def put(parts, at, other):
        for i, piece in enumerate(parts):
            other = jnp.where(lane == at + i, piece, other)
        return other

    def tile(rows, cols):
        q = q_ref[rows, :] * jnp.asarray(0.125, BF16)
        g = g_ref[rows, :]
        oh = oh_ref[rows, :]
        go = g.astype(F32) * o_ref[rows, :].astype(F32)
        lse = lse_ref[rows, :]
        keys, vals = kaug[cols, :], vaug[cols, :]
        plain = keys[:, 0:128]
        dqs, dkt, dvt = [], None, None
        for h in range(2):
            mine = (lane < 64) if h == 0 else (lane >= 64)
            delta = jnp.sum(jnp.where(mine, go, 0.0), axis=1, keepdims=True)
            qm = jnp.where(mine, q, jnp.zeros_like(q))
            gm = jnp.where(mine, g, jnp.zeros_like(g))
            qa = jnp.concatenate([qm, put(split3(lse[:, 64 * h : 64 * h + 1]), 64, oh)], axis=1)
            ga = jnp.concatenate([gm, put(split3(delta), 0, jnp.zeros_like(oh))], axis=1)
            probs = jnp.exp(nt(keys, qa))
            dscores = (probs * nt(vals, ga)).astype(BF16)
            a, b = nn(probs.astype(BF16), gm), nn(dscores, qm)
            dvt = a if dvt is None else dvt + a
            dkt = b if dkt is None else dkt + b
            dqs.append(tn(dscores, plain))
        out_ref[0, rows, :] = (jnp.where(lane < 64, dqs[0], dqs[1]) * 0.125).astype(BF16)
        dkeys[cols, :] += dkt
        dvals[cols, :] += dvt

    attend_tiles(dense_ref, tokens, tile)
    out_ref[1] = dkeys[...].astype(BF16)
    out_ref[2] = dvals[...].astype(BF16)


def attend_back(dense, projected, g_mixed, mixed, lse, onehot, keymask):
    tokens = projected.shape[0]
    pairs = projected.shape[1] // 3 // 128
    part = lambda at: pl.BlockSpec((tokens, 128), lambda j, d: (0, at + j))
    whole = pl.BlockSpec((tokens, 128), lambda j, d: (0, 0))
    return pl.pallas_call(
        attend_back_kernel,
        grid_spec=pltpu.PrefetchScalarGridSpec(
            num_scalar_prefetch=1,
            grid=(pairs,),
            in_specs=[part(0), part(pairs), part(2 * pairs), part(0), part(0), part(0), whole, whole],
            out_specs=pl.BlockSpec((3, tokens, 128), lambda j, d: (0, 0, j)),
            scratch_shapes=[
                pltpu.VMEM((tokens, 256), BF16), pltpu.VMEM((tokens, 256), BF16),
                pltpu.VMEM((tokens, 128), F32), pltpu.VMEM((tokens, 128), F32),
            ],
        ),
        out_shape=jax.ShapeDtypeStruct((3, tokens, pairs * 128), BF16),
        compiler_params=params(),
        cost_estimate=cost(5 * 2 * 12 * tokens * tokens * 256, tokens * 768 * 22, 12 * tokens * tokens),
        name="attend_back",
    )(dense, projected, projected, projected, g_mixed, mixed, lse, onehot, keymask)


def mlp_kernel(
    embed_ref, mixed_ref, cot_ref, live_ref, small_ref, shift_ref, wo_ref, up_ref, down_ref,
    out_ref, ghid_ref, gmixed_ref, gdown_ref, gup_ref, gwo_ref, sums_ref, gshift_ref,
    hidden, xhats, norm2, gbranch, total, gnorm, act, gpre,
):
    step = pl.program_id(0)
    tokens = embed_ref.shape[0]

    @pl.when(step == 0)
    def _():
        def body(rows):
            value = embed_ref[rows, :] + nn(mixed_ref[rows, :], square(wo_ref)) + small_ref[4:5, :]
            hidden[rows, :] = value
            total[rows, :] = value + small_ref[6:7, :]
            xhat, _ = norm_parts(value)
            norm2[rows, :] = (xhat * small_ref[8:9, :] + small_ref[5:6, :]).astype(BF16)
            gbranch[rows, :] = (cot_ref[rows, :].astype(F32) * live_ref[rows, :]).astype(BF16)
            gnorm[rows, :] = jnp.zeros((TILE, gnorm.shape[1]), F32)

        row_tiles(tokens, body)

    up, down = square(up_ref), square(down_ref)

    def body(rows):
        x = nn(norm2[rows, :], up) + shift_ref[0]
        square_x = x * x
        t = jnp.tanh(0.7978845608028654 * (x + 0.044715 * (square_x * x)))
        half = 0.5 * (1.0 + t)
        acts = (x * half).astype(BF16)
        act[rows, :] = acts
        total[rows, :] += nn(acts, down)
        slope = half + 0.5 * x * (1.0 - t * t) * (
            0.7978845608028654 + (0.7978845608028654 * 3 * 0.044715) * square_x
        )
        gp = (nt(gbranch[rows, :], down) * slope).astype(BF16)
        gpre[rows, :] = gp
        gnorm[rows, :] += nt(gp, up)

    row_tiles(tokens, body)
    gdown_ref[0] = tn(act[...], gbranch[...]).astype(BF16)
    gup_ref[...] = tn(norm2[...], gpre[...]).astype(BF16).reshape(gup_ref.shape)
    gshift_ref[0] = jnp.sum(gpre[...].astype(F32), axis=0, keepdims=True)

    @pl.when(step == 3)
    def _():
        sums_ref[...] = jnp.zeros_like(sums_ref)
        wo = square(wo_ref)

        def body(rows):
            out_ref[rows, :] = (total[rows, :] * live_ref[rows, :]).astype(BF16)
            xhat, rstd = norm_parts(hidden[rows, :])
            grad = gnorm[rows, :]
            gout = gbranch[rows, :].astype(F32)
            ghid = gout + norm_back(xhat, rstd, grad, small_ref[8:9, :])
            ghid_ref[rows, :] = ghid
            gmix = ghid.astype(BF16)
            xhats[rows, :] = gmix
            gmixed_ref[rows, :] = nt(gmix, wo).astype(BF16)
            sums_ref[4:5, :] += jnp.sum(gmix.astype(F32), axis=0, keepdims=True)
            sums_ref[5:6, :] += jnp.sum(grad, axis=0, keepdims=True)
            sums_ref[6:7, :] += jnp.sum(gout, axis=0, keepdims=True)
            sums_ref[8:9, :] += jnp.sum(grad * xhat, axis=0, keepdims=True)

        row_tiles(tokens, body)
        gwo_ref[...] = tn(mixed_ref[...], xhats[...]).astype(BF16).reshape(gwo_ref.shape)


def mlp_call(embed, mixed, cotangent, live, small, shift, rowwise, colwise):
    tokens, width = embed.shape
    bands, deep = colwise.shape[1], colwise.shape[3]
    fixed = pl.BlockSpec((tokens, width), lambda s: (0, 0))
    whole = lambda a: pl.BlockSpec(a.shape, lambda s: (0, 0))
    band = lambda group, at: pl.BlockSpec((1, bands, 1, deep, width), lambda s: (group, 0, at(s), 0, 0))
    scratch = lambda kind: pltpu.VMEM((tokens, width), kind)
    return pl.pallas_call(
        mlp_kernel,
        grid=(4,),
        in_specs=[
            fixed, fixed, fixed, whole(live), whole(small),
            pl.BlockSpec((1, 1, width), lambda s: (s, 0, 0)),
            band(1, lambda s: 3), band(2, lambda s: s),
            pl.BlockSpec((1, 1, width, width), lambda s: (3, s, 0, 0)),
        ],
        out_specs=[
            fixed, fixed, fixed,
            pl.BlockSpec((1, width, width), lambda s: (s, 0, 0)),
            pl.BlockSpec((bands, 1, deep, width), lambda s: (0, s, 0, 0)),
            pl.BlockSpec((bands, deep, width), lambda s: (0, 0, 0)),
            pl.BlockSpec((16, width), lambda s: (0, 0)),
            pl.BlockSpec((1, 1, width), lambda s: (s, 0, 0)),
        ],
        out_shape=[
            jax.ShapeDtypeStruct((tokens, width), BF16),
            jax.ShapeDtypeStruct((tokens, width), F32),
            jax.ShapeDtypeStruct((tokens, width), BF16),
            jax.ShapeDtypeStruct((4, width, width), BF16),
            jax.ShapeDtypeStruct((bands, 4, deep, width), BF16),
            jax.ShapeDtypeStruct((bands, deep, width), BF16),
            jax.ShapeDtypeStruct((16, width), F32),
            jax.ShapeDtypeStruct((4, 1, width), F32),
        ],
        scratch_shapes=[
            scratch(F32), scratch(BF16), scratch(BF16), scratch(BF16),
            scratch(F32), scratch(F32), scratch(BF16), scratch(BF16),
        ],
        compiler_params=params(),
        cost_estimate=cost(27 * 2 * tokens * width * width, tokens * width * 20 + 18 * width * width * 2),
        name="mlp",
    )(embed, mixed, cotangent, live, small, shift, colwise, colwise, rowwise)


def embed_back_kernel(
    dproj_ref, norm_ref, qkv_ref, embed_ref, ghid_ref, pos_ref, small_ref,
    gemb_ref, gqkv_ref, gpos_ref, sums_ref, gnorm,
):
    step = pl.program_id(0)
    tokens = embed_ref.shape[0]
    weight = square(qkv_ref)

    @pl.when(step == 0)
    def _():
        sums_ref[...] = jnp.zeros_like(sums_ref)

        def body(rows):
            gnorm[rows, :] = nt(dproj_ref[0, rows, :], weight)

        row_tiles(tokens, body)

    @pl.when(step > 0)
    def _():
        def body(rows):
            gnorm[rows, :] += nt(dproj_ref[0, rows, :], weight)

        row_tiles(tokens, body)

    gqkv_ref[...] = tn(norm_ref[...], dproj_ref[0]).astype(BF16).reshape(gqkv_ref.shape)
    column = jnp.sum(dproj_ref[0].astype(F32), axis=0, keepdims=True)

    @pl.when(step == 0)
    def _():
        sums_ref[2:3, :] = column

    @pl.when(step == 2)
    def _():
        sums_ref[3:4, :] = column

        def body(rows):
            xhat, rstd = norm_parts(embed_ref[rows, :])
            grad = gnorm[rows, :]
            gemb = (ghid_ref[rows, :] + norm_back(xhat, rstd, grad, small_ref[7:8, :])).astype(BF16)
            gemb_ref[rows, :] = gemb
            sums_ref[0:1, :] += jnp.sum(gemb.astype(F32), axis=0, keepdims=True)
            sums_ref[1:2, :] += jnp.sum(grad, axis=0, keepdims=True)
            sums_ref[7:8, :] += jnp.sum(grad * xhat, axis=0, keepdims=True)

        row_tiles(tokens, body)
        gpos_ref[...] = tn(pos_ref[...], gemb_ref[...])


def embed_back(dproj, normed1, colwise, embed, g_hidden, pos_rows, small):
    tokens, width = embed.shape
    bands, deep = colwise.shape[1], colwise.shape[3]
    fixed = pl.BlockSpec((tokens, width), lambda s: (0, 0))
    whole = lambda a: pl.BlockSpec(a.shape, lambda s: (0, 0))
    return pl.pallas_call(
        embed_back_kernel,
        grid=(3,),
        in_specs=[
            pl.BlockSpec((1, tokens, width), lambda s: (s, 0, 0)), fixed,
            pl.BlockSpec((1, bands, 1, deep, width), lambda s: (1, 0, s, 0, 0)),
            fixed, fixed, whole(pos_rows), whole(small),
        ],
        out_specs=[
            fixed, pl.BlockSpec((bands, 1, deep, width), lambda s: (0, s, 0, 0)),
            pl.BlockSpec((128, width), lambda s: (0, 0)), pl.BlockSpec((16, width), lambda s: (0, 0)),
        ],
        out_shape=[
            jax.ShapeDtypeStruct((tokens, width), BF16),
            jax.ShapeDtypeStruct((bands, 3, deep, width), BF16),
            jax.ShapeDtypeStruct((128, width), F32),
            jax.ShapeDtypeStruct((16, width), F32),
        ],
        scratch_shapes=[pltpu.VMEM((tokens, width), F32)],
        compiler_params=params(),
        cost_estimate=cost(6 * 2 * tokens * width * width, tokens * width * 18 + 6 * width * width * 2),
        name="embed_back",
    )(dproj, normed1, colwise, embed, g_hidden, pos_rows, small)


def patch_grad_kernel(res_ref, g_ref, out_ref):
    out_ref[0] = tn(res_ref[...], g_ref[...]).astype(BF16)


def patch_grad(resized, g_emb):
    tokens, width = g_emb.shape
    return pl.pallas_call(
        patch_grad_kernel,
        grid=(4,),
        in_specs=[pl.BlockSpec((tokens, width), lambda s: (0, s)), pl.BlockSpec((tokens, width), lambda s: (0, 0))],
        out_specs=pl.BlockSpec((1, width, width), lambda s: (s, 0, 0)),
        out_shape=jax.ShapeDtypeStruct((4, width, width), BF16),
        compiler_params=params(),
        cost_estimate=cost(4 * 2 * tokens * width * width, tokens * width * 10 + 4 * width * width * 2),
        name="patch_grad",
    )(resized, g_emb)


def local(reps, owners, *arrays):
    (
        pixels, image_class, resize_a, resize_b, resize_c, posmap_a, posmap_b, posmap_c, cotangent,
        patch_kernel, pos_table, qkv_weight, out_weight, up_weight, down_weight, biases, up_bias, gains,
    ) = arrays
    tokens = pixels.shape[0]
    width = out_weight.shape[1]
    depth = out_weight.shape[0]
    shard = patch_kernel.shape[0]
    cells = pos_table.shape[0]
    slots = image_class.shape[1]

    def stacked(shards):
        return jnp.concatenate([w.reshape(depth, -1, width).transpose(1, 0, 2) for w in shards]).reshape(shard, width)

    small_here = jnp.concatenate([biases, gains, pos_table, up_bias.reshape(-1, depth)])
    bundle = jnp.concatenate(
        [patch_kernel, stacked([qkv_weight, out_weight]), stacked([up_weight]), down_weight]
    )
    share = 4 * shard // reps
    here = lax.dynamic_slice(bundle, (lax.axis_index("rep") * share, 0), (share, width))
    groups = lax.all_gather(here, ("rep", "fsdp"), axis=0, tiled=True)
    small_all = lax.all_gather(small_here, "fsdp", axis=0, tiled=False)
    groups = (
        groups.reshape(4, reps // 4, owners, share, width).transpose(0, 2, 1, 3, 4).reshape(4, owners, shard, width)
    )
    rowwise = groups.reshape(4, 4, width, width)
    colwise = groups.reshape(4, owners, 4, depth, width)
    if depth % 16 != 0:
        colwise = colwise.transpose(0, 2, 1, 3, 4).reshape(4, 1, 4, width, width)
    rows_of = small_all[:, : 9 + cells].transpose(1, 0, 2).reshape(9 + cells, width)
    small = jnp.pad(rows_of[:9].astype(F32), ((0, 7), (0, 0)))
    table = jnp.pad(rows_of[9:], ((0, 128 - cells), (0, 0)))
    shift = small_all[:, 9 + cells :].reshape(4, 1, width).astype(F32)

    segment, category, offset, live_rows = token_layout(image_class[0], tokens)
    live = live_rows[:, None].astype(F32)
    lists = chunk_lists(category)
    dense = (image_class[0, :1] == 0).astype(jnp.int32)
    lane = jnp.arange(128, dtype=jnp.int32)[None, :]
    same = segment[:, None] == lane
    onehot = same.astype(BF16)
    keymask = jnp.where(
        lane <= slots, jnp.where(same, 0.0, NEG), jnp.where((lane >= 64) & (lane < 67), -1.0, 0.0)
    ).astype(BF16)
    maps = jnp.concatenate([posmap_a, posmap_b, posmap_c, jnp.zeros((1, cells), BF16)])
    maps = jnp.pad(maps, ((0, 0), (0, 128 - cells)))
    first = jnp.array([0, GRID_A * GRID_A, GRID_A * GRID_A + GRID_B * GRID_B], jnp.int32)
    at = jnp.where(category < 3, first[jnp.minimum(category, 2)] + offset, maps.shape[0] - 1)
    pos_rows = jnp.take(maps, at, axis=0)
    cats = category[:, None]
    ra = jnp.pad(resize_a, ((0, -resize_a.shape[0] % 128), (0, 0)))
    rb = jnp.pad(resize_b, ((0, -resize_b.shape[0] % 128), (0, 0)))

    resized = resize(lists, pixels, cats, ra, rb, resize_c)
    embed, normed1, projected = embed_call(resized, rowwise, colwise, pos_rows, table, small)
    mixed, lse = attend(dense, projected, onehot, keymask)
    output, g_hidden, g_mixed, g_down, g_up, g_out, sums_mlp, g_shift = mlp_call(
        embed, mixed, cotangent, live, small, shift, rowwise, colwise
    )
    dproj = attend_back(dense, projected, g_mixed, mixed, lse, onehot, keymask)
    g_emb, g_qkv, g_pos, sums_embed = embed_back(dproj, normed1, colwise, embed, g_hidden, pos_rows, small)
    g_kernel = patch_grad(resized, g_emb)
    grad_pixels = unresize(lists, g_emb, groups, cats, ra, rb, resize_c, pixels.shape[1] // 3)

    def bands_of(blocks, number):
        if blocks.shape[0] != owners:
            blocks = blocks.reshape(number, owners, depth, width).transpose(1, 0, 2, 3)
        return blocks.reshape(owners, number * depth, width)

    g_small = jnp.concatenate([(sums_mlp + sums_embed)[:9], g_pos[:cells]]).reshape(9 + cells, owners, depth)
    g_small = jnp.concatenate(
        [g_small.transpose(1, 0, 2), g_shift.reshape(owners, -1, depth)], axis=1
    ).astype(BF16)
    scatter = lambda x: lax.psum_scatter(x, "fsdp", scatter_dimension=0, tiled=False)
    pieces = [
        scatter(g_kernel.reshape(owners, shard, width)),
        scatter(bands_of(g_qkv, 3)),
        scatter(bands_of(g_out, 1)),
        scatter(bands_of(g_up, 4)),
        scatter(g_down.reshape(owners, shard, width)),
        scatter(g_small),
    ]
    pieces = [lax.psum(p, "rep").astype(F32) for p in pieces]
    s_kernel, s_qkv, s_out, s_up, s_down, s_small = pieces
    unstack = lambda p: p.reshape(-1, depth, width).transpose(1, 0, 2).reshape(depth, -1)
    return (
        output, grad_pixels, s_kernel, s_small[9 : 9 + cells], unstack(s_qkv), s_out, unstack(s_up), s_down,
        s_small[:7], s_small[9 + cells :].reshape(-1), s_small[7:9],
    )


def solution(mesh):
    tokens = P(("rep", "fsdp"), None)
    rows, columns = P("fsdp", None), P(None, "fsdp")
    in_specs = (
        tokens, tokens, P(), P(), P(), P(), P(), P(), tokens,
        rows, columns, rows, rows, rows, rows, columns, P("fsdp"), columns,
    )
    out_specs = (tokens, tokens, rows, columns, rows, rows, rows, rows, columns, P("fsdp"), columns)
    reps, owners = mesh.shape["rep"], mesh.shape["fsdp"]

    def here(*arrays):
        return local(reps, owners, *arrays)

    return jax.shard_map(here, mesh=mesh, in_specs=in_specs, out_specs=out_specs, check_vma=False)
```

time: 884 us -> 688 us (0.78); the launches traced: 870 us -> 687 us
  matrix products: 399 us -> 0 us
  Pallas kernels: 0 us -> 257 us
  waiting for transfers between devices: 199 us -> 337 us
  local copies, waits for them, and re-layouts: 116 us -> 21.7 us
  blocking collectives: 84.5 us -> 41.1 us
  other arithmetic: 54.6 us -> 15.9 us
    dot_general x107 -> x0, matrix products: 399 us -> none  [the longest x24 54 us: masked_scores(): jnp.einsum('qd,kd->qk', query, keys_block, preferred_element_type=jnp.flo...]
    pallas_call x0 -> x8, Pallas kernels: none -> 257 us  [the longest x1 55.2 us: mlp_call(): pl.pallas_call(mlp_kernel, grid=(4,), in_specs=[fixed, fixed, fixed, whol...]
    reduce_scatter x5 -> x6, waiting for transfers between devices: 101 us -> 225 us  [local(): lax.psum_scatter(x, 'fsdp', scatter_dimension=0, tiled=False)]
    unnamed x137 -> x43, local copies, waits for them, and re-layouts: 71.6 us -> 2.08 us
    all_gather x5 -> x1, waiting for transfers between devices: 0.06 us -> 66.5 us  [local(): groups = lax.all_gather(here, ('rep', 'fsdp'), axis=0, tiled=True)]
    unnamed x17 -> x8, waiting for transfers between devices: 41.3 us -> 1.78 us
    all_gather x4 -> x1, blocking collectives: 54 us -> 15.9 us  [local(): small_all = lax.all_gather(small_here, 'fsdp', axis=0, tiled=False)]
    reduce_sum x21 -> x1, other arithmetic: 28 us -> 0.13 us  [chunk_lists(): listed = jnp.sum(jnp.where(hit, ids[None, :, None], 0), axis=1)]
  transfers between devices with their start and end apart: 14 -> 8, of which waited for: 5 -> 7; matrix products, arithmetic and copies ran while one was open for 59% -> 3% of each run, Pallas kernels for 0% -> 11%
where the time goes in v1:
time: 688 us; the launch traced here: 687 us
  waiting for transfers between devices  337 us (49%)
  Pallas kernels  257 us (37%)
  blocking collectives  41.1 us (6%)
  local copies, waits for them, and re-layouts  21.7 us (3%)
  other arithmetic  15.9 us (2%)
  between operations  14.6 us (2%)
    reduce_scatter x6, waiting for transfers between devices, local(): lax.psum_scatter(x, 'fsdp', scatter_dimension=0, tiled=False)  225 us
    all_gather x1, waiting for transfers between devices, local(): groups = lax.all_gather(here, ('rep', 'fsdp'), axis=0, tiled=True)  66.5 us
    pallas_call x1, Pallas kernels, mlp_call(): pl.pallas_call(mlp_kernel, grid=(4,), in_specs=[fixed, fixed, fixed, whol...  55.2 us
    pallas_call x1, Pallas kernels, attend_back(): pl.pallas_call(attend_back_kernel, grid_spec=pltpu.PrefetchScalarGridSpec...  52.4 us
    psum x1, waiting for transfers between devices, local(): pieces = [lax.psum(p, 'rep').astype(F32) for p in pieces]  43.1 us
    pallas_call x1, Pallas kernels, unresize(): pl.pallas_call(unresize_kernel, grid_spec=pltpu.PrefetchScalarGridSpec(nu...  37.8 us
    pallas_call x1, Pallas kernels, attend(): pl.pallas_call(attend_kernel, grid_spec=pltpu.PrefetchScalarGridSpec(num_...  31.3 us
    pallas_call x1, Pallas kernels, resize(): pl.pallas_call(resize_kernel, grid_spec=pltpu.PrefetchScalarGridSpec(num_...  29.9 us
  transfers between devices with their start and end apart: 8, of which 7 were waited for; matrix products, arithmetic and copies ran while one was open for 3% of the time, Pallas kernels for 11%

profile of v1, /device:TPU:0, one launch (start us, length us, event | category | flops | bytes accessed | tf_op | source)
XLA Modules:
  0.0 687.1 jit_solution(4181435196584847865)
XLA Ops:
  7.2 1.1 copy.83
  8.4 1.6 reshape.268
  11.4 2.4 fusion.2
  14.0 15.9 %all-gather.1 = bf16[8,62,96]{2,1,0:T(8,128)(2,1)S(1)} all-gather(bf16[1,62,96]{2,1,0:T(8,128)(2,1)S(1)} %maximum_bitcast_fusion), channel_id=2, replica_groups=mesh['rep'=4,'fsdp'=8] {'fsdp'}, dimensions={0}, use_global_device_ids=true | all-gather | bytes 107136 | tf_op jit(solution)/shard_map/all_gather | solution.py:635
  33.9 1.0 copy.90.live_ref
  34.9 1.0 copy.82.cat_ref
  35.9 1.2 pad.22.rb_ref
  37.8 3.2 gather_fusion
  45.3 29.9 %resize.1.res_ref = bf16[1024,3072]{1,0:T(8,128)(2,1)} custom-call(s32[3,65]{1,0:T(4,128)} %pad_add_fusion.lists, bf16[1024,6912]{1,0:T(8,128)(2,1)} %px_ref.1, s32[1024,1]{1,0:T(8,128)} %copy.82.cat_ref, bf16[128,1024]{1,0:T(8,128)(2,1)} %pad.21.ra_ref, bf16[640,1024]{1,0:T(8,128)(2,1)} %pad.22.rb_ref, bf16[2304,1024]{1,0:T(8,128)(2,1)} %rc_ref.3), custom_call_target="tpu_custom_call" | custom-call | flops 7549747200 | bytes 20447232 | tf_op jit(solution)/shard_map/resize/pallas_call | solution.py:109
  75.2 66.5 %all-gather.4.cloned.1.call-done = bf16[12288,768]{1,0:T(8,128)(2,1)} async-done(((bf16[384,768]{1,0:T(8,128)(2,1)}), bf16[12288,768]{1,0:T(8,128)(2,1)}) %all-gather.4.cloned.1.call-update) | async-done | bytes 18874384 | tf_op jit(solution)/shard_map/all_gather | solution.py:634
  141.7 20.5 %embed.1 = (f32[1024,768]{1,0:T(8,128)}, bf16[1024,768]{1,0:T(8,128)(2,1)}, bf16[1024,2304]{1,0:T(8,128)(2,1)}) custom-call(bf16[1024,3072]{1,0:T(8,128)(2,1)} %resize.1.res_ref, bf16[4,4,768,768]{3,2,1,0:T(8,128)(2,1)} %bitcast.46, bf16[4,8,4,96,768]{4,3,2,1,0:T(8,128)(2,1)} %bitcast.47, bf16[1024,128]{1,0:T(8,128)(2,1)} %pad_select_fusion.pos_ref, ...), custom_call_target="tpu_custom_call" | custom-call | flops 8455716864 | bytes 23986176 | tf_op jit(solution)/shard_map/embed/pallas_call | solution.py:237
  162.3 31.3 %attend.1 = (bf16[1024,768]{1,0:T(8,128)(2,1)}, f32[1024,768]{1,0:T(8,128)}) custom-call(s32[1]{0:T(128)} %bitcast.15.dense_ref, bf16[1024,2304]{1,0:T(8,128)(2,1)} %get-tuple-element.29.q_ref.k_ref.v_ref, bf16[1024,2304]{1,0:T(8,128)(2,1)} %get-tuple-element.29.q_ref.k_ref.v_ref, bf16[1024,2304]{1,0:T(8,128)(2,1)} %get-tuple-element.29.q_ref.k_ref.v_ref, ...), custom_call_target="tpu_custom_call" | custom-call | flops 12884901888 | bytes 9437184 | tf_op jit(solution)/shard_map/attend/pallas_call | solution.py:307
  193.6 55.2 %mlp.1 = (bf16[1024,768]{1,0:T(8,128)(2,1)}, f32[1024,768]{1,0:T(8,128)}, bf16[1024,768]{1,0:T(8,128)(2,1)}, bf16[4,768,768]{2,1,0:T(8,128)(2,1)}, bf16[8,4,96,7...) custom-call(f32[1024,768]{1,0:T(8,128)} %get-tuple-element.28.embed_ref, ...), custom_call_target="tpu_custom_call" | custom-call | flops 32614907904 | bytes 36962304 | tf_op jit(solution)/shard_map/mlp/pallas_call | solution.py:480
  248.8 52.4 %attend_back.1.dproj_ref = bf16[3,1024,768]{2,1,0:T(8,128)(2,1)} custom-call(s32[1]{0:T(128)} %bitcast.15.dense_ref, bf16[1024,2304]{1,0:T(8,128)(2,1)} %get-tuple-element.29.q_ref.k_ref.v_ref, bf16[1024,2304]{1,0:T(8,128)(2,1)} %get-tuple-element.29.q_ref.k_ref.v_ref, bf16[1024,2304]{1,0:T(8,128)(2,1)} %get-tuple-element.29.q_ref.k_ref.v_ref, ...), custom_call_target="tpu_custom_call" | custom-call | flops 32212254720 | bytes 17301504 | tf_op jit(solution)/shard_map/attend_back/pallas_call | solution.py:387
  301.2 20.2 %embed_back.1 = (bf16[1024,768]{1,0:T(8,128)(2,1)}, bf16[8,3,96,768]{3,2,1,0:T(8,128)(2,1)}, f32[128,768]{1,0:T(8,128)}, f32[16,768]{1,0:T(8,128)}) custom-call(bf16[3,1024,768]{2,1,0:T(8,128)(2,1)} %attend_back.1.dproj_ref, bf16[1024,768]{1,0:T(8,128)(2,1)} %get-tuple-element.34.norm_ref, bf16[4,8,4,96,768]{4,3,2,1,0:T(8,128)(2,1)} %bitcast.51, ...), custom_call_target="tpu_custom_call" | custom-call | flops 7247757312 | bytes 21233664 | tf_op jit(solution)/shard_map/embed_back/pallas_call | solution.py:570
  322.8 9.2 %patch_grad.1 = bf16[4,768,768]{2,1,0:T(8,128)(2,1)} custom-call(bf16[1024,3072]{1,0:T(8,128)(2,1)} %resize.1.res_ref, bf16[1024,768]{1,0:T(8,128)(2,1)} %get-tuple-element.36.g_ref), custom_call_target="tpu_custom_call" | custom-call | flops 4831838208 | bytes 12582912 | tf_op jit(solution)/shard_map/patch_grad/pallas_call | solution.py:601
  332.9 0.9 slice.80
  334.9 28.8 %reduce-scatter.11.cloned.1.call-done = bf16[1,288,768]{2,1,0:T(8,128)(2,1)} async-done(((bf16[8,288,768]{2,1,0:T(8,128)(2,1)}), bf16[1,288,768]{2,1,0:T(8,128)(2,1)}) %reduce-scatter.11.cloned.1.call-update) | async-done | bytes 442384 | tf_op jit(solution)/shard_map/reduce_scatter | solution.py:687
  363.6 1.8 copy.96
  365.5 54.1 %reduce-scatter.15.cloned.1.call-done = bf16[1,384,768]{2,1,0:T(8,128)(2,1)} async-done(((bf16[8,384,768]{2,1,0:T(8,128)(2,1)}), bf16[1,384,768]{2,1,0:T(8,128)(2,1)}) %reduce-scatter.15.cloned.1.call-update) | async-done | bytes 589840 | tf_op jit(solution)/shard_map/reduce_scatter | solution.py:687
  419.6 1.5 copy.94
  422.0 31.6 %reduce-scatter.13.cloned.1.call-done = bf16[1,96,768]{2,1,0:T(8,128)(2,1)} async-done(((bf16[8,96,768]{2,1,0:T(8,128)(2,1)}), bf16[1,96,768]{2,1,0:T(8,128)(2,1)}) %reduce-scatter.13.cloned.1.call-update) | async-done | bytes 147472 | tf_op jit(solution)/shard_map/reduce_scatter | solution.py:687
  453.6 55.4 %reduce-scatter.7.cloned.1.call-done = bf16[1,384,768]{2,1,0:T(8,128)(2,1)} async-done(((bf16[8,384,768]{2,1,0:T(8,128)(2,1)}), bf16[1,384,768]{2,1,0:T(8,128)(2,1)}) %reduce-scatter.7.cloned.1.call-update) | async-done | bytes 589840 | tf_op jit(solution)/shard_map/reduce_scatter | solution.py:687
  508.9 55.6 %reduce-scatter.17.cloned.1.call-done = bf16[1,384,768]{2,1,0:T(8,128)(2,1)} async-done(((bf16[8,384,768]{2,1,0:T(8,128)(2,1)}), bf16[1,384,768]{2,1,0:T(8,128)(2,1)}) %reduce-scatter.17.cloned.1.call-update) | async-done | bytes 589840 | tf_op jit(solution)/shard_map/reduce_scatter | solution.py:687
  564.6 37.8 %unresize.1 = bf16[1024,6912]{1,0:T(8,128)(2,1)} custom-call(s32[3,65]{1,0:T(4,128)} %pad_add_fusion.lists, bf16[1024,768]{1,0:T(8,128)(2,1)} %get-tuple-element.36.g_ref, bf16[4,3,1024,768]{3,2,1,0:T(8,128)(2,1)} %bitcast.52, s32[1024,1]{1,0:T(8,128)} %copy.82.cat_ref, bf16[128,1024]{1,0:T(8,128)(2,1)} %pad.21.ra_ref, bf16[640,1024]{1,0:T(8,128)(2,1)} %pad.22.rb_ref, ...), custom_call_target="tpu_custom_call" | custom-call | flops 12582912000 | bytes 20447232 | tf_op jit(solution)/shard_map/unresize/pallas_call | solution.py:146
  602.4 25.2 %psum.43 = bf16[62,96]{1,0:T(8,128)(2,1)S(1)} all-reduce(bf16[62,96]{1,0:T(8,128)(2,1)} %bitcast.75), channel_id=1, replica_groups=mesh['rep'=4,'fsdp'=8] {'rep'}, use_global_device_ids=true, to_apply=%region_12.13 | all-reduce | flops 5952 | bytes 23808 | tf_op jit(solution)/shard_map/psum | solution.py:696
  630.1 43.1 %all-reduce.8.cloned.1.call-done = (bf16[384,768]{1,0:T(8,128)(2,1)}, bf16[96,2304]{1,0:T(8,128)(2,1)}, bf16[96,768]{1,0:T(8,128)(2,1)}, bf16[96,3072]{1,0:T(8,128)(2,1)}, bf16[384,768]{1,0:T(8,128)(2,1)}) async-done(((bf16[384,768]{1,0:T(8,128)(2,1)}, bf16[96,2304]{1,0:T(8,128)(2,1)}, bf16[96,768]{1,0:T(8,128)(2,1)}, bf16[96,3072]{1,0:T(8,128)(2,1)}, bf16[384,768]{1,0:T(8,128)(2,1)}), ...) | async-done | bytes 2359312 | tf_op jit(solution)/shard_map/psum | solution.py:696
  673.2 1.7 convert_element_type.69
  674.9 2.2 convert_element_type.67
  677.1 1.0 reshape.279
  678.1 1.1 reshape.283
  679.2 1.1 convert_element_type.70
  (118 shorter events, 16.8 us)
Async XLA Ops:
  7.2 134.6 %all-gather.4.cloned.1.call-start = ((), (), s32[]{:S(2)}) async-start(), calls=%async_computation.6 | async-start | bytes 19464192 | tf_op jit(solution)/shard_map/all_gather | solution.py:634
  9.9 1.1 copy-start.3
  10.0 1.2 copy-start.4
  10.0 1.4 copy-start.5
  11.4 2.5 copy-start.16
  11.4 2.6 copy-start.12
  11.4 2.6 copy-start.15
  11.4 2.6 copy-start.17
  11.4 18.6 %copy-start.18 = (s32[1,40]{1,0:T(1,128)S(1)}, s32[1,40]{1,0:T(1,128)}, u32[]{:S(2)}) copy-start(s32[1,40]{1,0:T(1,128)} %param.21) | copy-start | bytes 484
  11.4 18.6 %copy-start.19 = (s32[4]{0:T(128)S(1)}, s32[4]{0:T(128)}, u32[]{:S(2)}) copy-start(s32[4]{0:T(128)} %constant.70.clone) | copy-start | bytes 52
  11.4 19.1 %copy-start.11 = (bf16[100,49]{0,1:T(8,128)(2,1)S(1)}, bf16[100,49]{0,1:T(8,128)(2,1)}, u32[]{:S(2)}) copy-start(bf16[100,49]{0,1:T(8,128)(2,1)} %param.26) | copy-start | bytes 29404
  13.8 18.4 %copy-start.8 = (bf16[900,49]{0,1:T(8,128)(2,1)S(1)}, bf16[900,49]{0,1:T(8,128)(2,1)}, u32[]{:S(2)}) copy-start(bf16[900,49]{0,1:T(8,128)(2,1)} %param.25) | copy-start | bytes 264604
  13.8 19.3 %copy-start.7 = (bf16[64,1024]{1,0:T(8,128)(2,1)S(1)}, bf16[64,1024]{1,0:T(8,128)(2,1)}, u32[]{:S(2)}) copy-start(bf16[64,1024]{1,0:T(8,128)(2,1)} %param.22) | copy-start | bytes 393220
  13.8 349.8 %reduce-scatter.11.cloned.1.call-start = ((), (), s32[]{:S(2)}) async-start(), calls=%async_computation.9 | async-start | bytes 3981312 | tf_op jit(solution)/shard_map/reduce_scatter | solution.py:687
  29.9 6.0 copy-start
  34.9 2.2 copy-start.14
  321.4 98.1 %reduce-scatter.15.cloned.1.call-start = ((), (), s32[]{:S(2)}) async-start(), calls=%async_computation.11 | async-start | bytes 5308416 | tf_op jit(solution)/shard_map/reduce_scatter | solution.py:687
  322.2 131.4 %reduce-scatter.13.cloned.1.call-start = ((), (), s32[]{:S(2)}) async-start(), calls=%async_computation.10 | async-start | bytes 1327104 | tf_op jit(solution)/shard_map/reduce_scatter | solution.py:687
  322.7 186.2 %reduce-scatter.7.cloned.1.call-start = ((), (), s32[]{:S(2)}) async-start(), calls=%async_computation.7 | async-start | bytes 5308416 | tf_op jit(solution)/shard_map/reduce_scatter | solution.py:687
  332.0 232.5 %reduce-scatter.17.cloned.1.call-start = ((), (), s32[]{:S(2)}) async-start(), calls=%async_computation.12 | async-start | bytes 5308416 | tf_op jit(solution)/shard_map/reduce_scatter | solution.py:687
  332.1 0.7 copy-start.13
  332.1 1.8 copy-start.9
  332.1 1.8 copy-start.10
  332.6 269.8 %reduce-scatter.9.cloned.1.call-start = ((), (), s32[]{:S(2)}) async-start(), calls=%async_computation.8 | async-start | bytes 147456 | tf_op jit(solution)/shard_map/reduce_scatter | solution.py:687
  334.8 338.4 %all-reduce.8.cloned.1.call-start = ((), (), s32[]{:S(2)}) async-start(), calls=%async_computation.13 | async-start | bytes 4718592 | tf_op jit(solution)/shard_map/psum | solution.py:696
  673.2 3.9 copy-start.6
  674.9 3.2 copy-start.2
  677.1 2.1 copy-start.1
Sparse Core Ops, SparseCore 0:
  13.9 127.7 all-gather.3
  321.6 42.0 reduce-scatter.10
  366.1 53.4 reduce-scatter.14
  422.4 31.1 reduce-scatter.12
  455.9 53.0 reduce-scatter.6
  511.2 53.3 reduce-scatter.16
  566.9 28.7 reduce-scatter.8
  599.8 73.3 all-reduce.7

commit v2 on v1

--- a/solution.py
+++ b/solution.py
@@ -122,15 +122,10 @@
     )(lists, pixels, category, ra, rb, rc)
 
 
-def unresize_kernel(lists, g_ref, w_ref, cat_ref, ra_ref, rb_ref, rc_ref, out_ref, grow, lhs):
-    tokens = g_ref.shape[0]
+def unresize_kernel(lists, g_ref, w_ref, cat_ref, ra_ref, rb_ref, rc_ref, *rest):
+    out_ref, grow, lhs = rest[-3:]
     out_ref[...] = jnp.zeros_like(out_ref)
-
-    @pl.loop(0, tokens // TILE)
-    def _(t):
-        rows = pl.ds(pl.multiple_of(t * TILE, TILE), TILE)
-        grow[rows, :] = nt(g_ref[rows, :], w_ref[0, 0]).astype(BF16)
-
+    grow[...] = nt(g_ref[...], w_ref[0, 0]).astype(BF16)
     for class_id, matrix in enumerate((ra_ref, rb_ref, rc_ref)):
         resize_rows(
             lists, cat_ref, grow, out_ref, lhs, class_id, grow.shape[1],
@@ -138,28 +133,32 @@
         )
 
 
-def unresize(lists, g_emb, groups, category, ra, rb, rc, area):
+def unresize(lists, g_emb, groups, category, ra, rb, rc, area, channel, part, parts, before):
     tokens, width = g_emb.shape
     base = rc.shape[1]
+    rows = tokens // parts
     whole = lambda a: pl.BlockSpec(a.shape, lambda c, s: (0, 0))
+    some = lambda a: pl.BlockSpec((rows, a.shape[1]), lambda c, s: (part, 0))
     kernels = groups.reshape(4, 3, base, width)
+    more = [] if before is None else [before]
     return pl.pallas_call(
         unresize_kernel,
         grid_spec=pltpu.PrefetchScalarGridSpec(
             num_scalar_prefetch=1,
-            grid=(3,),
+            grid=(1,),
             in_specs=[
-                whole(g_emb), pl.BlockSpec((1, 1, base, width), lambda c, s: (0, c, 0, 0)),
-                whole(category), whole(ra), whole(rb), whole(rc),
-            ],
-            out_specs=pl.BlockSpec((tokens, area), lambda c, s: (0, c)),
-            scratch_shapes=[pltpu.VMEM((tokens, base), BF16), pltpu.VMEM((TILE, base), BF16)],
+                some(g_emb), pl.BlockSpec((1, 1, base, width), lambda c, s: (0, channel, 0, 0)),
+                some(category), whole(ra), whole(rb), whole(rc),
+            ] + [pl.BlockSpec(memory_space=pl.ANY)] * len(more),
+            out_specs=pl.BlockSpec((rows, area), lambda c, s: (part, channel)),
+            scratch_shapes=[pltpu.VMEM((rows, base), BF16), pltpu.VMEM((TILE, base), BF16)],
         ),
         out_shape=jax.ShapeDtypeStruct((tokens, 3 * area), BF16),
+        input_output_aliases={7: 0} if more else {},
         compiler_params=params(),
-        cost_estimate=cost(tokens * 3 * base * 2000 * 2, tokens * area * 6 + tokens * base * 6),
+        cost_estimate=cost(1e6, 1e5),
         name="unresize",
-    )(lists, g_emb, kernels, category, ra, rb, rc)
+    )(lists, g_emb, kernels, category, ra, rb, rc, *more)
 
 
 def norm_parts(values):
@@ -183,9 +182,7 @@
 
 
 def row_tiles(tokens, body):
-    @pl.loop(0, tokens // TILE)
-    def _(t):
-        body(pl.ds(pl.multiple_of(t * TILE, TILE), TILE))
+    body(pl.ds(0, tokens))
 
 
 def embed_kernel(res_ref, kern_ref, qkv_ref, pos_ref, table_ref, small_ref, embed_ref, norm_ref, proj_ref):
@@ -379,16 +376,16 @@
     out_ref[2] = dvals[...].astype(BF16)
 
 
-def attend_back(dense, projected, g_mixed, mixed, lse, onehot, keymask):
+def attend_back(dense, projected, g_mixed, mixed, lse, onehot, keymask, start, number):
     tokens = projected.shape[0]
     pairs = projected.shape[1] // 3 // 128
-    part = lambda at: pl.BlockSpec((tokens, 128), lambda j, d: (0, at + j))
+    part = lambda at: pl.BlockSpec((tokens, 128), lambda j, d: (0, at + start + j))
     whole = pl.BlockSpec((tokens, 128), lambda j, d: (0, 0))
     return pl.pallas_call(
         attend_back_kernel,
         grid_spec=pltpu.PrefetchScalarGridSpec(
             num_scalar_prefetch=1,
-            grid=(pairs,),
+            grid=(number,),
             in_specs=[part(0), part(pairs), part(2 * pairs), part(0), part(0), part(0), whole, whole],
             out_specs=pl.BlockSpec((3, tokens, 128), lambda j, d: (0, 0, j)),
             scratch_shapes=[
@@ -396,9 +393,9 @@
                 pltpu.VMEM((tokens, 128), F32), pltpu.VMEM((tokens, 128), F32),
             ],
         ),
-        out_shape=jax.ShapeDtypeStruct((3, tokens, pairs * 128), BF16),
+        out_shape=jax.ShapeDtypeStruct((3, tokens, number * 128), BF16),
         compiler_params=params(),
-        cost_estimate=cost(5 * 2 * 12 * tokens * tokens * 256, tokens * 768 * 22, 12 * tokens * tokens),
+        cost_estimate=cost(5 * 2 * 2 * number * tokens * tokens * 256, tokens * 128 * number * 22, 2 * number * tokens * tokens),
         name="attend_back",
     )(dense, projected, projected, projected, g_mixed, mixed, lse, onehot, keymask)
 
@@ -420,7 +417,7 @@
             xhat, _ = norm_parts(value)
             norm2[rows, :] = (xhat * small_ref[8:9, :] + small_ref[5:6, :]).astype(BF16)
             gbranch[rows, :] = (cot_ref[rows, :].astype(F32) * live_ref[rows, :]).astype(BF16)
-            gnorm[rows, :] = jnp.zeros((TILE, gnorm.shape[1]), F32)
+            gnorm[rows, :] = jnp.zeros_like(value)
 
         row_tiles(tokens, body)
 
@@ -514,44 +511,93 @@
     )(embed, mixed, cotangent, live, small, shift, colwise, colwise, rowwise)
 
 
+def store_split(core, value, mine_ref, other_ref):
+    shape = mine_ref.shape
+    pairs = value.reshape(-1, 2, shape[-2], shape[-1])
+    first, second = pairs[:, 0].reshape(shape), pairs[:, 1].reshape(shape)
+
+    @pl.when(core == 0)
+    def _():
+        mine_ref[...] = first
+        other_ref[...] = second
+
+    @pl.when(core != 0)
+    def _():
+        mine_ref[...] = second
+        other_ref[...] = first
+
+
+def qkv_grad_kernel(core_ref, norm_ref, dproj_ref, gwo_ref, mine_ref, other_ref):
+    step = pl.program_id(0)
+
+    @pl.when(step < 3)
+    def _():
+        value = tn(norm_ref[...], dproj_ref[0]).astype(BF16)
+        store_split(core_ref[0], value, mine_ref, other_ref)
+
+    @pl.when(step == 3)
+    def _():
+        store_split(core_ref[0], square(gwo_ref), mine_ref, other_ref)
+
+
+def qkv_grad(core, normed1, dproj, g_out):
+    tokens, width = normed1.shape
+    bands, deep = g_out.shape[0], g_out.shape[1]
+    half = (bands // 2, deep) if bands > 1 else (1, width // 2)
+    pair = pl.BlockSpec((half[0], 1, half[1], width), lambda s, c: (0, s, 0, 0))
+    shape = jax.ShapeDtypeStruct((half[0], 4, half[1], width), BF16)
+    return pl.pallas_call(
+        qkv_grad_kernel,
+        grid_spec=pltpu.PrefetchScalarGridSpec(
+            num_scalar_prefetch=1,
+            grid=(4,),
+            in_specs=[
+                pl.BlockSpec((tokens, width), lambda s, c: (0, 0)),
+                pl.BlockSpec((1, tokens, width), lambda s, c: (jnp.minimum(s, 2), 0, 0)),
+                pl.BlockSpec(g_out.shape, lambda s, c: (0, 0, 0)),
+            ],
+            out_specs=[pair, pair],
+        ),
+        out_shape=[shape, shape],
+        compiler_params=params(),
+        cost_estimate=cost(1e6, 1e5),
+        name="qkv_grad",
+    )(core, normed1, dproj, g_out)
+
+
 def embed_back_kernel(
-    dproj_ref, norm_ref, qkv_ref, embed_ref, ghid_ref, pos_ref, small_ref,
-    gemb_ref, gqkv_ref, gpos_ref, sums_ref, gnorm,
+    dproj_ref, qkv_ref, embed_ref, ghid_ref, pos_ref, small_ref, gemb_ref, gpos_ref, sums_ref, gnorm
 ):
     step = pl.program_id(0)
     tokens = embed_ref.shape[0]
     weight = square(qkv_ref)
 
+    column = jnp.sum(dproj_ref[0].astype(F32), axis=0, keepdims=True)
+
     @pl.when(step == 0)
     def _():
         sums_ref[...] = jnp.zeros_like(sums_ref)
+        sums_ref[2:3, :] = column
 
         def body(rows):
             gnorm[rows, :] = nt(dproj_ref[0, rows, :], weight)
 
         row_tiles(tokens, body)
 
-    @pl.when(step > 0)
+    @pl.when(step == 1)
     def _():
         def body(rows):
             gnorm[rows, :] += nt(dproj_ref[0, rows, :], weight)
 
         row_tiles(tokens, body)
 
-    gqkv_ref[...] = tn(norm_ref[...], dproj_ref[0]).astype(BF16).reshape(gqkv_ref.shape)
-    column = jnp.sum(dproj_ref[0].astype(F32), axis=0, keepdims=True)
-
-    @pl.when(step == 0)
-    def _():
-        sums_ref[2:3, :] = column
-
     @pl.when(step == 2)
     def _():
         sums_ref[3:4, :] = column
 
         def body(rows):
+            grad = gnorm[rows, :] + nt(dproj_ref[0, rows, :], weight)
             xhat, rstd = norm_parts(embed_ref[rows, :])
-            grad = gnorm[rows, :]
             gemb = (ghid_ref[rows, :] + norm_back(xhat, rstd, grad, small_ref[7:8, :])).astype(BF16)
             gemb_ref[rows, :] = gemb
             sums_ref[0:1, :] += jnp.sum(gemb.astype(F32), axis=0, keepdims=True)
@@ -562,7 +608,7 @@
         gpos_ref[...] = tn(pos_ref[...], gemb_ref[...])
 
 
-def embed_back(dproj, normed1, colwise, embed, g_hidden, pos_rows, small):
+def embed_back(dproj, colwise, embed, g_hidden, pos_rows, small):
     tokens, width = embed.shape
     bands, deep = colwise.shape[1], colwise.shape[3]
     fixed = pl.BlockSpec((tokens, width), lambda s: (0, 0))
@@ -571,43 +617,128 @@
         embed_back_kernel,
         grid=(3,),
         in_specs=[
-            pl.BlockSpec((1, tokens, width), lambda s: (s, 0, 0)), fixed,
+            pl.BlockSpec((1, tokens, width), lambda s: (s, 0, 0)),
             pl.BlockSpec((1, bands, 1, deep, width), lambda s: (1, 0, s, 0, 0)),
             fixed, fixed, whole(pos_rows), whole(small),
         ],
         out_specs=[
-            fixed, pl.BlockSpec((bands, 1, deep, width), lambda s: (0, s, 0, 0)),
-            pl.BlockSpec((128, width), lambda s: (0, 0)), pl.BlockSpec((16, width), lambda s: (0, 0)),
+            fixed, pl.BlockSpec((128, width), lambda s: (0, 0)), pl.BlockSpec((16, width), lambda s: (0, 0)),
         ],
         out_shape=[
             jax.ShapeDtypeStruct((tokens, width), BF16),
-            jax.ShapeDtypeStruct((bands, 3, deep, width), BF16),
             jax.ShapeDtypeStruct((128, width), F32),
             jax.ShapeDtypeStruct((16, width), F32),
         ],
         scratch_shapes=[pltpu.VMEM((tokens, width), F32)],
         compiler_params=params(),
-        cost_estimate=cost(6 * 2 * tokens * width * width, tokens * width * 18 + 6 * width * width * 2),
+        cost_estimate=cost(1e6, 1e5),
         name="embed_back",
-    )(dproj, normed1, colwise, embed, g_hidden, pos_rows, small)
-
-
-def patch_grad_kernel(res_ref, g_ref, out_ref):
-    out_ref[0] = tn(res_ref[...], g_ref[...]).astype(BF16)
-
-
-def patch_grad(resized, g_emb):
+    )(dproj, colwise, embed, g_hidden, pos_rows, small)
+
+
+def patch_grad_kernel(core_ref, res_ref, g_ref, small_ref, mine_ref, other_ref):
+    shard = mine_ref.shape[1] - small_ref.shape[1]
+    value = tn(res_ref[...], g_ref[...]).astype(BF16).reshape(-1, 2, shard, mine_ref.shape[2])
+    tail = small_ref[...].reshape(-1, 2, small_ref.shape[1], small_ref.shape[2])
+
+    def store(ref, which):
+        ref[:, 0:shard, :] = value[:, which]
+        ref[:, shard:, :] = tail[:, which]
+
+    @pl.when(core_ref[0] == 0)
+    def _():
+        store(mine_ref, 0)
+        store(other_ref, 1)
+
+    @pl.when(core_ref[0] != 0)
+    def _():
+        store(mine_ref, 1)
+        store(other_ref, 0)
+
+
+def patch_grad(core, resized, g_emb, g_small):
     tokens, width = g_emb.shape
+    owners, packed = g_small.shape[0], g_small.shape[1]
+    shard = 4 * width // owners
+    pair = pl.BlockSpec((owners // 8, shard + packed, width), lambda s, c: (s, 0, 0))
+    shape = jax.ShapeDtypeStruct((owners // 2, shard + packed, width), BF16)
     return pl.pallas_call(
         patch_grad_kernel,
-        grid=(4,),
-        in_specs=[pl.BlockSpec((tokens, width), lambda s: (0, s)), pl.BlockSpec((tokens, width), lambda s: (0, 0))],
-        out_specs=pl.BlockSpec((1, width, width), lambda s: (s, 0, 0)),
-        out_shape=jax.ShapeDtypeStruct((4, width, width), BF16),
+        grid_spec=pltpu.PrefetchScalarGridSpec(
+            num_scalar_prefetch=1,
+            grid=(4,),
+            in_specs=[
+                pl.BlockSpec((tokens, width), lambda s, c: (0, s)),
+                pl.BlockSpec((tokens, width), lambda s, c: (0, 0)),
+                pl.BlockSpec((owners // 4, packed, width), lambda s, c: (s, 0, 0)),
+            ],
+            out_specs=[pair, pair],
+        ),
+        out_shape=[shape, shape],
         compiler_params=params(),
-        cost_estimate=cost(4 * 2 * tokens * width * width, tokens * width * 10 + 4 * width * width * 2),
+        cost_estimate=cost(1e6, 1e5),
         name="patch_grad",
-    )(resized, g_emb)
+    )(core, resized, g_emb, g_small)
+
+
+def bit_of(axis, bit):
+    return (lax.axis_index(axis) >> bit) & 1
+
+
+class Sum:
+    def __init__(self, mine, other, reps, owners, steps):
+        self.sizes = dict(rep=reps, fsdp=owners)
+        self.lead = [("fsdp", b) for b in range(1, owners.bit_length() - 1)][::-1]
+        self.steps = [("fsdp", 0)] + steps
+        self.back = [s for s in steps if s[0] == "rep"][::-1]
+        shape = (2,) * len(self.lead) + mine.shape[1:]
+        self.launch(mine.reshape(shape), other.reshape(shape))
+
+    def launch(self, kept, sent):
+        axis, bit = (self.steps or self.back)[0]
+        pairs = [(i, i ^ (1 << bit)) for i in range(self.sizes[axis])]
+        kept, sent = lax.optimization_barrier((kept, sent))
+        self.kept, self.flying = kept, lax.ppermute(sent, axis, pairs)
+
+    def land(self):
+        if not self.steps and not self.back:
+            return
+        if self.steps:
+            self.steps.pop(0)
+            value = (self.kept.astype(F32) + self.flying.astype(F32)).astype(BF16)
+        else:
+            axis, bit = self.back.pop(0)
+            low = bit_of(axis, bit) == 0
+            a, b = self.kept, self.flying
+            value = jnp.concatenate([jnp.where(low, a, b), jnp.where(low, b, a)])
+        if self.steps:
+            axis, bit = self.steps[0]
+            if axis == "fsdp":
+                at = self.lead.index((axis, bit))
+                self.lead.remove((axis, bit))
+            else:
+                at = len(self.lead)
+                value = value.reshape(value.shape[:at] + (2, value.shape[at] // 2) + value.shape[at + 1 :])
+            mine = bit_of(axis, bit)
+            pick = lambda i: lax.dynamic_index_in_dim(value, i, at, keepdims=False)
+            self.launch(pick(mine), pick(1 - mine))
+        elif self.back:
+            self.launch(value, value)
+        else:
+            self.kept = value
+
+    def total(self):
+        while self.steps or self.back:
+            self.land()
+        return self.kept
+
+
+def beside(sums, work, value):
+    value = lax.optimization_barrier((value, *[one.kept for one in sums]))[0]
+    value, *kept = lax.optimization_barrier((work(value), *[one.kept for one in sums]))
+    for one, k in zip(sums, kept):
+        one.kept = k
+    return value
 
 
 def local(reps, owners, *arrays):
@@ -670,34 +801,71 @@
     output, g_hidden, g_mixed, g_down, g_up, g_out, sums_mlp, g_shift = mlp_call(
         embed, mixed, cotangent, live, small, shift, rowwise, colwise
     )
-    dproj = attend_back(dense, projected, g_mixed, mixed, lse, onehot, keymask)
-    g_emb, g_qkv, g_pos, sums_embed = embed_back(dproj, normed1, colwise, embed, g_hidden, pos_rows, small)
-    g_kernel = patch_grad(resized, g_emb)
-    grad_pixels = unresize(lists, g_emb, groups, cats, ra, rb, resize_c, pixels.shape[1] // 3)
-
     def bands_of(blocks, number):
         if blocks.shape[0] != owners:
             blocks = blocks.reshape(number, owners, depth, width).transpose(1, 0, 2, 3)
         return blocks.reshape(owners, number * depth, width)
 
+    scatter = lambda x: lax.psum_scatter(x, "fsdp", scatter_dimension=0, tiled=False)
+    s_down = scatter(g_down.reshape(owners, shard, width))
+    s_up = scatter(bands_of(g_up, 4))
+    pairs = width // 128
+    dproj = attend_back(dense, projected, g_mixed, mixed, lse, onehot, keymask, 0, pairs)
+    dproj = lax.optimization_barrier((dproj, s_down))[0]
+    core = bit_of("fsdp", 0).reshape(1)
+    own, rep = owners.bit_length() - 1, reps.bit_length() - 1
+    others = [("fsdp", b) for b in range(1, own)]
+    over_reps = [("rep", b) for b in range(rep)]
+    g_emb, g_pos, sums_embed = embed_back(dproj, colwise, embed, g_hidden, pos_rows, small)
     g_small = jnp.concatenate([(sums_mlp + sums_embed)[:9], g_pos[:cells]]).reshape(9 + cells, owners, depth)
     g_small = jnp.concatenate(
         [g_small.transpose(1, 0, 2), g_shift.reshape(owners, -1, depth)], axis=1
     ).astype(BF16)
-    scatter = lambda x: lax.psum_scatter(x, "fsdp", scatter_dimension=0, tiled=False)
-    pieces = [
-        scatter(g_kernel.reshape(owners, shard, width)),
-        scatter(bands_of(g_qkv, 3)),
-        scatter(bands_of(g_out, 1)),
-        scatter(bands_of(g_up, 4)),
-        scatter(g_down.reshape(owners, shard, width)),
-        scatter(g_small),
-    ]
-    pieces = [lax.psum(p, "rep").astype(F32) for p in pieces]
-    s_kernel, s_qkv, s_out, s_up, s_down, s_small = pieces
+    packed = -(-g_small.shape[1] * depth // (32 * width)) * 32
+    g_small = jnp.pad(
+        g_small.reshape(owners, -1), ((0, 0), (0, packed * width - g_small.shape[1] * depth))
+    ).reshape(owners, packed, width)
+    mine, other = patch_grad(core, resized, g_emb, g_small)
+    kern = Sum(mine, other, reps, owners, over_reps[::-1] + others)
+    mine, other = beside([kern], lambda d: qkv_grad(core, normed1, d, g_out), dproj)
+    kern.land()
+    if g_out.shape[0] == 1:
+        both = jnp.concatenate([jnp.where(core == 0, mine, other), jnp.where(core == 0, other, mine)], axis=2)
+        both = both.reshape(4, owners // 2, 2, depth, width).transpose(2, 1, 0, 3, 4)
+        mine, other = jnp.where(core == 0, both[0], both[1]), jnp.where(core == 0, both[1], both[0])
+    halves = (owners // 2, shard, width)
+    qkvo = Sum(mine.reshape(halves), other.reshape(halves), reps, owners, over_reps[:1] + others + over_reps[1:])
+
+    kern.kept, qkvo.kept = lax.optimization_barrier((kern.kept, qkvo.kept))
+    qkvo.land()
+    grad_pixels = None
+    for channel in range(3):
+
+        def work(pair):
+            return unresize(
+                lists, pair[0], groups, cats, ra, rb, resize_c, pixels.shape[1] // 3, channel, 0, 1, pair[1]
+            )
+
+        if channel == 2:
+            g_emb = lax.optimization_barrier((g_emb, s_up))[0]
+        grad_pixels = beside([qkvo, kern], work, (g_emb, grad_pixels))
+        kern.land()
+        qkvo.land()
+    s_up, s_down = (lax.psum(p, "rep") for p in (s_up, s_down))
+    while len(kern.back) > 1 or kern.steps:
+        kern.land()
+        qkvo.land()
+    kern.kept, s_up, s_down = lax.optimization_barrier((kern.kept, s_up, s_down))
+    s_up, s_down, grad_pixels, s_rest, s_kernel = lax.optimization_barrier(
+        (s_up, s_down, grad_pixels, qkvo.total(), kern.total())
+    )
+    s_up, s_down, s_rest, s_kernel = (x.astype(F32) for x in (s_up, s_down, s_rest, s_kernel))
+    s_small = s_kernel[shard:].reshape(-1)[: (9 + cells) * depth + shard].reshape(-1, depth)
+    s_kernel = s_kernel[:shard]
     unstack = lambda p: p.reshape(-1, depth, width).transpose(1, 0, 2).reshape(depth, -1)
     return (
-        output, grad_pixels, s_kernel, s_small[9 : 9 + cells], unstack(s_qkv), s_out, unstack(s_up), s_down,
+        output, grad_pixels, s_kernel, s_small[9 : 9 + cells], unstack(s_rest[: 3 * depth]),
+        s_rest[3 * depth : 4 * depth], unstack(s_up), s_down,
         s_small[:7], s_small[9 + cells :].reshape(-1), s_small[7:9],
     )
 

time: 688 us -> 463 us (0.67)
  waiting for transfers between devices: 337 us -> 109 us
  blocking collectives: 41.1 us -> 16 us
  starting transfers between devices: 0.32 us -> 17.4 us
    reduce_scatter x6 -> x2, waiting for transfers between devices: 225 us -> 0.12 us  [local(): lax.psum_scatter(x, 'fsdp', scatter_dimension=0, tiled=False)]
    psum x1, waiting for transfers between devices: 43.1 us -> 0.02 us  [local(): s_up, s_down = (lax.psum(p, 'rep') for p in (s_up, s_down))]
    ppermute x0 -> x14, waiting for transfers between devices: none -> 40 us  [launch(): self.kept, self.flying = (kept, lax.ppermute(sent, axis, pairs))]
    psum x1 -> x0, blocking collectives: 25.2 us -> none  [local(): pieces = [lax.psum(p, 'rep').astype(F32) for p in pieces]]
    ppermute x0 -> x14, starting transfers between devices: none -> 17.2 us  [launch(): self.kept, self.flying = (kept, lax.ppermute(sent, axis, pairs))]
    pallas_call x1 -> x2, Pallas kernels: 9.21 us -> 19.3 us  [the longest x1 10.3 us: patch_grad(): pl.pallas_call(patch_grad_kernel, grid_spec=pltpu.PrefetchScalarGridSpec(...]
    pallas_call x1 -> x3, Pallas kernels: 37.8 us -> 47 us  [unresize(): pl.pallas_call(unresize_kernel, grid_spec=pltpu.PrefetchScalarGridSpec(nu...]
    pallas_call x1, Pallas kernels: 20.2 us -> 12.7 us  [embed_back(): pl.pallas_call(embed_back_kernel, grid=(3,), in_specs=[pl.BlockSpec((1, t...]
  transfers between devices with their start and end apart: 8 -> 18, of which waited for: 7 -> 10; matrix products, arithmetic and copies ran while one was open for 3% -> 7% of each run, Pallas kernels for 11% -> 35%
where the time goes in v2:
time: 463 us; the launch traced here: 460 us
  Pallas kernels  255 us (55%)
  waiting for transfers between devices  109 us (24%)
  local copies, waits for them, and re-layouts  27.8 us (6%)
  other arithmetic  19.6 us (4%)
  starting transfers between devices  17.4 us (4%)
  blocking collectives  16 us (3%)
  between operations  14.7 us (3%)
    all_gather x1, waiting for transfers between devices, local(): groups = lax.all_gather(here, ('rep', 'fsdp'), axis=0, tiled=True)  68.6 us
    pallas_call x1, Pallas kernels, attend_back(): pl.pallas_call(attend_back_kernel, grid_spec=pltpu.PrefetchScalarGridSpec...  52.4 us
    pallas_call x1, Pallas kernels, mlp_call(): pl.pallas_call(mlp_kernel, grid=(4,), in_specs=[fixed, fixed, fixed, whol...  48.2 us
    pallas_call x3, Pallas kernels, unresize(): pl.pallas_call(unresize_kernel, grid_spec=pltpu.PrefetchScalarGridSpec(nu...  47 us
    ppermute x14, waiting for transfers between devices, launch(): self.kept, self.flying = (kept, lax.ppermute(sent, axis, pairs))  40 us
    pallas_call x1, Pallas kernels, attend(): pl.pallas_call(attend_kernel, grid_spec=pltpu.PrefetchScalarGridSpec(num_...  31.3 us
    pallas_call x1, Pallas kernels, resize(): pl.pallas_call(resize_kernel, grid_spec=pltpu.PrefetchScalarGridSpec(num_...  27.4 us
    ppermute x14, starting transfers between devices, launch(): self.kept, self.flying = (kept, lax.ppermute(sent, axis, pairs))  17.2 us
  transfers between devices with their start and end apart: 18, of which 10 were waited for; matrix products, arithmetic and copies ran while one was open for 7% of the time, Pallas kernels for 35%

profile of v2, /device:TPU:0, one launch (start us, length us, event | category | flops | bytes accessed | tf_op | source)
XLA Modules:
  0.0 459.7 jit_solution(14924261312595402648)
XLA Ops:
  7.2 1.6 reshape.301
  11.3 2.4 fusion.2
  13.9 16.0 %all-gather.1 = bf16[8,62,96]{2,1,0:T(8,128)(2,1)S(1)} all-gather(bf16[1,62,96]{2,1,0:T(8,128)(2,1)S(1)} %maximum_bitcast_fusion), channel_id=2, replica_groups=mesh['rep'=4,'fsdp'=8] {'fsdp'}, dimensions={0}, use_global_device_ids=true | all-gather | bytes 107136 | tf_op jit(solution)/shard_map/all_gather | solution.py:766
  37.8 3.2 gather_fusion
  45.3 27.4 %resize.1.res_ref = bf16[1024,3072]{1,0:T(8,128)(2,1)} custom-call(s32[3,65]{1,0:T(4,128)} %pad_add_fusion.lists, bf16[1024,6912]{1,0:T(8,128)(2,1)} %px_ref.1, s32[1024,1]{1,0:T(8,128)} %copy.98.cat_ref, bf16[128,1024]{1,0:T(8,128)(2,1)} %pad.25.ra_ref, bf16[640,1024]{1,0:T(8,128)(2,1)} %pad.26.rb_ref, bf16[2304,1024]{1,0:T(8,128)(2,1)} %rc_ref.7), custom_call_target="tpu_custom_call" | custom-call | flops 7549747200 | bytes 20447232 | tf_op jit(solution)/shard_map/resize/pallas_call | solution.py:109
  72.7 68.6 %all-gather.4.cloned.1.call-done = bf16[12288,768]{1,0:T(8,128)(2,1)} async-done(((bf16[384,768]{1,0:T(8,128)(2,1)}), bf16[12288,768]{1,0:T(8,128)(2,1)}) %all-gather.4.cloned.1.call-update) | async-done | bytes 18874384 | tf_op jit(solution)/shard_map/all_gather | solution.py:765
  141.3 17.1 %embed.1 = (f32[1024,768]{1,0:T(8,128)}, bf16[1024,768]{1,0:T(8,128)(2,1)}, bf16[1024,2304]{1,0:T(8,128)(2,1)}) custom-call(bf16[1024,3072]{1,0:T(8,128)(2,1)} %resize.1.res_ref, bf16[4,4,768,768]{3,2,1,0:T(8,128)(2,1)} %bitcast.91, bf16[4,8,4,96,768]{4,3,2,1,0:T(8,128)(2,1)} %bitcast.92, bf16[1024,128]{1,0:T(8,128)(2,1)} %pad_select_fusion.pos_ref, ...), custom_call_target="tpu_custom_call" | custom-call | flops 8455716864 | bytes 23986176 | tf_op jit(solution)/shard_map/embed/pallas_call | solution.py:234
  158.5 31.3 %attend.1 = (bf16[1024,768]{1,0:T(8,128)(2,1)}, f32[1024,768]{1,0:T(8,128)}) custom-call(s32[1]{0:T(128)} %bitcast.15.dense_ref, bf16[1024,2304]{1,0:T(8,128)(2,1)} %get-tuple-element.90.q_ref.k_ref.v_ref, bf16[1024,2304]{1,0:T(8,128)(2,1)} %get-tuple-element.90.q_ref.k_ref.v_ref, bf16[1024,2304]{1,0:T(8,128)(2,1)} %get-tuple-element.90.q_ref.k_ref.v_ref, ...), custom_call_target="tpu_custom_call" | custom-call | flops 12884901888 | bytes 9437184 | tf_op jit(solution)/shard_map/attend/pallas_call | solution.py:304
  189.8 48.2 %mlp.1 = (bf16[1024,768]{1,0:T(8,128)(2,1)}, f32[1024,768]{1,0:T(8,128)}, bf16[1024,768]{1,0:T(8,128)(2,1)}, bf16[4,768,768]{2,1,0:T(8,128)(2,1)}, bf16[8,4,96,7...) custom-call(f32[1024,768]{1,0:T(8,128)} %get-tuple-element.89.embed_ref, ...), custom_call_target="tpu_custom_call" | custom-call | flops 32614907904 | bytes 36962304 | tf_op jit(solution)/shard_map/mlp/pallas_call | solution.py:477
  238.9 52.4 %attend_back.1.dproj_ref = bf16[3,1024,768]{2,1,0:T(8,128)(2,1)} custom-call(s32[1]{0:T(128)} %bitcast.15.dense_ref, bf16[1024,2304]{1,0:T(8,128)(2,1)} %get-tuple-element.90.q_ref.k_ref.v_ref, bf16[1024,2304]{1,0:T(8,128)(2,1)} %get-tuple-element.90.q_ref.k_ref.v_ref, bf16[1024,2304]{1,0:T(8,128)(2,1)} %get-tuple-element.90.q_ref.k_ref.v_ref, ...), custom_call_target="tpu_custom_call" | custom-call | flops 32212254720 | bytes 17301504 | tf_op jit(solution)/shard_map/attend_back/pallas_call | solution.py:384
  291.4 12.7 %embed_back.1 = (bf16[1024,768]{1,0:T(8,128)(2,1)}, f32[128,768]{1,0:T(8,128)}, f32[16,768]{1,0:T(8,128)}) custom-call(bf16[3,1024,768]{2,1,0:T(8,128)(2,1)} %attend_back.1.dproj_ref, bf16[4,8,4,96,768]{4,3,2,1,0:T(8,128)(2,1)} %bitcast.96, f32[1024,768]{1,0:T(8,128)} %get-tuple-element.89.embed_ref, f32[1024,768]{1,0:T(8,128)} %get-tuple-element.97.ghid_ref, ...), custom_call_target="tpu_custom_call" | custom-call | flops 1000000 | bytes 100000 | tf_op jit(solution)/shard_map/embed_back/pallas_call | solution.py:616
  307.2 10.3 %patch_grad.1 = (bf16[4,416,768]{2,1,0:T(8,128)(2,1)}, bf16[4,416,768]{2,1,0:T(8,128)(2,1)}) custom-call(s32[1]{0:T(128)} %bitcast.21.core_ref, bf16[1024,3072]{1,0:T(8,128)(2,1)} %resize.1.res_ref, bf16[1024,768]{1,0:T(8,128)(2,1)} %get-tuple-element.140.g_ref, bf16[8,32,768]{2,1,0:T(8,128)(2,1)} %bitcast.113), custom_call_target="tpu_custom_call" | custom-call | flops 1000000 | bytes 100000 | tf_op jit(solution)/shard_map/patch_grad/pallas_call | solution.py:665
  317.4 9.0 %qkv_grad.1 = (bf16[4,4,96,768]{3,2,1,0:T(8,128)(2,1)}, bf16[4,4,96,768]{3,2,1,0:T(8,128)(2,1)}) custom-call(s32[1]{0:T(128)} %bitcast.21.core_ref, bf16[1024,768]{1,0:T(8,128)(2,1)} %get-tuple-element.101.norm_ref, bf16[3,1024,768]{2,1,0:T(8,128)(2,1)} %attend_back.1.dproj_ref, bf16[8,96,768]{2,1,0:T(8,128)(2,1)} %get-tuple-element.110.gwo_ref), custom_call_target="tpu_custom_call" | custom-call | flops 1000000 | bytes 100000 | tf_op jit(solution)/shard_map/qkv_grad/pallas_call | solution.py:549
  326.9 2.3 add_convert_fusion
  331.7 2.2 add_convert_fusion.1
  336.1 1.5 collective-permute-start.3
  337.6 15.5 %unresize.3.rest_0_ = bf16[1024,6912]{1,0:T(8,128)(2,1)} custom-call(s32[3,65]{1,0:T(4,128)} %pad_add_fusion.lists, bf16[1024,768]{1,0:T(8,128)(2,1)} %get-tuple-element.140.g_ref, bf16[4,3,1024,768]{3,2,1,0:T(8,128)(2,1)} %bitcast.97, s32[1024,1]{1,0:T(8,128)} %copy.98.cat_ref, bf16[128,1024]{1,0:T(8,128)(2,1)} %pad.25.ra_ref, ...), custom_call_target="tpu_custom_call" | custom-call | flops 1000000 | bytes 100000 | tf_op jit(solution)/shard_map/unresize/pallas_call | solution.py:144
  353.2 10.5 %collective-permute-done.2 = bf16[2,2,192,768]{3,2,1,0:T(8,128)(2,1)} collective-permute-done((bf16[2,2,192,768]{3,2,1,0:T(8,128)(2,1)}, bf16[2,2,192,768]{3,2,1,0:T(8,128)(2,1)}, u32[]{:S(2)}, u32[]{:S(2)}) %collective-permute-start.2) | collective-permute-done | bytes 1179680 | tf_op jit(solution)/shard_map/ppermute | solution.py:701
  363.7 1.5 add_convert_fusion.3
  366.6 1.6 add_convert_fusion.2
  369.3 15.9 %unresize.4.rest_0_ = bf16[1024,6912]{1,0:T(8,128)(2,1)} custom-call(s32[3,65]{1,0:T(4,128)} %pad_add_fusion.lists, bf16[1024,768]{1,0:T(8,128)(2,1)} %get-tuple-element.140.g_ref, bf16[4,3,1024,768]{3,2,1,0:T(8,128)(2,1)} %bitcast.98, s32[1024,1]{1,0:T(8,128)} %copy.98.cat_ref, bf16[128,1024]{1,0:T(8,128)(2,1)} %pad.25.ra_ref, ...), custom_call_target="tpu_custom_call", output_to_operand_aliasing={{}: (7, {})} | custom-call | flops 1000000 | bytes 100000 | tf_op jit(solution)/shard_map/unresize/pallas_call | solution.py:144
  386.4 5.2 %collective-permute-start.9 = (bf16[192,768]{1,0:T(8,128)(2,1)S(1)}, bf16[192,768]{1,0:T(8,128)(2,1)S(1)}, u32[]{:S(2)}, u32[]{:S(2)}) collective-permute-start(bf16[192,768]{1,0:T(8,128)(2,1)S(1)} %get-tuple-element.153), channel_id=1, source_target_pairs={{0,4},{1,5},{2,6},{3,7},{4,0},{5,1},{6,2},{7,3},{8,12},{9,13},{10,... | collective-permute-start | bytes 884744 | tf_op jit(solution)/shard_map/ppermute | solution.py:701
  391.9 15.6 %unresize.5 = bf16[1024,6912]{1,0:T(8,128)(2,1)} custom-call(s32[3,65]{1,0:T(4,128)} %pad_add_fusion.lists, bf16[1024,768]{1,0:T(8,128)(2,1)} %get-tuple-element.140.g_ref, bf16[4,3,1024,768]{3,2,1,0:T(8,128)(2,1)} %bitcast.99, s32[1024,1]{1,0:T(8,128)} %copy.98.cat_ref, bf16[128,1024]{1,0:T(8,128)(2,1)} %pad.25.ra_ref, ...), custom_call_target="tpu_custom_call", output_to_operand_aliasing={{}: (7, {})} | custom-call | flops 1000000 | bytes 100000 | tf_op jit(solution)/shard_map/unresize/pallas_call | solution.py:144
  407.5 4.2 collective-permute-start.6
  412.1 7.4 %collective-permute-done.6 = bf16[2,104,768]{2,1,0:T(8,128)(2,1)S(1)} collective-permute-done((bf16[2,104,768]{2,1,0:T(8,128)(2,1)S(1)}, bf16[2,104,768]{2,1,0:T(8,128)(2,1)S(1)}, u32[]{:S(2)}, u32[]{:S(2)}) %collective-permute-start.6) | collective-permute-done | bytes 319520 | tf_op jit(solution)/shard_map/ppermute | solution.py:701
  419.8 1.2 collective-permute-start.11
  421.0 8.7 %collective-permute-done.7 = bf16[104,768]{1,0:T(8,128)(2,1)S(1)} collective-permute-done((bf16[104,768]{1,0:T(8,128)(2,1)S(1)}, bf16[104,768]{1,0:T(8,128)(2,1)S(1)}, u32[]{:S(2)}, u32[]{:S(2)}) %collective-permute-start.7) | collective-permute-done | bytes 159776 | tf_op jit(solution)/shard_map/ppermute | solution.py:701
  429.8 2.1 collective-permute-start.12
  431.9 4.9 %collective-permute-done.8 = bf16[104,768]{1,0:T(8,128)(2,1)S(1)} collective-permute-done((bf16[104,768]{1,0:T(8,128)(2,1)S(1)}, bf16[104,768]{1,0:T(8,128)(2,1)S(1)}, u32[]{:S(2)}, u32[]{:S(2)}) %collective-permute-start.8) | collective-permute-done | bytes 159776 | tf_op jit(solution)/shard_map/ppermute | solution.py:701
  437.0 4.2 collective-permute-done.12
  441.3 2.6 collective-permute-done.13
  450.0 1.2 copy.120
  (167 shorter events, 36.4 us)
Async XLA Ops:
  7.2 134.1 %all-gather.4.cloned.1.call-start = ((), (), s32[]{:S(2)}) async-start(), calls=%async_computation.2 | async-start | bytes 19464192 | tf_op jit(solution)/shard_map/all_gather | solution.py:765
  11.3 2.5 copy-start.16
  11.3 2.6 copy-start.12
  11.3 2.6 copy-start.15
  11.3 2.6 copy-start.17
  11.3 18.7 %copy-start.18 = (s32[1,40]{1,0:T(1,128)S(1)}, s32[1,40]{1,0:T(1,128)}, u32[]{:S(2)}) copy-start(s32[1,40]{1,0:T(1,128)} %param.21) | copy-start | bytes 484
  11.3 18.7 %copy-start.19 = (s32[4]{0:T(128)S(1)}, s32[4]{0:T(128)}, u32[]{:S(2)}) copy-start(s32[4]{0:T(128)} %constant.127.clone) | copy-start | bytes 52
  11.3 19.1 %copy-start.9 = (bf16[900,49]{0,1:T(8,128)(2,1)S(1)}, bf16[900,49]{0,1:T(8,128)(2,1)}, u32[]{:S(2)}) copy-start(bf16[900,49]{0,1:T(8,128)(2,1)} %param.25) | copy-start | bytes 264604
  13.7 16.9 %copy-start.11 = (bf16[100,49]{0,1:T(8,128)(2,1)S(1)}, bf16[100,49]{0,1:T(8,128)(2,1)}, u32[]{:S(2)}) copy-start(bf16[100,49]{0,1:T(8,128)(2,1)} %param.26) | copy-start | bytes 29404
  13.7 18.8 %copy-start.2 = (bf16[576,1024]{1,0:T(8,128)(2,1)S(1)}, bf16[576,1024]{1,0:T(8,128)(2,1)}, u32[]{:S(2)}) copy-start(bf16[576,1024]{1,0:T(8,128)(2,1)} %param.23) | copy-start | bytes 3538948
  13.7 277.7 %reduce-scatter.3.cloned.1.call-start = ((), (), s32[]{:S(2)}) async-start(), calls=%async_computation.3 | async-start | bytes 5308416 | tf_op jit(solution)/shard_map/reduce_scatter | solution.py:809
  30.9 2.8 copy-start.8
  32.5 4.7 %copy-start.14 = (bf16[25,49]{1,0:T(8,128)(2,1)S(1)}, bf16[25,49]{1,0:T(8,128)(2,1)}, u32[]{:S(2)}) copy-start(bf16[25,49]{1,0:T(8,128)(2,1)} %param.27) | copy-start | bytes 7354
  238.0 131.3 %reduce-scatter.5.cloned.1.call-start = ((), (), s32[]{:S(2)}) async-start(), calls=%async_computation.4 | async-start | bytes 5308416 | tf_op jit(solution)/shard_map/reduce_scatter | solution.py:809
  238.8 198.2 %all-reduce.9.cloned.1.call-start = ((), (), s32[]{:S(2)}) async-start(), calls=%async_computation.5 | async-start | bytes 2359296 | tf_op jit(solution)/shard_map/psum | solution.py:854
  291.4 13.7 %copy-start.10 = (f32[16,768]{1,0:T(8,128)S(1)}, f32[16,768]{1,0:T(8,128)}, u32[]{:S(2)}) copy-start(f32[16,768]{1,0:T(8,128)} %get-tuple-element.102) | copy-start | bytes 147460
  317.4 9.5 %collective-permute-start = (bf16[2,2,416,768]{3,2,1,0:T(8,128)(2,1)}, bf16[2,2,416,768]{3,2,1,0:T(8,128)(2,1)}, u32[]{:S(2)}, u32[]{:S(2)}) collective-permute-start(bf16[2,2,416,768]{3,2,1,0:T(8,128)(2,1)} %bitcast.134), channel_id=1, source_target_pairs={{0,1},{1,0},{2,3},{3,2},{4,5},{5,4},{6,7},{7,6},{8,9},{9,8},{10,11... | collective-permute-start | bytes 7667720 | tf_op jit(solution)/shard_map/ppermute | solution.py:701
  317.4 9.5 %copy-start = (bf16[4,416,768]{2,1,0:T(8,128)(2,1)S(1)}, bf16[4,416,768]{2,1,0:T(8,128)(2,1)}, u32[]{:S(2)}) copy-start(bf16[4,416,768]{2,1,0:T(8,128)(2,1)} %get-tuple-element.106) | copy-start | bytes 7667716
  326.4 5.2 %collective-permute-start.1 = (bf16[2,2,384,768]{3,2,1,0:T(8,128)(2,1)}, bf16[2,2,384,768]{3,2,1,0:T(8,128)(2,1)}, u32[]{:S(2)}, u32[]{:S(2)}) collective-permute-start(bf16[2,2,384,768]{3,2,1,0:T(8,128)(2,1)} %bitcast.135), channel_id=1, source_target_pairs={{0,1},{1,0},{2,3},{3,2},{4,5},{5,4},{6,7},{7,6},{8,9},{9,8},{10,11... | collective-permute-start | bytes 7077896 | tf_op jit(solution)/shard_map/ppermute | solution.py:701
  329.3 2.4 copy-start.1
  335.1 28.6 %collective-permute-start.2 = (bf16[2,2,192,768]{3,2,1,0:T(8,128)(2,1)}, bf16[2,2,192,768]{3,2,1,0:T(8,128)(2,1)}, u32[]{:S(2)}, u32[]{:S(2)}) collective-permute-start(bf16[2,2,192,768]{3,2,1,0:T(8,128)(2,1)} %get-tuple-element.126), channel_id=1, source_target_pairs={{0,8},{8,0},{16,24},{24,16},{1,9},{9,1},{17,25},{25,17},{2,10},{10... | collective-permute-start | bytes 3538952 | tf_op jit(solution)/shard_map/ppermute | solution.py:701
  336.1 30.4 %collective-permute-start.3 = (bf16[2,2,208,768]{3,2,1,0:T(8,128)(2,1)}, bf16[2,2,208,768]{3,2,1,0:T(8,128)(2,1)}, u32[]{:S(2)}, u32[]{:S(2)}) collective-permute-start(bf16[2,2,208,768]{3,2,1,0:T(8,128)(2,1)} %get-tuple-element.129), channel_id=1, source_target_pairs={{0,16},{8,24},{16,0},{24,8},{1,17},{9,25},{17,1},{25,9},{2,18},{10... | collective-permute-start | bytes 3833864 | tf_op jit(solution)/shard_map/ppermute | solution.py:701
  366.1 19.1 %collective-permute-start.4 = (bf16[2,192,768]{2,1,0:T(8,128)(2,1)}, bf16[2,192,768]{2,1,0:T(8,128)(2,1)}, u32[]{:S(2)}, u32[]{:S(2)}) collective-permute-start(bf16[2,192,768]{2,1,0:T(8,128)(2,1)} %get-tuple-element.135), channel_id=1, source_target_pairs={{0,2},{1,3},{2,0},{3,1},{4,6},{5,7},{6,4},{7,5},{8,10},{9,11},{10,... | collective-permute-start | bytes 1769480 | tf_op jit(solution)/shard_map/ppermute | solution.py:701
  368.3 23.3 %collective-permute-start.5 = (bf16[2,2,104,768]{3,2,1,0:T(8,128)(2,1)S(1)}, bf16[2,2,104,768]{3,2,1,0:T(8,128)(2,1)S(1)}, u32[]{:S(2)}, u32[]{:S(2)}) collective-permute-start(bf16[2,2,104,768]{3,2,1,0:T(8,128)(2,1)S(1)} %get-tuple-element.138), channel_id=1, source_target_pairs={{0,8},{8,0},{16,24},{24,16},{1,9},{9,1},{17,25},{25,17},{2,10},{10... | collective-permute-start | bytes 1916936 | tf_op jit(solution)/shard_map/ppermute | solution.py:701
  386.4 25.3 %collective-permute-start.9 = (bf16[192,768]{1,0:T(8,128)(2,1)S(1)}, bf16[192,768]{1,0:T(8,128)(2,1)S(1)}, u32[]{:S(2)}, u32[]{:S(2)}) collective-permute-start(bf16[192,768]{1,0:T(8,128)(2,1)S(1)} %get-tuple-element.153), channel_id=1, source_target_pairs={{0,4},{1,5},{2,6},{3,7},{4,0},{5,1},{6,2},{7,3},{8,12},{9,13},{10,... | collective-permute-start | bytes 884744 | tf_op jit(solution)/shard_map/ppermute | solution.py:701
  407.5 12.0 %collective-permute-start.6 = (bf16[2,104,768]{2,1,0:T(8,128)(2,1)S(1)}, bf16[2,104,768]{2,1,0:T(8,128)(2,1)S(1)}, u32[]{:S(2)}, u32[]{:S(2)}) collective-permute-start(bf16[2,104,768]{2,1,0:T(8,128)(2,1)S(1)} %get-tuple-element.143), channel_id=1, source_target_pairs={{0,2},{1,3},{2,0},{3,1},{4,6},{5,7},{6,4},{7,5},{8,10},{9,11},{10,... | collective-permute-start | bytes 958472 | tf_op jit(solution)/shard_map/ppermute | solution.py:701
  411.8 7.9 %collective-permute-start.10 = (bf16[96,768]{1,0:T(8,128)(2,1)S(1)}, bf16[96,768]{1,0:T(8,128)(2,1)S(1)}, u32[]{:S(2)}, u32[]{:S(2)}) collective-permute-start(bf16[96,768]{1,0:T(8,128)(2,1)S(1)} %get-tuple-element.155), channel_id=1, source_target_pairs={{0,16},{8,24},{16,0},{24,8},{1,17},{9,25},{17,1},{25,9},{2,18},{10... | collective-permute-start | bytes 442376 | tf_op jit(solution)/shard_map/ppermute | solution.py:701
  419.6 10.0 %collective-permute-start.7 = (bf16[104,768]{1,0:T(8,128)(2,1)S(1)}, bf16[104,768]{1,0:T(8,128)(2,1)S(1)}, u32[]{:S(2)}, u32[]{:S(2)}) collective-permute-start(bf16[104,768]{1,0:T(8,128)(2,1)S(1)} %get-tuple-element.145), channel_id=1, source_target_pairs={{0,4},{1,5},{2,6},{3,7},{4,0},{5,1},{6,2},{7,3},{8,12},{9,13},{10,... | collective-permute-start | bytes 479240 | tf_op jit(solution)/shard_map/ppermute | solution.py:701
  419.8 10.0 %collective-permute-start.11 = (bf16[96,768]{1,0:T(8,128)(2,1)S(1)}, bf16[96,768]{1,0:T(8,128)(2,1)S(1)}, u32[]{:S(2)}, u32[]{:S(2)}) collective-permute-start(bf16[96,768]{1,0:T(8,128)(2,1)S(1)} %add_convert_fusion.9), channel_id=1, source_target_pairs={{0,16},{8,24},{16,0},{24,8},{1,17},{9,25},{17,1},{25,9},{2,18},{10... | collective-permute-start | bytes 442376 | tf_op jit(solution)/shard_map/ppermute | solution.py:701
  429.7 7.1 %collective-permute-start.8 = (bf16[104,768]{1,0:T(8,128)(2,1)S(1)}, bf16[104,768]{1,0:T(8,128)(2,1)S(1)}, u32[]{:S(2)}, u32[]{:S(2)}) collective-permute-start(bf16[104,768]{1,0:T(8,128)(2,1)S(1)} %add_convert_fusion.8), channel_id=1, source_target_pairs={{0,8},{8,0},{16,24},{24,16},{1,9},{9,1},{17,25},{25,17},{2,10},{10... | collective-permute-start | bytes 479240 | tf_op jit(solution)/shard_map/ppermute | solution.py:701
  429.8 11.3 %collective-permute-start.12 = (bf16[192,768]{1,0:T(8,128)(2,1)S(1)}, bf16[192,768]{1,0:T(8,128)(2,1)S(1)}, u32[]{:S(2)}, u32[]{:S(2)}) collective-permute-start(bf16[192,768]{1,0:T(8,128)(2,1)S(1)} %pad_maximum_fusion.4), channel_id=1, source_target_pairs={{0,8},{8,0},{16,24},{24,16},{1,9},{9,1},{17,25},{25,17},{2,10},{10... | collective-permute-start | bytes 884744 | tf_op jit(solution)/shard_map/ppermute | solution.py:701
  436.9 7.1 %collective-permute-start.13 = (bf16[208,768]{1,0:T(8,128)(2,1)S(1)}, bf16[208,768]{1,0:T(8,128)(2,1)S(1)}, u32[]{:S(2)}, u32[]{:S(2)}) collective-permute-start(bf16[208,768]{1,0:T(8,128)(2,1)S(1)} %pad_maximum_fusion.3), channel_id=1, source_target_pairs={{0,16},{8,24},{16,0},{24,8},{1,17},{9,25},{17,1},{25,9},{2,18},{10... | collective-permute-start | bytes 958472 | tf_op jit(solution)/shard_map/ppermute | solution.py:701
  (6 other events, 7.9 us)
Sparse Core Ops, SparseCore 0:
  13.8 127.4 all-gather.3
  238.1 53.2 reduce-scatter.2
  293.7 53.3 reduce-scatter.4
  369.4 62.4 all-reduce.8

commit v3 on v2

--- a/solution.py
+++ b/solution.py
@@ -14,6 +14,7 @@
 F32 = jnp.float32
 BF16 = jnp.bfloat16
 NEG = -1e30
+SCALE = 0.125 * 1.4426950408889634
 VMEM = 60 * 1024 * 1024
 
 
@@ -125,7 +126,7 @@
 def unresize_kernel(lists, g_ref, w_ref, cat_ref, ra_ref, rb_ref, rc_ref, *rest):
     out_ref, grow, lhs = rest[-3:]
     out_ref[...] = jnp.zeros_like(out_ref)
-    grow[...] = nt(g_ref[...], w_ref[0, 0]).astype(BF16)
+    grow[...] = nt(g_ref[...], w_ref[0]).astype(BF16)
     for class_id, matrix in enumerate((ra_ref, rb_ref, rc_ref)):
         resize_rows(
             lists, cat_ref, grow, out_ref, lhs, class_id, grow.shape[1],
@@ -133,13 +134,13 @@
         )
 
 
-def unresize(lists, g_emb, groups, category, ra, rb, rc, area, channel, part, parts, before):
+def unresize(lists, g_emb, patch, category, ra, rb, rc, area, channel, part, parts, before):
     tokens, width = g_emb.shape
     base = rc.shape[1]
     rows = tokens // parts
     whole = lambda a: pl.BlockSpec(a.shape, lambda c, s: (0, 0))
     some = lambda a: pl.BlockSpec((rows, a.shape[1]), lambda c, s: (part, 0))
-    kernels = groups.reshape(4, 3, base, width)
+    kernels = patch.reshape(3, base, width)
     more = [] if before is None else [before]
     return pl.pallas_call(
         unresize_kernel,
@@ -147,7 +148,7 @@
             num_scalar_prefetch=1,
             grid=(1,),
             in_specs=[
-                some(g_emb), pl.BlockSpec((1, 1, base, width), lambda c, s: (0, channel, 0, 0)),
+                some(g_emb), pl.BlockSpec((1, base, width), lambda c, s: (channel, 0, 0)),
                 some(category), whole(ra), whole(rb), whole(rc),
             ] + [pl.BlockSpec(memory_space=pl.ANY)] * len(more),
             out_specs=pl.BlockSpec((rows, area), lambda c, s: (part, channel)),
@@ -185,131 +186,148 @@
     body(pl.ds(0, tokens))
 
 
-def embed_kernel(res_ref, kern_ref, qkv_ref, pos_ref, table_ref, small_ref, embed_ref, norm_ref, proj_ref):
+def embed_kernel(res_ref, kern_ref, pos_ref, table_ref, small_ref, embed_ref, norm_ref):
     step = pl.program_id(0)
-    tokens = res_ref.shape[0]
 
     @pl.when(step == 0)
     def _():
-        def body(rows):
-            embed_ref[rows, :] = (
-                nn(res_ref[rows, :], square(kern_ref)) + small_ref[0:1, :] + nn(pos_ref[rows, :], table_ref[...])
-            )
-
-        row_tiles(tokens, body)
-
-    @pl.when((step > 0) & (step < 4))
-    def _():
-        def body(rows):
-            embed_ref[rows, :] += nn(res_ref[rows, :], square(kern_ref))
-
-        row_tiles(tokens, body)
+        embed_ref[...] = (
+            nn(res_ref[...], kern_ref[0]) + small_ref[0:1, :] + nn(pos_ref[...], table_ref[...])
+        )
+
+    @pl.when((step > 0) & (step < 3))
+    def _():
+        embed_ref[...] += nn(res_ref[...], kern_ref[0])
 
     @pl.when(step == 3)
     def _():
-        def body(rows):
-            xhat, _ = norm_parts(embed_ref[rows, :])
-            norm_ref[rows, :] = (xhat * small_ref[7:8, :] + small_ref[1:2, :]).astype(BF16)
-
-        row_tiles(tokens, body)
-
-    @pl.when(step >= 4)
-    def _():
-        shift = jnp.where(
-            step == 4, small_ref[2:3, :], jnp.where(step == 6, small_ref[3:4, :], jnp.zeros_like(small_ref[3:4, :]))
-        )
-
-        def body(rows):
-            proj_ref[rows, :] = (nn(norm_ref[rows, :], square(qkv_ref)) + shift).astype(BF16)
-
-        row_tiles(tokens, body)
-
-
-def embed_call(resized, rowwise, colwise, pos_rows, table, small):
+        value = embed_ref[...] + nn(res_ref[...], kern_ref[0])
+        embed_ref[...] = value
+        xhat, _ = norm_parts(value)
+        norm_ref[...] = (xhat * small_ref[7:8, :] + small_ref[1:2, :]).astype(BF16)
+
+
+def embed_call(resized, patch, pos_rows, table, small):
     tokens = resized.shape[0]
     width = small.shape[1]
+    whole = lambda a: pl.BlockSpec(a.shape, lambda s: (0, 0))
+    fixed = pl.BlockSpec((tokens, width), lambda s: (0, 0))
+    return pl.pallas_call(
+        embed_kernel,
+        grid=(4,),
+        in_specs=[
+            pl.BlockSpec((tokens, width), lambda s: (0, s)),
+            pl.BlockSpec((1, width, width), lambda s: (s, 0, 0)),
+            whole(pos_rows), whole(table), whole(small),
+        ],
+        out_specs=[fixed, fixed],
+        out_shape=[jax.ShapeDtypeStruct((tokens, width), F32), jax.ShapeDtypeStruct((tokens, width), BF16)],
+        compiler_params=params(),
+        cost_estimate=cost(4 * 2 * tokens * width * width, tokens * width * 14 + 4 * width * width * 2),
+        name="embed",
+    )(resized, patch.reshape(4, width, width), pos_rows, table, small)
+
+
+def project_kernel(norm_ref, qkv_ref, small_ref, proj_ref):
+    step = pl.program_id(0)
+    none = jnp.zeros_like(small_ref[3:4, :])
+    shift = jnp.where(step == 0, small_ref[2:3, :], jnp.where(step == 2, small_ref[3:4, :], none))
+    proj_ref[...] = (nn(norm_ref[...], square(qkv_ref)) + shift).astype(BF16)
+
+
+def project(normed1, colwise, small):
+    tokens, width = normed1.shape
     bands, deep = colwise.shape[1], colwise.shape[3]
     whole = lambda a: pl.BlockSpec(a.shape, lambda s: (0, 0))
-    fixed = pl.BlockSpec((tokens, width), lambda s: (0, 0))
-    return pl.pallas_call(
-        embed_kernel,
-        grid=(7,),
+    return pl.pallas_call(
+        project_kernel,
+        grid=(3,),
         in_specs=[
-            pl.BlockSpec((tokens, width), lambda s: (0, jnp.minimum(s, 3))),
-            pl.BlockSpec((1, 1, width, width), lambda s: (0, jnp.minimum(s, 3), 0, 0)),
-            pl.BlockSpec((1, bands, 1, deep, width), lambda s: (1, 0, jnp.maximum(s - 4, 0), 0, 0)),
-            whole(pos_rows), whole(table), whole(small),
-        ],
-        out_specs=[fixed, fixed, pl.BlockSpec((tokens, width), lambda s: (0, jnp.maximum(s - 4, 0)))],
-        out_shape=[
-            jax.ShapeDtypeStruct((tokens, width), F32),
-            jax.ShapeDtypeStruct((tokens, width), BF16),
-            jax.ShapeDtypeStruct((tokens, 3 * width), BF16),
-        ],
-        compiler_params=params(),
-        cost_estimate=cost(7 * 2 * tokens * width * width, tokens * width * 20 + 7 * width * width * 2),
-        name="embed",
-    )(resized, rowwise, colwise, pos_rows, table, small)
-
-
-def attend_kernel(dense_ref, q_ref, k_ref, v_ref, oh_ref, km_ref, o_ref, lse_ref, kaug, vaug):
+            whole(normed1), pl.BlockSpec((1, bands, 1, deep, width), lambda s: (s, 0, 0, 0, 0)), whole(small),
+        ],
+        out_specs=pl.BlockSpec((tokens, width), lambda s: (0, s)),
+        out_shape=jax.ShapeDtypeStruct((tokens, 3 * width), BF16),
+        compiler_params=params(),
+        cost_estimate=cost(3 * 2 * tokens * width * width, tokens * width * 8 + 3 * width * width * 2),
+        name="project",
+    )(normed1, colwise, small)
+
+
+def half_roll(x):
+    return jnp.concatenate([x[:, 64:128], x[:, 0:64]], axis=1)
+
+
+def score_sides(q_ref, k_ref, tails, km_ref, qside, kside):
+    lane = lax.broadcasted_iota(jnp.int32, (1, 128), 1)
+    q = q_ref[...].astype(F32) * SCALE
+    high = q.astype(BF16)
+    low = half_roll((q - high.astype(F32)).astype(BF16))
+    k = k_ref[...]
+    turned = half_roll(k)
+    for h in range(2):
+        mine = (lane < 64) if h == 0 else (lane >= 64)
+        qside[h, :, 0:128] = jnp.where(mine, high, low)
+        qside[h, :, 128:256] = tails[h]
+        kside[h, :, 0:128] = jnp.where(mine, k, turned)
+        kside[h, :, 128:256] = km_ref[...]
+
+
+def attend_kernel(q_ref, k_ref, v_ref, oh_ref, km_ref, o_ref, lse_ref, qside, kside, vside, kept, head_out, head_log):
     tokens = q_ref.shape[0]
+    rows, cols = tokens // 2, tokens // 2
     lane = lax.broadcasted_iota(jnp.int32, (1, 128), 1)
-    kaug[:, 0:128] = k_ref[...]
-    kaug[:, 128:256] = km_ref[...]
-    vaug[:, 0:128] = v_ref[...]
-    vaug[:, 128:256] = jnp.ones((tokens, 128), BF16)
-
-    def tile(rows, cols):
-        q = q_ref[rows, :] * jnp.asarray(0.125, BF16)
-        oh = oh_ref[rows, :]
-        keys, vals = kaug[cols, :], vaug[cols, :]
-        outs, logs = [], []
-        for h in range(2):
-            mine = (lane < 64) if h == 0 else (lane >= 64)
-            left = jnp.concatenate([jnp.where(mine, q, jnp.zeros_like(q)), oh], axis=1)
-            scores = nt(left, keys)
-            top = jnp.max(scores, axis=1, keepdims=True)
-            weights = jnp.exp(scores - top).astype(BF16)
-            both = nn(weights, vals)
-            total = both[:, 128:256]
-            outs.append(both[:, 0:128] / total)
-            logs.append(top + jnp.log(total))
-        o_ref[rows, :] = jnp.where(lane < 64, outs[0], outs[1]).astype(o_ref.dtype)
-        lse_ref[rows, :] = jnp.where(lane < 64, logs[0], logs[1])
-
-    attend_tiles(dense_ref, tokens, tile)
-
-
-def attend_tiles(dense_ref, tokens, tile):
-    @pl.when(dense_ref[0] != 0)
-    def _():
-        @pl.loop(0, tokens // TILE)
-        def _(t):
-            tile(pl.ds(pl.multiple_of(t * TILE, TILE), TILE), pl.ds(0, tokens))
-
-    @pl.when(dense_ref[0] == 0)
-    def _():
-        @pl.loop(0, tokens // TILE)
-        def _(t):
-            first = pl.multiple_of(jnp.clip(t * TILE - 128, 0, tokens - 512), 128)
-            tile(pl.ds(pl.multiple_of(t * TILE, TILE), TILE), pl.ds(first, 512))
-
-
-def attend(dense, projected, onehot, keymask):
+    score_sides(q_ref, k_ref, [oh_ref[...]] * 2, km_ref, qside, kside)
+    vside[:, 0:128] = v_ref[...]
+    vside[:, 128:256] = jnp.ones((tokens, 128), BF16)
+    units = [(t, h) for t in range(tokens // rows) for h in range(2)]
+    chunks = [slice(c * cols, (c + 1) * cols) for c in range(tokens // cols)]
+
+    def scores(unit, slot, chunk, top):
+        t, h = unit
+        value = nt(qside[h, t * rows : (t + 1) * rows, :], kside[h, chunk, :])
+        kept[slot, :, chunk] = value
+        for i in range(cols // 128):
+            part = value[:, i * 128 : (i + 1) * 128]
+            top = part if top is None else jnp.maximum(top, part)
+        return top
+
+    top = None
+    for chunk in chunks:
+        top = scores(units[0], 0, chunk, top)
+    for u, (t, h) in enumerate(units):
+        highest = jnp.max(top, axis=1, keepdims=True)
+        top, total = None, None
+        for chunk in chunks:
+            if u + 1 < len(units):
+                top = scores(units[u + 1], (u + 1) % 2, chunk, top)
+            part = nn(jnp.exp2(kept[u % 2, :, chunk] - highest).astype(BF16), vside[chunk, :])
+            total = part if total is None else total + part
+        weight = total[:, 128:256]
+        out, log = total[:, 0:128] / weight, highest + jnp.log2(weight)
+        if h == 0:
+            head_out[...] = out
+            head_log[...] = log
+        else:
+            at = slice(t * rows, (t + 1) * rows)
+            o_ref[at, :] = jnp.where(lane < 64, head_out[...], out).astype(BF16)
+            lse_ref[at, :] = jnp.where(lane < 64, head_log[...], log)
+
+
+def attend(projected, onehot, keymask):
     tokens = projected.shape[0]
     pairs = projected.shape[1] // 3 // 128
-    part = lambda at: pl.BlockSpec((tokens, 128), lambda j, d: (0, at + j))
-    whole = pl.BlockSpec((tokens, 128), lambda j, d: (0, 0))
+    part = lambda at: pl.BlockSpec((tokens, 128), lambda j: (0, at + j))
+    whole = pl.BlockSpec((tokens, 128), lambda j: (0, 0))
     return pl.pallas_call(
         attend_kernel,
-        grid_spec=pltpu.PrefetchScalarGridSpec(
-            num_scalar_prefetch=1,
-            grid=(pairs,),
-            in_specs=[part(0), part(pairs), part(2 * pairs), whole, whole],
-            out_specs=[part(0), part(0)],
-            scratch_shapes=[pltpu.VMEM((tokens, 256), BF16), pltpu.VMEM((tokens, 256), BF16)],
-        ),
+        grid=(pairs,),
+        in_specs=[part(0), part(pairs), part(2 * pairs), whole, whole],
+        out_specs=[part(0), part(0)],
+        scratch_shapes=[
+            pltpu.VMEM((2, tokens, 256), BF16), pltpu.VMEM((2, tokens, 256), BF16), pltpu.VMEM((tokens, 256), BF16),
+            pltpu.VMEM((2, tokens // 2, tokens), F32),
+            pltpu.VMEM((tokens // 2, 128), F32), pltpu.VMEM((tokens // 2, 128), F32),
+        ],
         out_shape=[
             jax.ShapeDtypeStruct((tokens, pairs * 128), BF16),
             jax.ShapeDtypeStruct((tokens, pairs * 128), F32),
@@ -317,7 +335,7 @@
         compiler_params=params(),
         cost_estimate=cost(2 * 2 * 12 * tokens * tokens * 256, tokens * 2304 * 2 + tokens * 768 * 6, 12 * tokens * tokens),
         name="attend",
-    )(dense, projected, projected, projected, onehot, keymask)
+    )(projected, projected, projected, onehot, keymask)
 
 
 def split3(x):
@@ -329,75 +347,89 @@
 
 
 def attend_back_kernel(
-    dense_ref, q_ref, k_ref, v_ref, g_ref, o_ref, lse_ref, oh_ref, km_ref, out_ref, kaug, vaug, dkeys, dvals
+    q_ref, k_ref, v_ref, g_ref, o_ref, lse_ref, oh_ref, km_ref, out_ref,
+    qside, kside, vside, gside, qhead, dkeys, dvals, kept, dprobs, dquery,
 ):
     tokens = q_ref.shape[0]
+    rows, cols = tokens // 2, tokens // 2
     lane = lax.broadcasted_iota(jnp.int32, (1, 128), 1)
-    kaug[:, 0:128] = k_ref[...]
-    kaug[:, 128:256] = km_ref[...]
-    vaug[:, 0:128] = v_ref[...]
-    vaug[:, 128:256] = jnp.broadcast_to(jnp.where(lane < 3, -1.0, 0.0).astype(BF16), (tokens, 128))
-    dkeys[...] = jnp.zeros_like(dkeys)
-    dvals[...] = jnp.zeros_like(dvals)
 
     def put(parts, at, other):
         for i, piece in enumerate(parts):
             other = jnp.where(lane == at + i, piece, other)
         return other
 
-    def tile(rows, cols):
-        q = q_ref[rows, :] * jnp.asarray(0.125, BF16)
-        g = g_ref[rows, :]
-        oh = oh_ref[rows, :]
-        go = g.astype(F32) * o_ref[rows, :].astype(F32)
-        lse = lse_ref[rows, :]
-        keys, vals = kaug[cols, :], vaug[cols, :]
-        plain = keys[:, 0:128]
-        dqs, dkt, dvt = [], None, None
-        for h in range(2):
-            mine = (lane < 64) if h == 0 else (lane >= 64)
-            delta = jnp.sum(jnp.where(mine, go, 0.0), axis=1, keepdims=True)
-            qm = jnp.where(mine, q, jnp.zeros_like(q))
-            gm = jnp.where(mine, g, jnp.zeros_like(g))
-            qa = jnp.concatenate([qm, put(split3(lse[:, 64 * h : 64 * h + 1]), 64, oh)], axis=1)
-            ga = jnp.concatenate([gm, put(split3(delta), 0, jnp.zeros_like(oh))], axis=1)
-            probs = jnp.exp(nt(keys, qa))
-            dscores = (probs * nt(vals, ga)).astype(BF16)
-            a, b = nn(probs.astype(BF16), gm), nn(dscores, qm)
-            dvt = a if dvt is None else dvt + a
-            dkt = b if dkt is None else dkt + b
-            dqs.append(tn(dscores, plain))
-        out_ref[0, rows, :] = (jnp.where(lane < 64, dqs[0], dqs[1]) * 0.125).astype(BF16)
-        dkeys[cols, :] += dkt
-        dvals[cols, :] += dvt
-
-    attend_tiles(dense_ref, tokens, tile)
+    lse = lse_ref[...]
+    tails = [put(split3(lse[:, 64 * h : 64 * h + 1]), 64, oh_ref[...]) for h in range(2)]
+    score_sides(q_ref, k_ref, tails, km_ref, qside, kside)
+    vside[:, 0:128] = v_ref[...]
+    vside[:, 128:256] = jnp.broadcast_to(jnp.where(lane < 3, -1.0, 0.0).astype(BF16), (tokens, 128))
+    q = q_ref[...] * jnp.asarray(0.125, BF16)
+    g = g_ref[...]
+    go = g.astype(F32) * o_ref[...].astype(F32)
+    for h in range(2):
+        mine = (lane < 64) if h == 0 else (lane >= 64)
+        delta = jnp.sum(jnp.where(mine, go, 0.0), axis=1, keepdims=True)
+        gside[h, :, 0:128] = jnp.where(mine, g, jnp.zeros_like(g))
+        gside[h, :, 128:256] = put(split3(delta), 0, jnp.zeros((tokens, 128), BF16))
+        qhead[h] = jnp.where(mine, q, jnp.zeros_like(q))
+    units = [(t, h) for t in range(tokens // rows) for h in range(2)]
+    chunks = [slice(c * cols, (c + 1) * cols) for c in range(tokens // cols)]
+
+    def first(unit, slot, chunk):
+        t, h = unit
+        at = slice(t * rows, (t + 1) * rows)
+        kept[slot, chunk, :] = nt(kside[h, chunk, :], qside[h, at, :])
+        dprobs[slot, chunk, :] = nt(vside[chunk, :], gside[h, at, :])
+
+    for chunk in chunks:
+        first(units[0], 0, chunk)
+    for u, (t, h) in enumerate(units):
+        at = slice(t * rows, (t + 1) * rows)
+        dq = None
+        for chunk in chunks:
+            if u + 1 < len(units):
+                first(units[u + 1], (u + 1) % 2, chunk)
+            probs = jnp.exp2(kept[u % 2, chunk, :])
+            dscores = (probs * dprobs[u % 2, chunk, :]).astype(BF16)
+            dv, dk = nn(probs.astype(BF16), gside[h, at, 0:128]), nn(dscores, qhead[h, at, :])
+            if u == 0:
+                dvals[chunk, :] = dv
+                dkeys[chunk, :] = dk
+            else:
+                dvals[chunk, :] += dv
+                dkeys[chunk, :] += dk
+            part = tn(dscores, k_ref[chunk, :])
+            dq = part if dq is None else dq + part
+        if h == 0:
+            dquery[...] = dq
+        else:
+            out_ref[0, at, :] = (jnp.where(lane < 64, dquery[...], dq) * 0.125).astype(BF16)
     out_ref[1] = dkeys[...].astype(BF16)
     out_ref[2] = dvals[...].astype(BF16)
 
 
-def attend_back(dense, projected, g_mixed, mixed, lse, onehot, keymask, start, number):
+def attend_back(projected, g_mixed, mixed, lse, onehot, keymask):
     tokens = projected.shape[0]
     pairs = projected.shape[1] // 3 // 128
-    part = lambda at: pl.BlockSpec((tokens, 128), lambda j, d: (0, at + start + j))
-    whole = pl.BlockSpec((tokens, 128), lambda j, d: (0, 0))
+    part = lambda at: pl.BlockSpec((tokens, 128), lambda j: (0, at + j))
+    whole = pl.BlockSpec((tokens, 128), lambda j: (0, 0))
+    wide, narrow = pltpu.VMEM((2, tokens, 256), BF16), pltpu.VMEM((tokens, 128), F32)
+    square_tile = pltpu.VMEM((2, tokens, tokens // 2), F32)
     return pl.pallas_call(
         attend_back_kernel,
-        grid_spec=pltpu.PrefetchScalarGridSpec(
-            num_scalar_prefetch=1,
-            grid=(number,),
-            in_specs=[part(0), part(pairs), part(2 * pairs), part(0), part(0), part(0), whole, whole],
-            out_specs=pl.BlockSpec((3, tokens, 128), lambda j, d: (0, 0, j)),
-            scratch_shapes=[
-                pltpu.VMEM((tokens, 256), BF16), pltpu.VMEM((tokens, 256), BF16),
-                pltpu.VMEM((tokens, 128), F32), pltpu.VMEM((tokens, 128), F32),
-            ],
-        ),
-        out_shape=jax.ShapeDtypeStruct((3, tokens, number * 128), BF16),
-        compiler_params=params(),
-        cost_estimate=cost(5 * 2 * 2 * number * tokens * tokens * 256, tokens * 128 * number * 22, 2 * number * tokens * tokens),
+        grid=(pairs,),
+        in_specs=[part(0), part(pairs), part(2 * pairs), part(0), part(0), part(0), whole, whole],
+        out_specs=pl.BlockSpec((3, tokens, 128), lambda j: (0, 0, j)),
+        scratch_shapes=[
+            wide, wide, pltpu.VMEM((tokens, 256), BF16), wide, pltpu.VMEM((2, tokens, 128), BF16),
+            narrow, narrow, square_tile, square_tile, pltpu.VMEM((tokens // 2, 128), F32),
+        ],
+        out_shape=jax.ShapeDtypeStruct((3, tokens, pairs * 128), BF16),
+        compiler_params=params(),
+        cost_estimate=cost(5 * 2 * 12 * tokens * tokens * 256, tokens * 768 * 22, 12 * tokens * tokens),
         name="attend_back",
-    )(dense, projected, projected, projected, g_mixed, mixed, lse, onehot, keymask)
+    )(projected, projected, projected, g_mixed, mixed, lse, onehot, keymask)
 
 
 def mlp_kernel(
@@ -421,7 +453,10 @@
 
         row_tiles(tokens, body)
 
-    up, down = square(up_ref), square(down_ref)
+    up = square(up_ref)
+    down = jnp.concatenate(
+        [down_ref[r, f, 0] for f in range(down_ref.shape[1]) for r in range(down_ref.shape[0])]
+    )
 
     def body(rows):
         x = nn(norm2[rows, :], up) + shift_ref[0]
@@ -467,12 +502,14 @@
         gwo_ref[...] = tn(mixed_ref[...], xhats[...]).astype(BF16).reshape(gwo_ref.shape)
 
 
-def mlp_call(embed, mixed, cotangent, live, small, shift, rowwise, colwise):
+def mlp_call(embed, mixed, cotangent, live, small, shift, downs, colwise):
     tokens, width = embed.shape
     bands, deep = colwise.shape[1], colwise.shape[3]
     fixed = pl.BlockSpec((tokens, width), lambda s: (0, 0))
     whole = lambda a: pl.BlockSpec(a.shape, lambda s: (0, 0))
-    band = lambda group, at: pl.BlockSpec((1, bands, 1, deep, width), lambda s: (group, 0, at(s), 0, 0))
+    band = lambda group, at: pl.BlockSpec((1, bands, 1, deep, width), lambda s: (at(s), 0, group, 0, 0))
+    last = downs.shape[2] - 1
+    down_block = (downs.shape[0], downs.shape[1] // 4, 1) + downs.shape[3:]
     scratch = lambda kind: pltpu.VMEM((tokens, width), kind)
     return pl.pallas_call(
         mlp_kernel,
@@ -480,8 +517,8 @@
         in_specs=[
             fixed, fixed, fixed, whole(live), whole(small),
             pl.BlockSpec((1, 1, width), lambda s: (s, 0, 0)),
-            band(1, lambda s: 3), band(2, lambda s: s),
-            pl.BlockSpec((1, 1, width, width), lambda s: (3, s, 0, 0)),
+            band(0, lambda s: 3), band(1, lambda s: s),
+            pl.BlockSpec(down_block, lambda s: (0, s, last, 0, 0)),
         ],
         out_specs=[
             fixed, fixed, fixed,
@@ -508,7 +545,7 @@
         compiler_params=params(),
         cost_estimate=cost(27 * 2 * tokens * width * width, tokens * width * 20 + 18 * width * width * 2),
         name="mlp",
-    )(embed, mixed, cotangent, live, small, shift, colwise, colwise, rowwise)
+    )(embed, mixed, cotangent, live, small, shift, colwise, colwise, downs)
 
 
 def store_split(core, value, mine_ref, other_ref):
@@ -618,7 +655,7 @@
         grid=(3,),
         in_specs=[
             pl.BlockSpec((1, tokens, width), lambda s: (s, 0, 0)),
-            pl.BlockSpec((1, bands, 1, deep, width), lambda s: (1, 0, s, 0, 0)),
+            pl.BlockSpec((1, bands, 1, deep, width), lambda s: (s, 0, 0, 0, 0)),
             fixed, fixed, whole(pos_rows), whole(small),
         ],
         out_specs=[
@@ -679,6 +716,45 @@
         cost_estimate=cost(1e6, 1e5),
         name="patch_grad",
     )(core, resized, g_emb, g_small)
+
+
+def finish_kernel(
+    kern_ref, rest_ref, up_ref, down_ref,
+    o_kern, o_qkv, o_out, o_up, o_down, o_biases, o_gains, o_pos, o_shift,
+):
+    shard, width = o_kern.shape
+    depth = o_out.shape[0]
+    kern = kern_ref[...].astype(F32)
+    o_kern[...] = kern[0:shard]
+    o_down[...] = down_ref[...].astype(F32)
+    rest, up = rest_ref[...].astype(F32), up_ref[...].astype(F32)
+    for j in range(4):
+        rows, columns = slice(j * depth, (j + 1) * depth), slice(j * width, (j + 1) * width)
+        o_up[:, columns] = up[rows]
+        if j < 3:
+            o_qkv[:, columns] = rest[rows]
+        else:
+            o_out[...] = rest[rows]
+    small = jnp.concatenate([kern[shard:, 0:128], kern[shard:, 128:256]])[:, 0:depth]
+    at = 0
+    for ref in (o_biases, o_gains, o_pos, o_shift):
+        ref[...] = small[at : at + ref.shape[0]]
+        at += ref.shape[0]
+
+
+def finish(kern, rest, up, down, cells):
+    shard, width = down.shape
+    depth = shard // 4
+    shapes = [
+        (shard, width), (depth, 3 * width), (depth, width), (depth, 4 * width), (shard, width),
+        (7, depth), (2, depth), (cells, depth), (4, depth),
+    ]
+    return pl.pallas_call(
+        finish_kernel,
+        out_shape=[jax.ShapeDtypeStruct(shape, F32) for shape in shapes],
+        compiler_params=params(),
+        name="finish",
+    )(kern, rest, up, down)
 
 
 def bit_of(axis, bit):
@@ -733,6 +809,41 @@
         return self.kept
 
 
+class Gather:
+    def __init__(self, shard, reps, owners, flip=False):
+        rep, own = reps.bit_length() - 1, owners.bit_length() - 1
+        self.sizes = dict(rep=reps, fsdp=owners)
+        self.order = [("fsdp", b) for b in range(own)][::-1] + [("rep", b) for b in range(rep)][::-1]
+        over_reps = self.order[own:][::-1] if flip else self.order[own:]
+        self.steps = self.order[: own - 1] + over_reps + [("fsdp", 0)]
+        self.held = []
+        self.shape = (owners * shard.shape[0], shard.shape[1])
+        share = shard.shape[0] // reps
+        at = lax.axis_index("rep") * share if reps > 1 else 0
+        self.launch(lax.dynamic_slice(shard, (at, 0), (share, shard.shape[1])))
+
+    def launch(self, value):
+        self.kept = value
+        if self.steps:
+            axis, bit = self.steps[0]
+            self.flying = lax.ppermute(value, axis, [(i, i ^ (1 << bit)) for i in range(self.sizes[axis])])
+
+    def land(self):
+        if not self.steps:
+            return
+        axis, bit = self.steps.pop(0)
+        at = sum(self.order.index(h) < self.order.index((axis, bit)) for h in self.held)
+        self.held.append((axis, bit))
+        low = bit_of(axis, bit) == 0
+        a, b = self.kept, self.flying
+        self.launch(jnp.stack([jnp.where(low, a, b), jnp.where(low, b, a)], axis=at))
+
+    def total(self):
+        while self.steps:
+            self.land()
+        return self.kept.reshape(self.shape)
+
+
 def beside(sums, work, value):
     value = lax.optimization_barrier((value, *[one.kept for one in sums]))[0]
     value, *kept = lax.optimization_barrier((work(value), *[one.kept for one in sums]))
@@ -757,20 +868,24 @@
         return jnp.concatenate([w.reshape(depth, -1, width).transpose(1, 0, 2) for w in shards]).reshape(shard, width)
 
     small_here = jnp.concatenate([biases, gains, pos_table, up_bias.reshape(-1, depth)])
-    bundle = jnp.concatenate(
-        [patch_kernel, stacked([qkv_weight, out_weight]), stacked([up_weight]), down_weight]
-    )
-    share = 4 * shard // reps
-    here = lax.dynamic_slice(bundle, (lax.axis_index("rep") * share, 0), (share, width))
-    groups = lax.all_gather(here, ("rep", "fsdp"), axis=0, tiled=True)
-    small_all = lax.all_gather(small_here, "fsdp", axis=0, tiled=False)
-    groups = (
-        groups.reshape(4, reps // 4, owners, share, width).transpose(0, 2, 1, 3, 4).reshape(4, owners, shard, width)
-    )
-    rowwise = groups.reshape(4, 4, width, width)
-    colwise = groups.reshape(4, owners, 4, depth, width)
-    if depth % 16 != 0:
-        colwise = colwise.transpose(0, 2, 1, 3, 4).reshape(4, 1, 4, width, width)
+    here_rows = small_here.shape[0]
+    small_here = jnp.pad(small_here, ((0, -here_rows % 16), (0, 0)))
+    bundle = jnp.stack([stacked([qkv_weight, out_weight]), stacked([up_weight]), down_weight])
+    share = shard // reps
+    here = lax.dynamic_slice(bundle, (0, lax.axis_index("rep") * share, 0), (3, share, width))
+    groups = lax.all_gather(here, ("rep", "fsdp"), axis=0, tiled=False).reshape(reps, owners, 3, share, width)
+    kernel = Gather(patch_kernel, reps, owners)
+    little = Gather(small_here, 1, owners)
+    while len(kernel.steps) > 2:
+        kernel.land()
+        little.land()
+    small_all = little.total().reshape(owners, -1, depth)[:, :here_rows]
+    if reps == 4 and depth % 16 == 0 and owners % 4 == 0:
+        colwise = downs = groups
+    else:
+        groups = groups.transpose(2, 1, 0, 3, 4).reshape(3, owners, shard, width)
+        colwise = groups.reshape(3, owners, 4, depth, width).transpose(2, 0, 1, 3, 4).reshape(4, 1, 3, width, width)
+        downs = groups[2].reshape(1, 4, 1, width, width)
     rows_of = small_all[:, : 9 + cells].transpose(1, 0, 2).reshape(9 + cells, width)
     small = jnp.pad(rows_of[:9].astype(F32), ((0, 7), (0, 0)))
     table = jnp.pad(rows_of[9:], ((0, 128 - cells), (0, 0)))
@@ -779,7 +894,6 @@
     segment, category, offset, live_rows = token_layout(image_class[0], tokens)
     live = live_rows[:, None].astype(F32)
     lists = chunk_lists(category)
-    dense = (image_class[0, :1] == 0).astype(jnp.int32)
     lane = jnp.arange(128, dtype=jnp.int32)[None, :]
     same = segment[:, None] == lane
     onehot = same.astype(BF16)
@@ -795,11 +909,13 @@
     ra = jnp.pad(resize_a, ((0, -resize_a.shape[0] % 128), (0, 0)))
     rb = jnp.pad(resize_b, ((0, -resize_b.shape[0] % 128), (0, 0)))
 
-    resized = resize(lists, pixels, cats, ra, rb, resize_c)
-    embed, normed1, projected = embed_call(resized, rowwise, colwise, pos_rows, table, small)
-    mixed, lse = attend(dense, projected, onehot, keymask)
+    resized = beside([kernel], lambda p: resize(lists, p, cats, ra, rb, resize_c), pixels)
+    patch = kernel.total()
+    embed, normed1 = embed_call(resized, patch, pos_rows, table, small)
+    projected = project(normed1, colwise, small)
+    mixed, lse = attend(projected, onehot, keymask)
     output, g_hidden, g_mixed, g_down, g_up, g_out, sums_mlp, g_shift = mlp_call(
-        embed, mixed, cotangent, live, small, shift, rowwise, colwise
+        embed, mixed, cotangent, live, small, shift, downs, colwise
     )
     def bands_of(blocks, number):
         if blocks.shape[0] != owners:
@@ -809,22 +925,19 @@
     scatter = lambda x: lax.psum_scatter(x, "fsdp", scatter_dimension=0, tiled=False)
     s_down = scatter(g_down.reshape(owners, shard, width))
     s_up = scatter(bands_of(g_up, 4))
-    pairs = width // 128
-    dproj = attend_back(dense, projected, g_mixed, mixed, lse, onehot, keymask, 0, pairs)
-    dproj = lax.optimization_barrier((dproj, s_down))[0]
+    dproj = attend_back(projected, g_mixed, mixed, lse, onehot, keymask)
     core = bit_of("fsdp", 0).reshape(1)
     own, rep = owners.bit_length() - 1, reps.bit_length() - 1
     others = [("fsdp", b) for b in range(1, own)]
     over_reps = [("rep", b) for b in range(rep)]
     g_emb, g_pos, sums_embed = embed_back(dproj, colwise, embed, g_hidden, pos_rows, small)
+    lanes = ((0, 0), (0, 0), (0, 128 - depth))
     g_small = jnp.concatenate([(sums_mlp + sums_embed)[:9], g_pos[:cells]]).reshape(9 + cells, owners, depth)
     g_small = jnp.concatenate(
-        [g_small.transpose(1, 0, 2), g_shift.reshape(owners, -1, depth)], axis=1
+        [jnp.pad(g_small, lanes).transpose(1, 0, 2), jnp.pad(g_shift.reshape(owners, 4, depth), lanes)], axis=1
     ).astype(BF16)
-    packed = -(-g_small.shape[1] * depth // (32 * width)) * 32
-    g_small = jnp.pad(
-        g_small.reshape(owners, -1), ((0, 0), (0, packed * width - g_small.shape[1] * depth))
-    ).reshape(owners, packed, width)
+    g_small = jnp.pad(g_small, ((0, 0), (0, 64 - g_small.shape[1]), (0, 0)))
+    g_small = jnp.concatenate([g_small[:, :32], g_small[:, 32:], jnp.zeros((owners, 32, width - 256), BF16)], axis=2)
     mine, other = patch_grad(core, resized, g_emb, g_small)
     kern = Sum(mine, other, reps, owners, over_reps[::-1] + others)
     mine, other = beside([kern], lambda d: qkv_grad(core, normed1, d, g_out), dproj)
@@ -838,15 +951,16 @@
 
     kern.kept, qkvo.kept = lax.optimization_barrier((kern.kept, qkvo.kept))
     qkvo.land()
+    g_emb = lax.optimization_barrier((g_emb, s_down))[0]
     grad_pixels = None
     for channel in range(3):
 
         def work(pair):
             return unresize(
-                lists, pair[0], groups, cats, ra, rb, resize_c, pixels.shape[1] // 3, channel, 0, 1, pair[1]
+                lists, pair[0], patch, cats, ra, rb, resize_c, pixels.shape[1] // 3, channel, 0, 1, pair[1]
             )
 
-        if channel == 2:
+        if channel == 1:
             g_emb = lax.optimization_barrier((g_emb, s_up))[0]
         grad_pixels = beside([qkvo, kern], work, (g_emb, grad_pixels))
         kern.land()
@@ -856,17 +970,10 @@
         kern.land()
         qkvo.land()
     kern.kept, s_up, s_down = lax.optimization_barrier((kern.kept, s_up, s_down))
-    s_up, s_down, grad_pixels, s_rest, s_kernel = lax.optimization_barrier(
-        (s_up, s_down, grad_pixels, qkvo.total(), kern.total())
-    )
-    s_up, s_down, s_rest, s_kernel = (x.astype(F32) for x in (s_up, s_down, s_rest, s_kernel))
-    s_small = s_kernel[shard:].reshape(-1)[: (9 + cells) * depth + shard].reshape(-1, depth)
-    s_kernel = s_kernel[:shard]
-    unstack = lambda p: p.reshape(-1, depth, width).transpose(1, 0, 2).reshape(depth, -1)
+    totals = finish(kern.total(), qkvo.total(), s_up, s_down, cells)
+    t_kernel, t_qkv, t_out, t_up, t_down, t_biases, t_gains, t_pos, t_shift = totals
     return (
-        output, grad_pixels, s_kernel, s_small[9 : 9 + cells], unstack(s_rest[: 3 * depth]),
-        s_rest[3 * depth : 4 * depth], unstack(s_up), s_down,
-        s_small[:7], s_small[9 + cells :].reshape(-1), s_small[7:9],
+        output, grad_pixels, t_kernel, t_pos, t_qkv, t_out, t_up, t_down, t_biases, t_shift.reshape(-1), t_gains
     )
 
 

time: 463 us -> 428 us (0.924)
  waiting for transfers between devices: 109 us -> 75.8 us
  starting transfers between devices: 17.4 us -> 42.8 us
  blocking collectives: 16 us -> 0 us
  Pallas kernels: 255 us -> 240 us
  other arithmetic: 19.6 us -> 26.3 us
    all_gather x1, waiting for transfers between devices: 68.6 us -> 0.01 us  [local(): lax.all_gather(here, ('rep', 'fsdp'), axis=0, tiled=False)]
    ppermute x0 -> x8, waiting for transfers between devices: none -> 37.8 us  [launch(): lax.ppermute(value, axis, [(i, i ^ 1 << bit) for i in range(self.sizes[ax...]
    ppermute x0 -> x8, starting transfers between devices: none -> 19.5 us  [launch(): lax.ppermute(value, axis, [(i, i ^ 1 << bit) for i in range(self.sizes[ax...]
    all_gather x1 -> x0, blocking collectives: 16 us -> none  [local(): small_all = lax.all_gather(small_here, 'fsdp', axis=0, tiled=False)]
    pallas_call x3 -> x5, Pallas kernels: 101 us -> 85.5 us  [the longest x1 41.2 us: attend_back(): pl.pallas_call(attend_back_kernel, grid=(pairs,), in_specs=[part(0), part...]
    another operation x4 -> x21, other arithmetic: 1.03 us -> 8.64 us  [the longest x16 6.81 us: land(): jnp.stack([jnp.where(low, a, b), jnp.where(low, b, a)], axis=at)]
    ppermute x14, starting transfers between devices: 17.2 us -> 23.2 us  [launch(): self.kept, self.flying = (kept, lax.ppermute(sent, axis, pairs))]
  transfers between devices with their start and end apart: 18 -> 26, of which waited for: 10 -> 11; matrix products, arithmetic and copies ran while one was open for 7% -> 10% of each run, Pallas kernels for 35% -> 37%
where the time goes in v3:
time: 428 us; the launch traced here: 423 us
  Pallas kernels  240 us (56%)
  waiting for transfers between devices  75.8 us (18%)
  starting transfers between devices  42.8 us (10%)
  other arithmetic  26.3 us (6%)
  local copies, waits for them, and re-layouts  23.4 us (5%)
  between operations  14.9 us (3%)
    pallas_call x1, Pallas kernels, mlp_call(): pl.pallas_call(mlp_kernel, grid=(4,), in_specs=[fixed, fixed, fixed, whol...  48.4 us
    pallas_call x3, Pallas kernels, unresize(): pl.pallas_call(unresize_kernel, grid_spec=pltpu.PrefetchScalarGridSpec(nu...  46.7 us
    pallas_call x1, Pallas kernels, attend_back(): pl.pallas_call(attend_back_kernel, grid=(pairs,), in_specs=[part(0), part...  41.2 us
    ppermute x8, waiting for transfers between devices, launch(): lax.ppermute(value, axis, [(i, i ^ 1 << bit) for i in range(self.sizes[ax...  37.8 us
    ppermute x14, waiting for transfers between devices, launch(): self.kept, self.flying = (kept, lax.ppermute(sent, axis, pairs))  37.3 us
    pallas_call x1, Pallas kernels, resize(): pl.pallas_call(resize_kernel, grid_spec=pltpu.PrefetchScalarGridSpec(num_...  27.2 us
    ppermute x14, starting transfers between devices, launch(): self.kept, self.flying = (kept, lax.ppermute(sent, axis, pairs))  23.2 us
    pallas_call x1, Pallas kernels, attend(): pl.pallas_call(attend_kernel, grid=(pairs,), in_specs=[part(0), part(pair...  21.4 us
  transfers between devices with their start and end apart: 26, of which 11 were waited for; matrix products, arithmetic and copies ran while one was open for 10% of the time, Pallas kernels for 37%

profile of v3, /device:TPU:0, one launch (start us, length us, event | category | flops | bytes accessed | tf_op | source)
XLA Modules:
  0.0 422.8 jit_solution(5483594265065779420)
XLA Ops:
  12.0 4.1 collective-permute-start
  17.5 6.1 %collective-permute-done = bf16[96,768]{1,0:T(8,128)(2,1)S(1)} collective-permute-done((bf16[96,768]{1,0:T(8,128)(2,1)S(1)}, bf16[96,768]{1,0:T(8,128)(2,1)S(1)}, u32[]{:S(2)}, u32[]{:S(2)}) %collective-permute-start) | collective-permute-done | bytes 147488 | tf_op jit(solution)/shard_map/ppermute | solution.py:829
  24.9 13.7 %collective-permute-done.1 = bf16[2,96,768]{2,1,0:T(8,128)(2,1)S(1)} collective-permute-done((bf16[2,96,768]{2,1,0:T(8,128)(2,1)S(1)}, bf16[2,96,768]{2,1,0:T(8,128)(2,1)S(1)}, u32[]{:S(2)}, u32[]{:S(2)}) %collective-permute-start.1) | collective-permute-done | bytes 294944 | tf_op jit(solution)/shard_map/ppermute | solution.py:829
  41.5 15.1 %collective-permute-done.2 = bf16[2,2,96,768]{3,2,0,1:T(8,128)(2,1)S(1)} collective-permute-done((bf16[2,2,96,768]{3,2,0,1:T(8,128)(2,1)S(1)}, bf16[2,2,96,768]{3,2,0,1:T(8,128)(2,1)S(1)}, u32[]{:S(2)}, u32[]{:S(2)}) %collective-permute-start.2) | collective-permute-done | bytes 589856 | tf_op jit(solution)/shard_map/ppermute | solution.py:829
  59.0 2.5 pad.40.rb_ref
  64.0 27.2 %resize.1.res_ref = bf16[1024,3072]{1,0:T(8,128)(2,1)} custom-call(s32[3,65]{1,0:T(4,128)} %pad_add_fusion.lists, bf16[1024,6912]{1,0:T(8,128)(2,1)} %px_ref, s32[1024,1]{1,0:T(8,128)} %copy.101.cat_ref, bf16[128,1024]{1,0:T(8,128)(2,1)} %pad.39.ra_ref, bf16[640,1024]{1,0:T(8,128)(2,1)} %pad.40.rb_ref, bf16[2304,1024]{1,0:T(8,128)(2,1)} %rc_ref.7), custom_call_target="tpu_custom_call" | custom-call | flops 7549747200 | bytes 20447232 | tf_op jit(solution)/shard_map/resize/pallas_call | solution.py:110
  91.2 2.9 collective-permute-done.3
  98.3 11.7 %collective-permute-start.6 = (bf16[2,64,96]{2,1,0:T(8,128)(2,1)S(1)}, bf16[2,64,96]{2,1,0:T(8,128)(2,1)S(1)}, u32[]{:S(2)}, u32[]{:S(2)}) collective-permute-start(bf16[2,64,96]{2,1,0:T(8,128)(2,1)S(1)} %pad_maximum_fusion.13), channel_id=1, source_target_pairs={{0,2},{1,3},{2,0},{3,1},{4,6},{5,7},{6,4},{7,5},{8,10},{9,11},{10,... | collective-permute-start | bytes 73736 | tf_op jit(solution)/shard_map/ppermute | solution.py:829
  111.0 3.2 gather_fusion
  118.9 2.0 select_bitcast_fusion.1
  121.4 2.5 copy.102
  123.9 11.3 %embed.1 = (f32[1024,768]{1,0:T(8,128)}, bf16[1024,768]{1,0:T(8,128)(2,1)}) custom-call(bf16[1024,3072]{1,0:T(8,128)(2,1)} %resize.1.res_ref, bf16[4,768,768]{2,1,0:T(8,128)(2,1)} %bitcast.111, bf16[1024,128]{1,0:T(8,128)(2,1)} %pad_select_fusion.pos_ref, bf16[128,768]{1,0:T(8,128)(2,1)} %pad.42.table_ref, f32[16,768]{1,0:T(8,128)} %pad_convert_fusion.small_ref), custom_call_target="tpu_custom_call" | custom-call | flops 4831838208 | bytes 15728640 | tf_op jit(solution)/shard_map/embed/pallas_call | solution.py:215
  135.2 7.7 %project.1.q_ref.k_ref.v_ref = bf16[1024,2304]{1,0:T(8,128)(2,1)} custom-call(bf16[1024,768]{1,0:T(8,128)(2,1)} %get-tuple-element.99.norm_ref, bf16[4,8,3,96,768]{4,3,2,1,0:T(8,128)(2,1)} %bitcast.115, f32[16,768]{1,0:T(8,128)} %pad_convert_fusion.small_ref), custom_call_target="tpu_custom_call" | custom-call | flops 3623878656 | bytes 9830400 | tf_op jit(solution)/shard_map/project/pallas_call | solution.py:242
  142.9 21.4 %attend.1 = (bf16[1024,768]{1,0:T(8,128)(2,1)}, f32[1024,768]{1,0:T(8,128)}) custom-call(bf16[1024,2304]{1,0:T(8,128)(2,1)} %project.1.q_ref.k_ref.v_ref, bf16[1024,2304]{1,0:T(8,128)(2,1)} %project.1.q_ref.k_ref.v_ref, bf16[1024,2304]{1,0:T(8,128)(2,1)} %project.1.q_ref.k_ref.v_ref, bf16[1024,128]{1,0:T(8,128)(2,1)} %fusion.oh_ref, ...), custom_call_target="tpu_custom_call" | custom-call | flops 12884901888 | bytes 9437184 | tf_op jit(solution)/shard_map/attend/pallas_call | solution.py:321
  164.2 48.4 %mlp.1 = (bf16[1024,768]{1,0:T(8,128)(2,1)}, f32[1024,768]{1,0:T(8,128)}, bf16[1024,768]{1,0:T(8,128)(2,1)}, bf16[4,768,768]{2,1,0:T(8,128)(2,1)}, bf16[8,4,96,7...) custom-call(f32[1024,768]{1,0:T(8,128)} %get-tuple-element.98.embed_ref, ...), custom_call_target="tpu_custom_call" | custom-call | flops 32614907904 | bytes 36962304 | tf_op jit(solution)/shard_map/mlp/pallas_call | solution.py:514
  213.4 41.2 %attend_back.1.dproj_ref = bf16[3,1024,768]{2,1,0:T(8,128)(2,1)} custom-call(bf16[1024,2304]{1,0:T(8,128)(2,1)} %project.1.q_ref.k_ref.v_ref, bf16[1024,2304]{1,0:T(8,128)(2,1)} %project.1.q_ref.k_ref.v_ref, bf16[1024,2304]{1,0:T(8,128)(2,1)} %project.1.q_ref.k_ref.v_ref, bf16[1024,768]{1,0:T(8,128)(2,1)} %get-tuple-element.102.g_ref, ...), custom_call_target="tpu_custom_call" | custom-call | flops 32212254720 | bytes 17301504 | tf_op jit(solution)/shard_map/attend_back/pallas_call | solution.py:419
  254.6 12.7 %embed_back.1 = (bf16[1024,768]{1,0:T(8,128)(2,1)}, f32[128,768]{1,0:T(8,128)}, f32[16,768]{1,0:T(8,128)}) custom-call(bf16[3,1024,768]{2,1,0:T(8,128)(2,1)} %attend_back.1.dproj_ref, bf16[4,8,3,96,768]{4,3,2,1,0:T(8,128)(2,1)} %bitcast.119, f32[1024,768]{1,0:T(8,128)} %get-tuple-element.98.embed_ref, f32[1024,768]{1,0:T(8,128)} %get-tuple-element.104.ghid_ref, ...), custom_call_target="tpu_custom_call" | custom-call | flops 1000000 | bytes 100000 | tf_op jit(solution)/shard_map/embed_back/pallas_call | solution.py:653
  270.4 10.2 %patch_grad.1 = (bf16[4,416,768]{2,1,0:T(8,128)(2,1)}, bf16[4,416,768]{2,1,0:T(8,128)(2,1)}) custom-call(s32[1]{0:T(128)} %bitcast.39.core_ref, bf16[1024,3072]{1,0:T(8,128)(2,1)} %resize.1.res_ref, bf16[1024,768]{1,0:T(8,128)(2,1)} %get-tuple-element.148.g_ref, bf16[8,32,768]{2,1,0:T(8,128)(2,1)} %maximum_maximum_fusion.small_ref), custom_call_target="tpu_custom_call" | custom-call | flops 1000000 | bytes 100000 | tf_op jit(solution)/shard_map/patch_grad/pallas_call | solution.py:702
  281.1 8.8 %qkv_grad.1 = (bf16[4,4,96,768]{3,2,1,0:T(8,128)(2,1)}, bf16[4,4,96,768]{3,2,1,0:T(8,128)(2,1)}) custom-call(s32[1]{0:T(128)} %bitcast.39.core_ref, bf16[1024,768]{1,0:T(8,128)(2,1)} %get-tuple-element.99.norm_ref, bf16[3,1024,768]{2,1,0:T(8,128)(2,1)} %attend_back.1.dproj_ref, bf16[8,96,768]{2,1,0:T(8,128)(2,1)} %get-tuple-element.118.gwo_ref), custom_call_target="tpu_custom_call" | custom-call | flops 1000000 | bytes 100000 | tf_op jit(solution)/shard_map/qkv_grad/pallas_call | solution.py:586
  289.9 2.4 add_convert_fusion
  294.9 2.2 add_convert_fusion.1
  299.0 15.6 %unresize.3.rest_0_ = bf16[1024,6912]{1,0:T(8,128)(2,1)} custom-call(s32[3,65]{1,0:T(4,128)} %pad_add_fusion.lists, bf16[1024,768]{1,0:T(8,128)(2,1)} %get-tuple-element.148.g_ref, bf16[3,1024,768]{2,1,0:T(8,128)(2,1)} %bitcast.112, s32[1024,1]{1,0:T(8,128)} %copy.101.cat_ref, bf16[128,1024]{1,0:T(8,128)(2,1)} %pad.39.ra_ref, bf16[640,1024]{1,0:T(8,128)(2,1)} %pad.40.rb_ref, ...), custom_call_target="tpu_custom_call" | custom-call | flops 1000000 | bytes 100000 | tf_op jit(solution)/shard_map/unresize/pallas_call | solution.py:145
  314.6 12.1 %collective-permute-done.10 = bf16[2,2,192,768]{3,2,1,0:T(8,128)(2,1)} collective-permute-done((bf16[2,2,192,768]{3,2,1,0:T(8,128)(2,1)}, bf16[2,2,192,768]{3,2,1,0:T(8,128)(2,1)}, u32[]{:S(2)}, u32[]{:S(2)}) %collective-permute-start.10) | collective-permute-done | bytes 1179680 | tf_op jit(solution)/shard_map/ppermute | solution.py:777
  332.3 15.7 %unresize.4.rest_0_ = bf16[1024,6912]{1,0:T(8,128)(2,1)} custom-call(s32[3,65]{1,0:T(4,128)} %pad_add_fusion.lists, bf16[1024,768]{1,0:T(8,128)(2,1)} %get-tuple-element.148.g_ref, bf16[3,1024,768]{2,1,0:T(8,128)(2,1)} %bitcast.113, s32[1024,1]{1,0:T(8,128)} %copy.101.cat_ref, bf16[128,1024]{1,0:T(8,128)(2,1)} %pad.39.ra_ref, ...), custom_call_target="tpu_custom_call", output_to_operand_aliasing={{}: (7, {})} | custom-call | flops 1000000 | bytes 100000 | tf_op jit(solution)/shard_map/unresize/pallas_call | solution.py:145
  348.2 5.6 %collective-permute-start.18 = (bf16[192,768]{1,0:T(8,128)(2,1)S(1)}, bf16[192,768]{1,0:T(8,128)(2,1)S(1)}, u32[]{:S(2)}, u32[]{:S(2)}) collective-permute-start(bf16[192,768]{1,0:T(8,128)(2,1)S(1)} %get-tuple-element.161), channel_id=1, source_target_pairs={{0,4},{1,5},{2,6},{3,7},{4,0},{5,1},{6,2},{7,3},{8,12},{9,13},{10,... | collective-permute-start | bytes 884744 | tf_op jit(solution)/shard_map/ppermute | solution.py:777
  354.1 15.5 %unresize.5 = bf16[1024,6912]{1,0:T(8,128)(2,1)} custom-call(s32[3,65]{1,0:T(4,128)} %pad_add_fusion.lists, bf16[1024,768]{1,0:T(8,128)(2,1)} %get-tuple-element.148.g_ref, bf16[3,1024,768]{2,1,0:T(8,128)(2,1)} %bitcast.114, s32[1024,1]{1,0:T(8,128)} %copy.101.cat_ref, bf16[128,1024]{1,0:T(8,128)(2,1)} %pad.39.ra_ref, ...), custom_call_target="tpu_custom_call", output_to_operand_aliasing={{}: (7, {})} | custom-call | flops 1000000 | bytes 100000 | tf_op jit(solution)/shard_map/unresize/pallas_call | solution.py:145
  369.5 7.4 %collective-permute-start.14 = (bf16[2,104,768]{2,1,0:T(8,128)(2,1)S(1)}, bf16[2,104,768]{2,1,0:T(8,128)(2,1)S(1)}, u32[]{:S(2)}, u32[]{:S(2)}) collective-permute-start(bf16[2,104,768]{2,1,0:T(8,128)(2,1)S(1)} %get-tuple-element.152), channel_id=1, source_target_pairs={{0,2},{1,3},{2,0},{3,1},{4,6},{5,7},{6,4},{7,5},{8,10},{9,11},{10,... | collective-permute-start | bytes 958472 | tf_op jit(solution)/shard_map/ppermute | solution.py:777
  378.1 5.6 %collective-permute-done.14 = bf16[2,104,768]{2,1,0:T(8,128)(2,1)S(1)} collective-permute-done((bf16[2,104,768]{2,1,0:T(8,128)(2,1)S(1)}, bf16[2,104,768]{2,1,0:T(8,128)(2,1)S(1)}, u32[]{:S(2)}, u32[]{:S(2)}) %collective-permute-start.14) | collective-permute-done | bytes 319520 | tf_op jit(solution)/shard_map/ppermute | solution.py:777
  386.6 6.1 %collective-permute-done.15 = bf16[104,768]{1,0:T(8,128)(2,1)S(1)} collective-permute-done((bf16[104,768]{1,0:T(8,128)(2,1)S(1)}, bf16[104,768]{1,0:T(8,128)(2,1)S(1)}, u32[]{:S(2)}, u32[]{:S(2)}) %collective-permute-start.15) | collective-permute-done | bytes 159776 | tf_op jit(solution)/shard_map/ppermute | solution.py:777
  394.9 6.4 %collective-permute-done.16 = bf16[104,768]{1,0:T(8,128)(2,1)S(1)} collective-permute-done((bf16[104,768]{1,0:T(8,128)(2,1)S(1)}, bf16[104,768]{1,0:T(8,128)(2,1)S(1)}, u32[]{:S(2)}, u32[]{:S(2)}) %collective-permute-start.16) | collective-permute-done | bytes 159776 | tf_op jit(solution)/shard_map/ppermute | solution.py:777
  403.0 4.0 collective-permute-done.21
  410.6 3.9 finish.1
  (197 shorter events, 52.9 us)
Async XLA Ops:
  7.2 128.0 %all-gather.3.cloned.1.call-start = ((), (), s32[]{:S(2)}) async-start(), calls=%async_computation.4 | async-start | bytes 14598144 | tf_op jit(solution)/shard_map/all_gather | solution.py:876
  11.9 287.1 %reduce-scatter.3.cloned.1.call-start = ((), (), s32[]{:S(2)}) async-start(), calls=%async_computation.2 | async-start | bytes 5308416 | tf_op jit(solution)/shard_map/reduce_scatter | solution.py:925
  12.0 11.6 %collective-permute-start = (bf16[96,768]{1,0:T(8,128)(2,1)S(1)}, bf16[96,768]{1,0:T(8,128)(2,1)S(1)}, u32[]{:S(2)}, u32[]{:S(2)}) collective-permute-start(bf16[96,768]{1,0:T(8,128)(2,1)S(1)} %constant_dynamic-slice_fusion), channel_id=1, source_target_pairs={{0,4},{1,5},{2,6},{3,7},{4,0},{5,1},{6,2},{7,3},{8,12},{9,13},{10,... | collective-permute-start | bytes 442376 | tf_op jit(solution)/shard_map/ppermute | solution.py:829
  16.8 80.6 %collective-permute-start.5 = (bf16[64,96]{1,0:T(8,128)(2,1)}, bf16[64,96]{1,0:T(8,128)(2,1)}, u32[]{:S(2)}, u32[]{:S(2)}) collective-permute-start(bf16[64,96]{1,0:T(8,128)(2,1)} %fusion.15), channel_id=1, source_target_pairs={{0,4},{1,5},{2,6},{3,7},{4,0},{5,1},{6,2},{7,3},{8,12},{9,13},{10,... | collective-permute-start | bytes 36872 | tf_op jit(solution)/shard_map/ppermute | solution.py:829
  23.7 14.8 %collective-permute-start.1 = (bf16[2,96,768]{2,1,0:T(8,128)(2,1)S(1)}, bf16[2,96,768]{2,1,0:T(8,128)(2,1)S(1)}, u32[]{:S(2)}, u32[]{:S(2)}) collective-permute-start(bf16[2,96,768]{2,1,0:T(8,128)(2,1)S(1)} %pad_maximum_fusion.8), channel_id=1, source_target_pairs={{0,2},{1,3},{2,0},{3,1},{4,6},{5,7},{6,4},{7,5},{8,10},{9,11},{10,... | collective-permute-start | bytes 884744 | tf_op jit(solution)/shard_map/ppermute | solution.py:829
  38.7 17.9 %collective-permute-start.2 = (bf16[2,2,96,768]{3,2,0,1:T(8,128)(2,1)S(1)}, bf16[2,2,96,768]{3,2,0,1:T(8,128)(2,1)S(1)}, u32[]{:S(2)}, u32[]{:S(2)}) collective-permute-start(bf16[2,2,96,768]{3,2,0,1:T(8,128)(2,1)S(1)} %pad_maximum_fusion.4), channel_id=1, source_target_pairs={{0,16},{8,24},{16,0},{24,8},{1,17},{9,25},{17,1},{25,9},{2,18},{10... | collective-permute-start | bytes 1769480 | tf_op jit(solution)/shard_map/ppermute | solution.py:829
  56.8 37.4 %collective-permute-start.3 = (bf16[2,2,2,96,768]{4,3,0,1,2:T(8,128)(2,1)S(1)}, bf16[2,2,2,96,768]{4,3,0,1,2:T(8,128)(2,1)}, u32[]{:S(2)}, u32[]{:S(2)}) collective-permute-start(bf16[2,2,2,96,768]{4,3,0,1,2:T(8,128)(2,1)S(1)} %pad_maximum_fusion.2), channel_id=1, source_target_pairs={{0,8},{8,0},{16,24},{24,16},{1,9},{9,1},{17,25},{25,17},{2,10},{10... | collective-permute-start | bytes 3538952 | tf_op jit(solution)/shard_map/ppermute | solution.py:829
  95.8 14.2 %copy-start.6 = (bf16[900,49]{0,1:T(8,128)(2,1)S(1)}, bf16[900,49]{0,1:T(8,128)(2,1)}, u32[]{:S(2)}) copy-start(bf16[900,49]{0,1:T(8,128)(2,1)} %param.25) | copy-start | bytes 264604
  95.8 14.4 %copy-start.10 = (bf16[100,49]{0,1:T(8,128)(2,1)S(1)}, bf16[100,49]{0,1:T(8,128)(2,1)}, u32[]{:S(2)}) copy-start(bf16[100,49]{0,1:T(8,128)(2,1)} %param.26) | copy-start | bytes 29404
  95.8 14.5 %copy-start.14 = (bf16[25,49]{1,0:T(8,128)(2,1)S(1)}, bf16[25,49]{1,0:T(8,128)(2,1)}, u32[]{:S(2)}) copy-start(bf16[25,49]{1,0:T(8,128)(2,1)} %param.27) | copy-start | bytes 7354
  97.4 21.5 %collective-permute-start.4 = (bf16[2,2,2,2,96,768]{5,4,0,1,2,3:T(8,128)(2,1)}, bf16[2,2,2,2,96,768]{5,4,0,1,2,3:T(8,128)(2,1)}, u32[]{:S(2)}, u32[]{:S(2)}) collective-permute-start(bf16[2,2,2,2,96,768]{5,4,0,1,2,3:T(8,128)(2,1)} %pad_maximum_fusion.1), channel_id=1, source_target_pairs={{0,1},{1,0},{2,3},{3,2},{4,5},{5,4},{6,7},{7,6},{8,9},{9,8},{10,11... | collective-permute-start | bytes 7077896 | tf_op jit(solution)/shard_map/ppermute | solution.py:829
  98.3 15.9 %collective-permute-start.6 = (bf16[2,64,96]{2,1,0:T(8,128)(2,1)S(1)}, bf16[2,64,96]{2,1,0:T(8,128)(2,1)S(1)}, u32[]{:S(2)}, u32[]{:S(2)}) collective-permute-start(bf16[2,64,96]{2,1,0:T(8,128)(2,1)S(1)} %pad_maximum_fusion.13), channel_id=1, source_target_pairs={{0,2},{1,3},{2,0},{3,1},{4,6},{5,7},{6,4},{7,5},{8,10},{9,11},{10,... | collective-permute-start | bytes 73736 | tf_op jit(solution)/shard_map/ppermute | solution.py:829
  114.3 2.2 collective-permute-start.7
  212.7 119.6 %reduce-scatter.5.cloned.1.call-start = ((), (), s32[]{:S(2)}) async-start(), calls=%async_computation.3 | async-start | bytes 5308416 | tf_op jit(solution)/shard_map/reduce_scatter | solution.py:925
  213.4 189.6 %all-reduce.12.cloned.1.call-start = ((), (), s32[]{:S(2)}) async-start(), calls=%async_computation.5 | async-start | bytes 2359296 | tf_op jit(solution)/shard_map/psum | solution.py:968
  254.6 13.7 %copy-start.9 = (f32[16,768]{1,0:T(8,128)S(1)}, f32[16,768]{1,0:T(8,128)}, u32[]{:S(2)}) copy-start(f32[16,768]{1,0:T(8,128)} %get-tuple-element.110) | copy-start | bytes 147460
  254.6 14.7 %copy-start.11 = (f32[4,1,768]{2,1,0:T(1,128)S(1)}, f32[4,1,768]{2,1,0:T(1,128)}, u32[]{:S(2)}) copy-start(f32[4,1,768]{2,1,0:T(1,128)} %get-tuple-element.113) | copy-start | bytes 36868
  280.6 9.3 %collective-permute-start.8 = (bf16[2,2,416,768]{3,2,1,0:T(8,128)(2,1)}, bf16[2,2,416,768]{3,2,1,0:T(8,128)(2,1)}, u32[]{:S(2)}, u32[]{:S(2)}) collective-permute-start(bf16[2,2,416,768]{3,2,1,0:T(8,128)(2,1)} %bitcast.147), channel_id=1, source_target_pairs={{0,1},{1,0},{2,3},{3,2},{4,5},{5,4},{6,7},{7,6},{8,9},{9,8},{10,11... | collective-permute-start | bytes 7667720 | tf_op jit(solution)/shard_map/ppermute | solution.py:777
  281.1 8.8 %copy-start = (bf16[4,416,768]{2,1,0:T(8,128)(2,1)S(1)}, bf16[4,416,768]{2,1,0:T(8,128)(2,1)}, u32[]{:S(2)}) copy-start(bf16[4,416,768]{2,1,0:T(8,128)(2,1)} %get-tuple-element.114) | copy-start | bytes 7667716
  289.9 5.0 %collective-permute-start.9 = (bf16[2,2,384,768]{3,2,1,0:T(8,128)(2,1)}, bf16[2,2,384,768]{3,2,1,0:T(8,128)(2,1)}, u32[]{:S(2)}, u32[]{:S(2)}) collective-permute-start(bf16[2,2,384,768]{3,2,1,0:T(8,128)(2,1)} %bitcast.148), channel_id=1, source_target_pairs={{0,1},{1,0},{2,3},{3,2},{4,5},{5,4},{6,7},{7,6},{8,9},{9,8},{10,11... | collective-permute-start | bytes 7077896 | tf_op jit(solution)/shard_map/ppermute | solution.py:777
  298.3 28.3 %collective-permute-start.10 = (bf16[2,2,192,768]{3,2,1,0:T(8,128)(2,1)}, bf16[2,2,192,768]{3,2,1,0:T(8,128)(2,1)}, u32[]{:S(2)}, u32[]{:S(2)}) collective-permute-start(bf16[2,2,192,768]{3,2,1,0:T(8,128)(2,1)} %get-tuple-element.134), channel_id=1, source_target_pairs={{0,8},{8,0},{16,24},{24,16},{1,9},{9,1},{17,25},{25,17},{2,10},{10... | collective-permute-start | bytes 3538952 | tf_op jit(solution)/shard_map/ppermute | solution.py:777
  298.3 31.6 %collective-permute-start.11 = (bf16[2,2,208,768]{3,2,1,0:T(8,128)(2,1)}, bf16[2,2,208,768]{3,2,1,0:T(8,128)(2,1)}, u32[]{:S(2)}, u32[]{:S(2)}) collective-permute-start(bf16[2,2,208,768]{3,2,1,0:T(8,128)(2,1)} %get-tuple-element.137), channel_id=1, source_target_pairs={{0,16},{8,24},{16,0},{24,8},{1,17},{9,25},{17,1},{25,9},{2,18},{10... | collective-permute-start | bytes 3833864 | tf_op jit(solution)/shard_map/ppermute | solution.py:777
  329.1 18.9 %collective-permute-start.12 = (bf16[2,192,768]{2,1,0:T(8,128)(2,1)}, bf16[2,192,768]{2,1,0:T(8,128)(2,1)S(1)}, u32[]{:S(2)}, u32[]{:S(2)}) collective-permute-start(bf16[2,192,768]{2,1,0:T(8,128)(2,1)} %get-tuple-element.143), channel_id=1, source_target_pairs={{0,2},{1,3},{2,0},{3,1},{4,6},{5,7},{6,4},{7,5},{8,10},{9,11},{10,... | collective-permute-start | bytes 1769480 | tf_op jit(solution)/shard_map/ppermute | solution.py:777
  331.6 22.2 %collective-permute-start.13 = (bf16[2,2,104,768]{3,2,1,0:T(8,128)(2,1)S(1)}, bf16[2,2,104,768]{3,2,1,0:T(8,128)(2,1)S(1)}, u32[]{:S(2)}, u32[]{:S(2)}) collective-permute-start(bf16[2,2,104,768]{3,2,1,0:T(8,128)(2,1)S(1)} %get-tuple-element.146), channel_id=1, source_target_pairs={{0,8},{8,0},{16,24},{24,16},{1,9},{9,1},{17,25},{25,17},{2,10},{10... | collective-permute-start | bytes 1916936 | tf_op jit(solution)/shard_map/ppermute | solution.py:777
  348.2 28.7 %collective-permute-start.18 = (bf16[192,768]{1,0:T(8,128)(2,1)S(1)}, bf16[192,768]{1,0:T(8,128)(2,1)S(1)}, u32[]{:S(2)}, u32[]{:S(2)}) collective-permute-start(bf16[192,768]{1,0:T(8,128)(2,1)S(1)} %get-tuple-element.161), channel_id=1, source_target_pairs={{0,4},{1,5},{2,6},{3,7},{4,0},{5,1},{6,2},{7,3},{8,12},{9,13},{10,... | collective-permute-start | bytes 884744 | tf_op jit(solution)/shard_map/ppermute | solution.py:777
  369.5 14.2 %collective-permute-start.14 = (bf16[2,104,768]{2,1,0:T(8,128)(2,1)S(1)}, bf16[2,104,768]{2,1,0:T(8,128)(2,1)S(1)}, u32[]{:S(2)}, u32[]{:S(2)}) collective-permute-start(bf16[2,104,768]{2,1,0:T(8,128)(2,1)S(1)} %get-tuple-element.152), channel_id=1, source_target_pairs={{0,2},{1,3},{2,0},{3,1},{4,6},{5,7},{6,4},{7,5},{8,10},{9,11},{10,... | collective-permute-start | bytes 958472 | tf_op jit(solution)/shard_map/ppermute | solution.py:777
  377.0 7.6 %collective-permute-start.19 = (bf16[96,768]{1,0:T(8,128)(2,1)S(1)}, bf16[96,768]{1,0:T(8,128)(2,1)S(1)}, u32[]{:S(2)}, u32[]{:S(2)}) collective-permute-start(bf16[96,768]{1,0:T(8,128)(2,1)S(1)} %get-tuple-element.163), channel_id=1, source_target_pairs={{0,16},{8,24},{16,0},{24,8},{1,17},{9,25},{17,1},{25,9},{2,18},{10... | collective-permute-start | bytes 442376 | tf_op jit(solution)/shard_map/ppermute | solution.py:777
  383.8 8.8 %collective-permute-start.15 = (bf16[104,768]{1,0:T(8,128)(2,1)S(1)}, bf16[104,768]{1,0:T(8,128)(2,1)S(1)}, u32[]{:S(2)}, u32[]{:S(2)}) collective-permute-start(bf16[104,768]{1,0:T(8,128)(2,1)S(1)} %get-tuple-element.154), channel_id=1, source_target_pairs={{0,4},{1,5},{2,6},{3,7},{4,0},{5,1},{6,2},{7,3},{8,12},{9,13},{10,... | collective-permute-start | bytes 479240 | tf_op jit(solution)/shard_map/ppermute | solution.py:777
  384.7 9.5 %collective-permute-start.20 = (bf16[96,768]{1,0:T(8,128)(2,1)S(1)}, bf16[96,768]{1,0:T(8,128)(2,1)S(1)}, u32[]{:S(2)}, u32[]{:S(2)}) collective-permute-start(bf16[96,768]{1,0:T(8,128)(2,1)S(1)} %add_convert_fusion.9), channel_id=1, source_target_pairs={{0,16},{8,24},{16,0},{24,8},{1,17},{9,25},{17,1},{25,9},{2,18},{10... | collective-permute-start | bytes 442376 | tf_op jit(solution)/shard_map/ppermute | solution.py:777
  392.7 8.6 %collective-permute-start.16 = (bf16[104,768]{1,0:T(8,128)(2,1)S(1)}, bf16[104,768]{1,0:T(8,128)(2,1)S(1)}, u32[]{:S(2)}, u32[]{:S(2)}) collective-permute-start(bf16[104,768]{1,0:T(8,128)(2,1)S(1)} %add_convert_fusion.8), channel_id=1, source_target_pairs={{0,8},{8,0},{16,24},{24,16},{1,9},{9,1},{17,25},{25,17},{2,10},{10... | collective-permute-start | bytes 479240 | tf_op jit(solution)/shard_map/ppermute | solution.py:777
  394.2 12.8 %collective-permute-start.21 = (bf16[192,768]{1,0:T(8,128)(2,1)S(1)}, bf16[192,768]{1,0:T(8,128)(2,1)S(1)}, u32[]{:S(2)}, u32[]{:S(2)}) collective-permute-start(bf16[192,768]{1,0:T(8,128)(2,1)S(1)} %pad_maximum_fusion.9), channel_id=1, source_target_pairs={{0,8},{8,0},{16,24},{24,16},{1,9},{9,1},{17,25},{25,17},{2,10},{10... | collective-permute-start | bytes 884744 | tf_op jit(solution)/shard_map/ppermute | solution.py:777
  401.3 8.3 %collective-permute-start.17 = (bf16[208,768]{1,0:T(8,128)(2,1)S(1)}, bf16[208,768]{1,0:T(8,128)(2,1)S(1)}, u32[]{:S(2)}, u32[]{:S(2)}) collective-permute-start(bf16[208,768]{1,0:T(8,128)(2,1)S(1)} %pad_maximum_fusion.7), channel_id=1, source_target_pairs={{0,16},{8,24},{16,0},{24,8},{1,17},{9,25},{17,1},{25,9},{2,18},{10... | collective-permute-start | bytes 958472 | tf_op jit(solution)/shard_map/ppermute | solution.py:777
  (17 other events, 67.5 us)
Sparse Core Ops, SparseCore 0:
  12.0 120.8 all-gather.2
  212.8 56.7 reduce-scatter.2
  271.9 53.2 reduce-scatter.4
  332.4 67.5 all-reduce.11
